TPU v7x, 128 devices: a whole 4x4x4 slice. The times are simulated.
128 devices in a mesh: lon: 32 (over z, x, core), lat: 4 (over y).
Axes of the slice: x: 4, y: 4, z: 4, core: 2. Of those that a mesh axis runs over, the one named last changes fastest.
Arguments:
- courant: float32 [4, 2, 137, 128, 512], P(None, None, None, 'lon', 'lat'), may hold values from -0.45 to 0.45
- slot_column_cells: int32 [4, 128, 128, 4], P(None, ('lon', 'lat')), may hold values from 0 to 511
- column_counts: int32 [4, 128, 128], P(None, ('lon', 'lat')), may hold values from 1 to 4, as said below
- innovations: float32 [4, 128, 128, 4, 128], P(None, ('lon', 'lat')), may hold values from -6 to 6
- error_weight: float32 [4, 128, 128, 4, 128], P(None, ('lon', 'lat')), may hold values from 0.3 to 3
- weighting: float32 [274, 128], replicated, may hold values from -0.375 to 0.375
Outputs:
- solution: float32 [2, 137, 128, 512], P(None, None, 'lon', 'lat')
- residual: float32 [2, 137, 128, 512], P(None, None, 'lon', 'lat')
Inputs may be any that keep to these rules, and one draw needn't show every extreme that they name: `slot_column_cells`: A cell of the sending device's block, numbered longitude-major over its 4 x 128 cells; only slots below the matching count are read. `column_counts`: at every timestep some owner receives 4 live slots from every sending device.
All inputs are finite; a program needn't handle non-finite values.
Results may differ from a plain program's by a relative error of at most 0.00016.
Values sent between devices are 32-bit elements; how exact they have to be, the bound alone decides.
No kernel may reach another device: no remote copies, remote signals or barrier semaphores. Data moves between devices by JAX's collectives and lax.ppermute only.
A program may use at most 128 MiB of HBM per device.

v0:
```python
import jax
import jax.numpy as jnp
from jax import lax
from jax.sharding import PartitionSpec as P

ITERS = 2


def padded(cells, sides, width, closed):
    for axis, dim in sides:
        count = lax.axis_size(axis)
        ends = count if closed else count - 1
        head = lax.slice_in_dim(cells, 0, width, axis=dim)
        tail = lax.slice_in_dim(cells, cells.shape[dim] - width, cells.shape[dim], axis=dim)
        cells = jnp.concatenate(
            [
                lax.ppermute(tail, axis, [(i, (i + 1) % count) for i in range(ends)]),
                cells,
                lax.ppermute(head, axis, [((i + 1) % count, i) for i in range(ends)]),
            ],
            axis=dim,
        )
    return cells


def extend_halo(states):
    lon_padded = padded(states, (("lon", 2),), 1, True)
    lat_padded = padded(states, (("lat", 3),), 1, False)
    return (lon_padded, lat_padded)


def advance(states, east_courant, north_courant):
    lon_padded, lat_padded = extend_halo(states)
    result = (1.0 - jnp.abs(east_courant) - jnp.abs(north_courant)) * states
    result = result + jnp.maximum(east_courant, 0.0) * lon_padded[:, :, :-2]
    result = result + jnp.maximum(-east_courant, 0.0) * lon_padded[:, :, 2:]
    result = result + jnp.maximum(north_courant, 0.0) * lat_padded[:, :, :, :-2]
    result = result + jnp.maximum(-north_courant, 0.0) * lat_padded[:, :, :, 2:]
    return result


def retreat(states, east_rim, north_rim):
    east_courant = east_rim[:, 1:-1]
    north_courant = north_rim[:, :, 1:-1]
    lon_padded, lat_padded = extend_halo(states)
    result = (1.0 - jnp.abs(east_courant) - jnp.abs(north_courant)) * states
    result = result + jnp.maximum(east_rim[:, 2:], 0.0) * lon_padded[:, :, 2:]
    result = result + jnp.maximum(-east_rim[:, :-2], 0.0) * lon_padded[:, :, :-2]
    result = result + jnp.maximum(north_rim[:, :, 2:], 0.0) * lat_padded[:, :, :, 2:]
    result = result + jnp.maximum(-north_rim[:, :, :-2], 0.0) * lat_padded[:, :, :, :-2]
    return result


def squared_norm(residual):
    return lax.psum(jnp.sum(residual * residual), ("lon", "lat"))


def body(courant, slot_column_cells, column_counts, innovations, error_weight, weighting):
    time_moments = courant.shape[0]
    vertical_levels = courant.shape[2]
    slab_extent = courant.shape[3]
    band_extent = courant.shape[4]
    owner_devices = slot_column_cells.shape[2]
    slot_capacity = slot_column_cells.shape[3]
    column_depth = 2 * vertical_levels
    cell_count = slab_extent * band_extent
    highest = lax.Precision.HIGHEST
    slot_lookup = slot_column_cells[:, 0].reshape(time_moments, owner_devices * slot_capacity)
    slot_position = lax.broadcasted_iota(jnp.int32, (time_moments, owner_devices, slot_capacity), 2)
    active = (slot_position < column_counts[:, 0][:, :, None]).astype(jnp.float32)
    longitude_edges, latitude_edges = extend_halo(
        courant.reshape(time_moments * 2, vertical_levels, slab_extent, band_extent)
    )
    weights_here = error_weight[:, 0]
    target_field = weights_here * innovations[:, 0]

    def spread(weighted):
        return jnp.einsum("gch,kh->gck", weighted, weighting, precision=highest)

    def deposit(sensitivity, gradient, time_moment):
        masked = gradient * active[time_moment][:, :, None]
        flattened = sensitivity.reshape(column_depth, cell_count)
        flattened = flattened.at[:, slot_lookup[time_moment]].add(
            masked.reshape(owner_devices * slot_capacity, column_depth).T
        )
        return flattened.reshape(sensitivity.shape)

    def owner_contribution(weighted):
        return spread(weighted)

    def adjoint_sweep(payloads):
        sensitivity = jnp.zeros((2, vertical_levels, slab_extent, band_extent), jnp.float32)
        for time_moment in reversed(range(time_moments)):
            gradient = lax.all_to_all(
                payloads[time_moment], ("lon", "lat"), split_axis=0, concat_axis=0, tiled=True
            )
            sensitivity = deposit(sensitivity, gradient, time_moment)
            sensitivity = retreat(
                sensitivity, longitude_edges[2 * time_moment], latitude_edges[2 * time_moment + 1]
            )
        return sensitivity

    right_hand_side = adjoint_sweep(
        [owner_contribution(target_field[time_moment]) for time_moment in range(time_moments)]
    )
    solution = jnp.zeros((2, vertical_levels, slab_extent, band_extent), jnp.float32)
    residual = right_hand_side
    direction = right_hand_side
    residual_norm = squared_norm(residual)
    for iteration in range(ITERS):
        tangent_states = direction
        tangent_payloads = []
        for tangent_time_moment in range(time_moments):
            tangent_states = advance(
                tangent_states, courant[tangent_time_moment, 0], courant[tangent_time_moment, 1]
            )
            select_flattened = tangent_states.reshape(column_depth, cell_count)
            columns = jnp.take(select_flattened, slot_lookup[tangent_time_moment], axis=1)
            columns = columns.T.reshape(owner_devices, slot_capacity, column_depth)
            tangent_columns = columns * active[tangent_time_moment][:, :, None]
            arrived = lax.all_to_all(
                tangent_columns, ("lon", "lat"), split_axis=0, concat_axis=0, tiled=True
            )
            tangent_payloads.append(
                spread(
                    weights_here[tangent_time_moment]
                    * jnp.einsum("gck,kh->gch", arrived, weighting, precision=highest)
                )
            )
        hessian_image = direction + adjoint_sweep(tangent_payloads)
        curvature = lax.psum(jnp.sum(direction * hessian_image), ("lon", "lat"))
        step_length = residual_norm / curvature
        solution = solution + step_length * direction
        residual = residual - step_length * hessian_image
        if iteration + 1 < ITERS:
            updated = squared_norm(residual)
            direction = residual + updated / residual_norm * direction
            residual_norm = updated
    return (solution, residual)


def solution(mesh):
    in_specs = (
        P(None, None, None, "lon", "lat"),
        P(None, ("lon", "lat"), None, None),
        P(None, ("lon", "lat"), None),
        P(None, ("lon", "lat"), None, None, None),
        P(None, ("lon", "lat"), None, None, None),
        P(),
    )
    out_specs = (P(None, None, "lon", "lat"), P(None, None, "lon", "lat"))
    return jax.shard_map(body, mesh=mesh, in_specs=in_specs, out_specs=out_specs, check_vma=False)
```

profile of v0, /device:TPU:1, one launch (start us, length us, event | category | flops | bytes accessed | tf_op | source)
XLA Modules:
  0.0 1227.3 jit_solution(17305340132202456047)
XLA Ops:
  26.5 13.0 %all-to-all-start = ((f32[128,4,274]{2,1,0:T(4,128)}), f32[128,4,274]{2,1,0:T(4,128)}, u32[]{:S(2)}, u32[]{:S(2)}) async-start(f32[128,4,274]{2,1,0:T(4,128)} %copy.1495), calls=%async_computation | async-start | bytes 1572864 | tf_op jit(solution)/shard_map/all_to_all | solution.py:94
  57.3 10.4 all-to-all-start.1
  81.0 13.8 %pad_maximum_fusion.84 = (f32[1,137,4,130]{3,0,2,1:T(1,128)}, f32[1,137,4,130]{3,0,2,1:T(1,128)}, f32[1,137,4,130]{3,0,2,1:T(1,128)}, f32[1,137,4,130]{3,0,2,1:T(1,128)}) fusion(f32[8,137,4,1]{3,0,2,1:T(8,128)} %copy.1476, f32[8,137,4,128]{3,0,2,1:T(8,128)S(1)} %bitcast.277, f32[8,137,4,1]{3,0,2,1:T(8,128)} %copy.1475), kind=kLoop, calls=%fused_computation.287 | loop fusion | flops 569920 | bytes 3419520 | tf_op jit(solution)/shard_map/slice | solution.py:99
  94.8 10.2 all-to-all-start.2
  108.6 12.7 %all-to-all-done.2 = f32[128,4,274]{2,1,0:T(4,128)} async-done(((f32[128,4,274]{2,1,0:T(4,128)}), f32[128,4,274]{2,1,0:T(4,128)}, u32[]{:S(2)}, u32[]{:S(2)}) %all-to-all-start.2) | async-done | bytes 561184 | tf_op jit(solution)/shard_map/all_to_all | solution.py:94
  121.3 5.2 all-to-all-start.3
  131.7 5.1 scatter_custom_fusion
  146.7 4.6 collective-permute-start.7
  168.1 4.6 pad_maximum_fusion.89
  218.1 4.6 collective-permute-start.15
  222.6 5.1 collective-permute-start.12
  248.5 7.6 collective-permute-start.16
  294.0 6.8 collective-permute-start.25
  310.0 9.4 all-to-all-start.10
  356.6 4.9 collective-permute-start.34
  380.6 10.1 all-to-all-start.8
  407.0 8.5 all-to-all-start.4
  420.5 11.3 all-to-all-done.4
  443.2 9.2 all-to-all-done.6
  452.4 4.8 all-to-all-start.5
  464.4 9.2 all-to-all-done.5
  482.3 5.0 scatter_custom_fusion.4
  496.8 4.6 collective-permute-start.39
  505.4 12.6 %all-to-all-start.9 = ((f32[128,4,274]{2,1,0:T(4,128)}), f32[128,4,274]{2,1,0:T(4,128)}, u32[]{:S(2)}, u32[]{:S(2)}) async-start(f32[128,4,274]{2,1,0:T(4,128)} %copy.1590), calls=%async_computation.9 | async-start | bytes 1572864 | tf_op jit(solution)/shard_map/all_to_all | solution.py:94
  531.4 4.5 scatter_fusion.3
  543.0 4.8 collective-permute-start.43
  550.9 12.5 %all-to-all-start.11 = ((f32[128,4,274]{2,1,0:T(4,128)}), f32[128,4,274]{2,1,0:T(4,128)}, u32[]{:S(2)}, u32[]{:S(2)}) async-start(f32[128,4,274]{2,1,0:T(4,128)} %copy.1601), calls=%async_computation.11 | async-start | bytes 1572864 | tf_op jit(solution)/shard_map/all_to_all | solution.py:94
  576.8 4.5 scatter_fusion.4
  606.9 4.9 scatter_fusion.5
  615.0 4.7 collective-permute-start.48
  633.0 6.1 multiply_reduce_fusion.2
  639.0 70.6 %all-reduce = (f32[]{:T(128)}, f32[]{:T(128)}) all-reduce(f32[]{:T(128)} %get-tuple-element.4, f32[]{:T(128)} %get-tuple-element.3), channel_id=1, replica_groups=mesh['lon'=32,'lat'=4] {'lon','lat'}, use_global_device_ids=true, to_apply=%region_5.0 | all-reduce | flops 2 | bytes 16 | tf_op jit(solution)/shard_map/psum | solution.py:55
  714.1 62.5 %psum.30 = f32[]{:T(128)} all-reduce(f32[]{:T(128)} %multiply_reduce_fusion.1), channel_id=1, replica_groups=mesh['lon'=32,'lat'=4] {'lon','lat'}, use_global_device_ids=true, to_apply=%region_13.15 | all-reduce | flops 1 | bytes 8 | tf_op jit(solution)/shard_map/psum | solution.py:55
  823.2 10.4 all-to-all-start.18
  872.7 4.9 collective-permute-start.66
  898.9 10.7 all-to-all-start.16
  926.0 8.6 all-to-all-start.12
  940.4 10.4 all-to-all-done.12
  963.0 8.5 all-to-all-done.14
  971.4 4.8 all-to-all-start.13
  984.4 8.3 all-to-all-done.13
  992.7 5.2 all-to-all-start.15
  1019.6 12.6 %all-to-all-start.17 = ((f32[128,4,274]{2,1,0:T(4,128)}), f32[128,4,274]{2,1,0:T(4,128)}, u32[]{:S(2)}, u32[]{:S(2)}) async-start(f32[128,4,274]{2,1,0:T(4,128)} %copy.1643), calls=%async_computation.17 | async-start | bytes 1572864 | tf_op jit(solution)/shard_map/all_to_all | solution.py:94
  1063.9 12.5 %all-to-all-start.19 = ((f32[128,4,274]{2,1,0:T(4,128)}), f32[128,4,274]{2,1,0:T(4,128)}, u32[]{:S(2)}, u32[]{:S(2)}) async-start(f32[128,4,274]{2,1,0:T(4,128)} %copy.1652), calls=%async_computation.19 | async-start | bytes 1572864 | tf_op jit(solution)/shard_map/all_to_all | solution.py:94
  1119.8 4.7 scatter_fusion.8
  1127.8 4.8 collective-permute-start.80
  1145.7 5.4 multiply_reduce_fusion
  1151.1 70.6 %psum.31 = f32[]{:T(128)} all-reduce(f32[]{:T(128)} %get-tuple-element.7), channel_id=1, replica_groups=mesh['lon'=32,'lat'=4] {'lon','lat'}, use_global_device_ids=true, to_apply=%region_19.21 | all-reduce | flops 1 | bytes 8 | tf_op jit(solution)/shard_map/psum | solution.py:131
  (738 shorter events, 669.2 us)
Async XLA Ops:
  9.6 63.2 %collective-permute-start.2 = (f32[8,137,4,1]{1,0,3,2:T(8,128)S(1)}, f32[8,137,4,1]{1,0,3,2:T(8,128)S(1)}, u32[]{:S(2)}, u32[]{:S(2)}) collective-permute-start(f32[8,137,4,1]{1,0,3,2:T(8,128)S(1)} %copy.1473), channel_id=1, source_target_pairs={{0,1},{1,2},{2,3},{4,5},{5,6},{6,7},{8,9},{9,10},{10,11},{12,13},{... | collective-permute-start | bytes 52616 | tf_op jit(solution)/shard_map/ppermute | solution.py:17
  17.0 59.5 %collective-permute-start.3 = (f32[8,137,4,1]{1,0,3,2:T(8,128)S(1)}, f32[8,137,4,1]{1,0,3,2:T(8,128)}, u32[]{:S(2)}, u32[]{:S(2)}) collective-permute-start(f32[8,137,4,1]{1,0,3,2:T(8,128)S(1)} %copy.1474), channel_id=1, source_target_pairs={{1,0},{2,1},{3,2},{5,4},{6,5},{7,6},{9,8},{10,9},{11,10},{13,12},{... | collective-permute-start | bytes 52616 | tf_op jit(solution)/shard_map/ppermute | solution.py:19
  19.5 148.6 %collective-permute-start = (f32[8,137,1,128]{3,0,2,1:T(8,128)}, f32[8,137,1,128]{3,0,2,1:T(8,128)}, u32[]{:S(2)}, u32[]{:S(2)}) collective-permute-start(f32[8,137,1,128]{3,0,2,1:T(8,128)} %get-tuple-element.38), channel_id=1, source_target_pairs={{0,4},{4,8},{8,12},{12,16},{16,20},{20,24},{24,28},{28,32},{32,36}... | collective-permute-start | bytes 1683464 | tf_op jit(solution)/shard_map/ppermute | solution.py:17
  21.6 146.5 %collective-permute-start.1 = (f32[8,137,1,128]{3,0,2,1:T(8,128)}, f32[8,137,1,128]{3,0,2,1:T(8,128)}, u32[]{:S(2)}, u32[]{:S(2)}) collective-permute-start(f32[8,137,1,128]{3,0,2,1:T(8,128)} %get-tuple-element.39), channel_id=1, source_target_pairs={{4,0},{8,4},{12,8},{16,12},{20,16},{24,20},{28,24},{32,28},{36,32}... | collective-permute-start | bytes 1683464 | tf_op jit(solution)/shard_map/ppermute | solution.py:19
  26.5 30.9 %all-to-all-start = ((f32[128,4,274]{2,1,0:T(4,128)}), f32[128,4,274]{2,1,0:T(4,128)}, u32[]{:S(2)}, u32[]{:S(2)}) async-start(f32[128,4,274]{2,1,0:T(4,128)} %copy.1495), calls=%async_computation | async-start | bytes 1572864 | tf_op jit(solution)/shard_map/all_to_all | solution.py:94
  57.3 37.4 %all-to-all-start.1 = ((f32[128,4,274]{2,1,0:T(4,128)}), f32[128,4,274]{2,1,0:T(4,128)S(1)}, u32[]{:S(2)}, u32[]{:S(2)}) async-start(f32[128,4,274]{2,1,0:T(4,128)} %copy.1508), calls=%async_computation.1 | async-start | bytes 1572864 | tf_op jit(solution)/shard_map/all_to_all | solution.py:94
  94.8 26.5 %all-to-all-start.2 = ((f32[128,4,274]{2,1,0:T(4,128)}), f32[128,4,274]{2,1,0:T(4,128)}, u32[]{:S(2)}, u32[]{:S(2)}) async-start(f32[128,4,274]{2,1,0:T(4,128)} %copy.1522), calls=%async_computation.2 | async-start | bytes 1572864 | tf_op jit(solution)/shard_map/all_to_all | solution.py:94
  121.3 32.6 %all-to-all-start.3 = ((f32[128,4,274]{2,1,0:T(4,128)}), f32[128,4,274]{2,1,0:T(4,128)}, u32[]{:S(2)}, u32[]{:S(2)}) async-start(f32[128,4,274]{2,1,0:T(4,128)} %copy.1536), calls=%async_computation.3 | async-start | bytes 1572864 | tf_op jit(solution)/shard_map/all_to_all | solution.py:94
  152.2 22.7 %collective-permute-start.4 = (f32[2,137,1,128]{3,2,1,0:T(1,128)}, f32[2,137,1,128]{3,2,1,0:T(1,128)}, u32[]{:S(2)}, u32[]{:S(2)}) collective-permute-start(f32[2,137,1,128]{3,2,1,0:T(1,128)} %get-tuple-element.134), channel_id=1, source_target_pairs={{4,0},{8,4},{12,8},{16,12},{20,16},{24,20},{28,24},{32,28},{36,32}... | collective-permute-start | bytes 420872 | tf_op jit(solution)/shard_map/ppermute | solution.py:19
  287.3 32.1 %collective-permute-start.26 = (f32[2,137,4,1]{1,2,3,0:T(4,128)S(1)}, f32[2,137,4,1]{1,2,3,0:T(4,128)S(1)}, u32[]{:S(2)}, u32[]{:S(2)}) collective-permute-start(f32[2,137,4,1]{1,2,3,0:T(4,128)S(1)} %copy.1555), channel_id=1, source_target_pairs={{0,1},{1,2},{2,3},{4,5},{5,6},{6,7},{8,9},{9,10},{10,11},{12,13},{... | collective-permute-start | bytes 13160 | tf_op jit(solution)/shard_map/ppermute | solution.py:17
  292.7 28.0 %collective-permute-start.27 = (f32[2,137,4,1]{1,2,3,0:T(4,128)}, f32[2,137,4,1]{1,2,3,0:T(4,128)}, u32[]{:S(2)}, u32[]{:S(2)}) collective-permute-start(f32[2,137,4,1]{1,2,3,0:T(4,128)} %copy.1557), channel_id=1, source_target_pairs={{1,0},{2,1},{3,2},{5,4},{6,5},{7,6},{9,8},{10,9},{11,10},{13,12},{... | collective-permute-start | bytes 13160 | tf_op jit(solution)/shard_map/ppermute | solution.py:19
  293.9 28.6 %collective-permute-start.24 = (f32[2,137,1,128]{3,2,1,0:T(1,128)}, f32[2,137,1,128]{3,2,1,0:T(1,128)}, u32[]{:S(2)}, u32[]{:S(2)}) collective-permute-start(f32[2,137,1,128]{3,2,1,0:T(1,128)} %get-tuple-element.114), channel_id=1, source_target_pairs={{0,4},{4,8},{8,12},{12,16},{16,20},{20,24},{24,28},{28,32},{32,36}... | collective-permute-start | bytes 420872 | tf_op jit(solution)/shard_map/ppermute | solution.py:17
  294.0 28.5 %collective-permute-start.25 = (f32[2,137,1,128]{3,2,1,0:T(1,128)}, f32[2,137,1,128]{3,2,1,0:T(1,128)}, u32[]{:S(2)}, u32[]{:S(2)}) collective-permute-start(f32[2,137,1,128]{3,2,1,0:T(1,128)} %get-tuple-element.115), channel_id=1, source_target_pairs={{4,0},{8,4},{12,8},{16,12},{20,16},{24,20},{28,24},{32,28},{36,32}... | collective-permute-start | bytes 420872 | tf_op jit(solution)/shard_map/ppermute | solution.py:19
  310.0 70.6 %all-to-all-start.10 = ((f32[128,4,274]{2,1,0:T(4,128)}), f32[128,4,274]{2,1,0:T(4,128)}, u32[]{:S(2)}, u32[]{:S(2)}) async-start(f32[128,4,274]{2,1,0:T(4,128)} %broadcast_multiply_fusion.3), calls=%async_computation.10 | async-start | bytes 1572864 | tf_op jit(solution)/shard_map/all_to_all | solution.py:121
  364.7 25.9 %collective-permute-start.32 = (f32[2,137,1,128]{3,2,1,0:T(1,128)}, f32[2,137,1,128]{3,2,1,0:T(1,128)}, u32[]{:S(2)}, u32[]{:S(2)}) collective-permute-start(f32[2,137,1,128]{3,2,1,0:T(1,128)} %get-tuple-element.106), channel_id=1, source_target_pairs={{0,4},{4,8},{8,12},{12,16},{16,20},{20,24},{24,28},{28,32},{32,36}... | collective-permute-start | bytes 420872 | tf_op jit(solution)/shard_map/ppermute | solution.py:17
  366.7 23.9 %collective-permute-start.33 = (f32[2,137,1,128]{3,2,1,0:T(1,128)}, f32[2,137,1,128]{3,2,1,0:T(1,128)}, u32[]{:S(2)}, u32[]{:S(2)}) collective-permute-start(f32[2,137,1,128]{3,2,1,0:T(1,128)} %get-tuple-element.107), channel_id=1, source_target_pairs={{4,0},{8,4},{12,8},{16,12},{20,16},{24,20},{28,24},{32,28},{36,32}... | collective-permute-start | bytes 420872 | tf_op jit(solution)/shard_map/ppermute | solution.py:19
  380.6 26.4 %all-to-all-start.8 = ((f32[128,4,274]{2,1,0:T(4,128)}), f32[128,4,274]{2,1,0:T(4,128)}, u32[]{:S(2)}, u32[]{:S(2)}) async-start(f32[128,4,274]{2,1,0:T(4,128)} %broadcast_multiply_fusion.8), calls=%async_computation.8 | async-start | bytes 1572864 | tf_op jit(solution)/shard_map/all_to_all | solution.py:121
  407.0 24.7 %all-to-all-start.4 = ((f32[128,4,274]{2,1,0:T(4,128)}), f32[128,4,274]{2,1,0:T(4,128)}, u32[]{:S(2)}, u32[]{:S(2)}) async-start(f32[128,4,274]{2,1,0:T(4,128)} %broadcast_multiply_fusion.18), calls=%async_computation.4 | async-start | bytes 1572864 | tf_op jit(solution)/shard_map/all_to_all | solution.py:121
  473.7 30.8 %all-to-all-start.7 = ((f32[128,4,274]{2,1,0:T(4,128)}), f32[128,4,274]{2,1,0:T(4,128)S(1)}, u32[]{:S(2)}, u32[]{:S(2)}) async-start(f32[128,4,274]{2,1,0:T(4,128)} %copy.1579), calls=%async_computation.7 | async-start | bytes 1572864 | tf_op jit(solution)/shard_map/all_to_all | solution.py:94
  493.5 29.1 %collective-permute-start.38 = (f32[2,137,4,1]{1,2,3,0:T(4,128)S(1)}, f32[2,137,4,1]{1,2,3,0:T(4,128)}, u32[]{:S(2)}, u32[]{:S(2)}) collective-permute-start(f32[2,137,4,1]{1,2,3,0:T(4,128)S(1)} %copy.1571), channel_id=1, source_target_pairs={{1,0},{2,1},{3,2},{5,4},{6,5},{7,6},{9,8},{10,9},{11,10},{13,12},{... | collective-permute-start | bytes 13160 | tf_op jit(solution)/shard_map/ppermute | solution.py:19
  496.8 27.7 %collective-permute-start.39 = (f32[2,137,4,1]{1,2,3,0:T(4,128)}, f32[2,137,4,1]{1,2,3,0:T(4,128)}, u32[]{:S(2)}, u32[]{:S(2)}) collective-permute-start(f32[2,137,4,1]{1,2,3,0:T(4,128)} %copy.1573), channel_id=1, source_target_pairs={{0,1},{1,2},{2,3},{4,5},{5,6},{6,7},{8,9},{9,10},{10,11},{12,13},{... | collective-permute-start | bytes 13160 | tf_op jit(solution)/shard_map/ppermute | solution.py:17
  502.3 24.1 %collective-permute-start.36 = (f32[2,137,1,128]{3,2,1,0:T(1,128)}, f32[2,137,1,128]{3,2,1,0:T(1,128)}, u32[]{:S(2)}, u32[]{:S(2)}) collective-permute-start(f32[2,137,1,128]{3,2,1,0:T(1,128)} %get-tuple-element.102), channel_id=1, source_target_pairs={{4,0},{8,4},{12,8},{16,12},{20,16},{24,20},{28,24},{32,28},{36,32}... | collective-permute-start | bytes 420872 | tf_op jit(solution)/shard_map/ppermute | solution.py:19
  504.0 22.4 %collective-permute-start.37 = (f32[2,137,1,128]{3,2,1,0:T(1,128)}, f32[2,137,1,128]{3,2,1,0:T(1,128)}, u32[]{:S(2)}, u32[]{:S(2)}) collective-permute-start(f32[2,137,1,128]{3,2,1,0:T(1,128)} %get-tuple-element.103), channel_id=1, source_target_pairs={{0,4},{4,8},{8,12},{12,16},{16,20},{20,24},{24,28},{28,32},{32,36}... | collective-permute-start | bytes 420872 | tf_op jit(solution)/shard_map/ppermute | solution.py:17
  505.4 45.5 %all-to-all-start.9 = ((f32[128,4,274]{2,1,0:T(4,128)}), f32[128,4,274]{2,1,0:T(4,128)}, u32[]{:S(2)}, u32[]{:S(2)}) async-start(f32[128,4,274]{2,1,0:T(4,128)} %copy.1590), calls=%async_computation.9 | async-start | bytes 1572864 | tf_op jit(solution)/shard_map/all_to_all | solution.py:94
  540.8 27.3 %collective-permute-start.42 = (f32[2,137,4,1]{1,2,3,0:T(4,128)S(1)}, f32[2,137,4,1]{1,2,3,0:T(4,128)}, u32[]{:S(2)}, u32[]{:S(2)}) collective-permute-start(f32[2,137,4,1]{1,2,3,0:T(4,128)S(1)} %copy.1582), channel_id=1, source_target_pairs={{1,0},{2,1},{3,2},{5,4},{6,5},{7,6},{9,8},{10,9},{11,10},{13,12},{... | collective-permute-start | bytes 13160 | tf_op jit(solution)/shard_map/ppermute | solution.py:19
  543.0 26.9 %collective-permute-start.43 = (f32[2,137,4,1]{1,2,3,0:T(4,128)}, f32[2,137,4,1]{1,2,3,0:T(4,128)}, u32[]{:S(2)}, u32[]{:S(2)}) collective-permute-start(f32[2,137,4,1]{1,2,3,0:T(4,128)} %copy.1584), channel_id=1, source_target_pairs={{0,1},{1,2},{2,3},{4,5},{5,6},{6,7},{8,9},{9,10},{10,11},{12,13},{... | collective-permute-start | bytes 13160 | tf_op jit(solution)/shard_map/ppermute | solution.py:17
  548.7 23.1 %collective-permute-start.40 = (f32[2,137,1,128]{3,2,1,0:T(1,128)}, f32[2,137,1,128]{3,2,1,0:T(1,128)S(1)}, u32[]{:S(2)}, u32[]{:S(2)}) collective-permute-start(f32[2,137,1,128]{3,2,1,0:T(1,128)} %get-tuple-element.98), channel_id=1, source_target_pairs={{4,0},{8,4},{12,8},{16,12},{20,16},{24,20},{28,24},{32,28},{36,32}... | collective-permute-start | bytes 420872 | tf_op jit(solution)/shard_map/ppermute | solution.py:19
  550.4 21.4 %collective-permute-start.41 = (f32[2,137,1,128]{3,2,1,0:T(1,128)}, f32[2,137,1,128]{3,2,1,0:T(1,128)}, u32[]{:S(2)}, u32[]{:S(2)}) collective-permute-start(f32[2,137,1,128]{3,2,1,0:T(1,128)} %get-tuple-element.99), channel_id=1, source_target_pairs={{0,4},{4,8},{8,12},{12,16},{16,20},{20,24},{24,28},{28,32},{32,36}... | collective-permute-start | bytes 420872 | tf_op jit(solution)/shard_map/ppermute | solution.py:17
  550.9 44.1 %all-to-all-start.11 = ((f32[128,4,274]{2,1,0:T(4,128)}), f32[128,4,274]{2,1,0:T(4,128)}, u32[]{:S(2)}, u32[]{:S(2)}) async-start(f32[128,4,274]{2,1,0:T(4,128)} %copy.1601), calls=%async_computation.11 | async-start | bytes 1572864 | tf_op jit(solution)/shard_map/all_to_all | solution.py:94
  800.9 32.7 %collective-permute-start.58 = (f32[2,137,4,1]{1,2,3,0:T(4,128)}, f32[2,137,4,1]{1,2,3,0:T(4,128)}, u32[]{:S(2)}, u32[]{:S(2)}) collective-permute-start(f32[2,137,4,1]{1,2,3,0:T(4,128)} %copy.1612), channel_id=1, source_target_pairs={{0,1},{1,2},{2,3},{4,5},{5,6},{6,7},{8,9},{9,10},{10,11},{12,13},{... | collective-permute-start | bytes 13160 | tf_op jit(solution)/shard_map/ppermute | solution.py:17
  806.2 29.2 %collective-permute-start.59 = (f32[2,137,4,1]{1,2,3,0:T(4,128)}, f32[2,137,4,1]{1,2,3,0:T(4,128)}, u32[]{:S(2)}, u32[]{:S(2)}) collective-permute-start(f32[2,137,4,1]{1,2,3,0:T(4,128)} %copy.1614), channel_id=1, source_target_pairs={{1,0},{2,1},{3,2},{5,4},{6,5},{7,6},{9,8},{10,9},{11,10},{13,12},{... | collective-permute-start | bytes 13160 | tf_op jit(solution)/shard_map/ppermute | solution.py:19
  807.5 29.8 %collective-permute-start.56 = (f32[2,137,1,128]{3,2,1,0:T(1,128)}, f32[2,137,1,128]{3,2,1,0:T(1,128)}, u32[]{:S(2)}, u32[]{:S(2)}) collective-permute-start(f32[2,137,1,128]{3,2,1,0:T(1,128)} %get-tuple-element.82), channel_id=1, source_target_pairs={{0,4},{4,8},{8,12},{12,16},{16,20},{20,24},{24,28},{28,32},{32,36}... | collective-permute-start | bytes 420872 | tf_op jit(solution)/shard_map/ppermute | solution.py:17
  811.0 26.3 %collective-permute-start.57 = (f32[2,137,1,128]{3,2,1,0:T(1,128)}, f32[2,137,1,128]{3,2,1,0:T(1,128)}, u32[]{:S(2)}, u32[]{:S(2)}) collective-permute-start(f32[2,137,1,128]{3,2,1,0:T(1,128)} %get-tuple-element.83), channel_id=1, source_target_pairs={{4,0},{8,4},{12,8},{16,12},{20,16},{24,20},{28,24},{32,28},{36,32}... | collective-permute-start | bytes 420872 | tf_op jit(solution)/shard_map/ppermute | solution.py:19
  823.2 75.8 %all-to-all-start.18 = ((f32[128,4,274]{2,1,0:T(4,128)}), f32[128,4,274]{2,1,0:T(4,128)}, u32[]{:S(2)}, u32[]{:S(2)}) async-start(f32[128,4,274]{2,1,0:T(4,128)} %broadcast_multiply_fusion.1), calls=%async_computation.18 | async-start | bytes 1572864 | tf_op jit(solution)/shard_map/all_to_all | solution.py:121
  872.7 22.5 %collective-permute-start.66 = (f32[2,137,4,1]{1,2,3,0:T(4,128)S(1)}, f32[2,137,4,1]{1,2,3,0:T(4,128)}, u32[]{:S(2)}, u32[]{:S(2)}) collective-permute-start(f32[2,137,4,1]{1,2,3,0:T(4,128)S(1)} %copy.1620), channel_id=1, source_target_pairs={{0,1},{1,2},{2,3},{4,5},{5,6},{6,7},{8,9},{9,10},{10,11},{12,13},{... | collective-permute-start | bytes 13160 | tf_op jit(solution)/shard_map/ppermute | solution.py:17
  881.8 27.8 %collective-permute-start.64 = (f32[2,137,1,128]{3,2,1,0:T(1,128)}, f32[2,137,1,128]{3,2,1,0:T(1,128)}, u32[]{:S(2)}, u32[]{:S(2)}) collective-permute-start(f32[2,137,1,128]{3,2,1,0:T(1,128)} %get-tuple-element.74), channel_id=1, source_target_pairs={{0,4},{4,8},{8,12},{12,16},{16,20},{20,24},{24,28},{28,32},{32,36}... | collective-permute-start | bytes 420872 | tf_op jit(solution)/shard_map/ppermute | solution.py:17
  883.8 25.8 %collective-permute-start.65 = (f32[2,137,1,128]{3,2,1,0:T(1,128)}, f32[2,137,1,128]{3,2,1,0:T(1,128)}, u32[]{:S(2)}, u32[]{:S(2)}) collective-permute-start(f32[2,137,1,128]{3,2,1,0:T(1,128)} %get-tuple-element.75), channel_id=1, source_target_pairs={{4,0},{8,4},{12,8},{16,12},{20,16},{24,20},{28,24},{32,28},{36,32}... | collective-permute-start | bytes 420872 | tf_op jit(solution)/shard_map/ppermute | solution.py:19
  898.9 27.1 %all-to-all-start.16 = ((f32[128,4,274]{2,1,0:T(4,128)}), f32[128,4,274]{2,1,0:T(4,128)}, u32[]{:S(2)}, u32[]{:S(2)}) async-start(f32[128,4,274]{2,1,0:T(4,128)} %broadcast_multiply_fusion.6), calls=%async_computation.16 | async-start | bytes 1572864 | tf_op jit(solution)/shard_map/all_to_all | solution.py:121
  926.0 24.8 %all-to-all-start.12 = ((f32[128,4,274]{2,1,0:T(4,128)}), f32[128,4,274]{2,1,0:T(4,128)}, u32[]{:S(2)}, u32[]{:S(2)}) async-start(f32[128,4,274]{2,1,0:T(4,128)} %broadcast_multiply_fusion.16), calls=%async_computation.12 | async-start | bytes 1572864 | tf_op jit(solution)/shard_map/all_to_all | solution.py:121
  992.7 26.9 %all-to-all-start.15 = ((f32[128,4,274]{2,1,0:T(4,128)}), f32[128,4,274]{2,1,0:T(4,128)}, u32[]{:S(2)}, u32[]{:S(2)}) async-start(f32[128,4,274]{2,1,0:T(4,128)} %copy.1634), calls=%async_computation.15 | async-start | bytes 1572864 | tf_op jit(solution)/shard_map/all_to_all | solution.py:94
  1009.8 27.0 %collective-permute-start.70 = (f32[2,137,4,1]{1,2,3,0:T(4,128)S(1)}, f32[2,137,4,1]{1,2,3,0:T(4,128)S(1)}, u32[]{:S(2)}, u32[]{:S(2)}) collective-permute-start(f32[2,137,4,1]{1,2,3,0:T(4,128)S(1)} %copy.1628), channel_id=1, source_target_pairs={{1,0},{2,1},{3,2},{5,4},{6,5},{7,6},{9,8},{10,9},{11,10},{13,12},{... | collective-permute-start | bytes 13160 | tf_op jit(solution)/shard_map/ppermute | solution.py:19
  1012.5 25.5 %collective-permute-start.71 = (f32[2,137,4,1]{1,2,3,0:T(4,128)S(1)}, f32[2,137,4,1]{1,2,3,0:T(4,128)S(1)}, u32[]{:S(2)}, u32[]{:S(2)}) collective-permute-start(f32[2,137,4,1]{1,2,3,0:T(4,128)S(1)} %copy.1630), channel_id=1, source_target_pairs={{0,1},{1,2},{2,3},{4,5},{5,6},{6,7},{8,9},{9,10},{10,11},{12,13},{... | collective-permute-start | bytes 13160 | tf_op jit(solution)/shard_map/ppermute | solution.py:17
  1017.4 21.7 %collective-permute-start.68 = (f32[2,137,1,128]{3,2,1,0:T(1,128)}, f32[2,137,1,128]{3,2,1,0:T(1,128)S(1)}, u32[]{:S(2)}, u32[]{:S(2)}) collective-permute-start(f32[2,137,1,128]{3,2,1,0:T(1,128)} %get-tuple-element.70), channel_id=1, source_target_pairs={{4,0},{8,4},{12,8},{16,12},{20,16},{24,20},{28,24},{32,28},{36,32}... | collective-permute-start | bytes 420872 | tf_op jit(solution)/shard_map/ppermute | solution.py:19
  1019.6 44.2 %all-to-all-start.17 = ((f32[128,4,274]{2,1,0:T(4,128)}), f32[128,4,274]{2,1,0:T(4,128)}, u32[]{:S(2)}, u32[]{:S(2)}) async-start(f32[128,4,274]{2,1,0:T(4,128)} %copy.1643), calls=%async_computation.17 | async-start | bytes 1572864 | tf_op jit(solution)/shard_map/all_to_all | solution.py:94
  1053.8 27.1 %collective-permute-start.74 = (f32[2,137,4,1]{1,2,3,0:T(4,128)S(1)}, f32[2,137,4,1]{1,2,3,0:T(4,128)S(1)}, u32[]{:S(2)}, u32[]{:S(2)}) collective-permute-start(f32[2,137,4,1]{1,2,3,0:T(4,128)S(1)} %copy.1637), channel_id=1, source_target_pairs={{1,0},{2,1},{3,2},{5,4},{6,5},{7,6},{9,8},{10,9},{11,10},{13,12},{... | collective-permute-start | bytes 13160 | tf_op jit(solution)/shard_map/ppermute | solution.py:19
  1056.5 25.6 %collective-permute-start.75 = (f32[2,137,4,1]{1,2,3,0:T(4,128)S(1)}, f32[2,137,4,1]{1,2,3,0:T(4,128)S(1)}, u32[]{:S(2)}, u32[]{:S(2)}) collective-permute-start(f32[2,137,4,1]{1,2,3,0:T(4,128)S(1)} %copy.1639), channel_id=1, source_target_pairs={{0,1},{1,2},{2,3},{4,5},{5,6},{6,7},{8,9},{9,10},{10,11},{12,13},{... | collective-permute-start | bytes 13160 | tf_op jit(solution)/shard_map/ppermute | solution.py:17
  1061.7 21.6 %collective-permute-start.72 = (f32[2,137,1,128]{3,2,1,0:T(1,128)}, f32[2,137,1,128]{3,2,1,0:T(1,128)S(1)}, u32[]{:S(2)}, u32[]{:S(2)}) collective-permute-start(f32[2,137,1,128]{3,2,1,0:T(1,128)} %get-tuple-element.66), channel_id=1, source_target_pairs={{4,0},{8,4},{12,8},{16,12},{20,16},{24,20},{28,24},{32,28},{36,32}... | collective-permute-start | bytes 420872 | tf_op jit(solution)/shard_map/ppermute | solution.py:19
  1063.9 43.9 %all-to-all-start.19 = ((f32[128,4,274]{2,1,0:T(4,128)}), f32[128,4,274]{2,1,0:T(4,128)}, u32[]{:S(2)}, u32[]{:S(2)}) async-start(f32[128,4,274]{2,1,0:T(4,128)} %copy.1652), calls=%async_computation.19 | async-start | bytes 1572864 | tf_op jit(solution)/shard_map/all_to_all | solution.py:94
  (150 other events, 1867.2 us)
where the time goes:
time: 1240 us; the launch traced here: 1230 us
  starting transfers between devices  364 us (29%)
  local copies, waits for them, and re-layouts  331 us (27%)
  other arithmetic  211 us (17%)
  blocking collectives  204 us (16%)
  waiting for transfers between devices  79.2 us (6%)
  matrix products  31.1 us (3%)
    psum x2, blocking collectives, squared_norm(): return lax.psum(jnp.sum(residual * residual), ('lon', 'lat'))  133 us
    all_to_all x12, starting transfers between devices, adjoint_sweep(): lax.all_to_all(payloads[time_moment], ('lon', 'lat'), split_axis=0, conca...  108 us
    ppermute x42, starting transfers between devices, padded(): lax.ppermute(tail, axis, [(i, (i + 1) % count) for i in range(ends)])  105 us
    ppermute x42, starting transfers between devices, padded(): lax.ppermute(head, axis, [((i + 1) % count, i) for i in range(ends)])  85.4 us
    psum x1, blocking collectives, body(): curvature = lax.psum(jnp.sum(direction * hessian_image), ('lon', 'lat'))  70.6 us
    all_to_all x8, starting transfers between devices, body(): lax.all_to_all(tangent_columns, ('lon', 'lat'), split_axis=0, concat_axis...  65.3 us
    slice x45, local copies, waits for them, and re-layouts, padded(): head = lax.slice_in_dim(cells, 0, width, axis=dim)  54.9 us
    scatter-add x12, other arithmetic, deposit(): flattened.at[:, slot_lookup[time_moment]]  53.9 us
  transfers between devices with their start and end apart: 104, of which 12 were waited for; matrix products, arithmetic and copies ran while one was open for 38% of the time, Pallas kernels for 0%

commit v1 on v0

v1 whole, which is shorter than its diff:
```python
import functools

import jax
import jax.numpy as jnp
from jax import lax
from jax.experimental import pallas as pl
from jax.experimental.pallas import tpu as pltpu
from jax.sharding import PartitionSpec as P

F32 = jnp.float32
BF16 = jnp.bfloat16
NT = 4
SLAB = 4
BAND = 128
EXT = 3 * SLAB
PLANES = {(0, 1): 0, (0, 2): 1, (0, 3): 2, (1, 1): 3, (1, 2): 4, (2, 1): 5}
VMEM = pl.BlockSpec(memory_space=pltpu.VMEM)
SMEM = pl.BlockSpec(memory_space=pltpu.SMEM)


def call(kernel, shapes, inputs, scratch=(), specs=None, flops=0):
    nbytes = sum(x.size * x.dtype.itemsize for x in inputs)
    return pl.pallas_call(
        kernel,
        out_shape=[jax.ShapeDtypeStruct(s, F32) for s in shapes],
        in_specs=specs or [VMEM] * len(inputs),
        out_specs=[VMEM] * len(shapes),
        scratch_shapes=list(scratch),
        compiler_params=pltpu.CompilerParams(vmem_limit_bytes=40 << 20),
        cost_estimate=pl.CostEstimate(flops=flops, bytes_accessed=nbytes, transcendentals=0),
    )(*inputs)


def turn(x, shift):
    shift %= 128
    return pltpu.roll(x, shift, x.ndim - 1) if shift else x


def lanes(shape=(8, 128)):
    return lax.broadcasted_iota(jnp.int32, shape, len(shape) - 1)


def parts(u):
    plus = jnp.maximum(u, 0.0)
    return plus, plus - u


def factors(u, v):
    up, um = parts(u)
    vp, vm = parts(v)
    return 1.0 - (up + um) - (vp + vm), up, um, vp, vm


def coefficients(refs, t, e, rows):
    own, west, east = refs[:3]
    if e < SLAB:
        k = 2 * PLANES[t, SLAB - e]
        return west[k, rows], west[k + 1, rows]
    if e >= 2 * SLAB:
        k = 2 * PLANES[t, e - 2 * SLAB + 1]
        return east[k, rows], east[k + 1, rows]
    k = 8 * t + e - SLAB
    return own[k, rows], own[k + SLAB, rows]


def pack_coefficients(refs, t, rows, group):
    own, west, east = refs[3:]
    out = []
    for k in (0, 1):
        p = jnp.where(group < 4, turn(west[k, rows], -32 * t), turn(own[k, rows], 32 - 32 * t))
        p = jnp.where(group < 8, p, turn(east[k, rows], 64 - 32 * t))
        out.append(jnp.where(group < 12, p, 0.0))
    return out


def adjoint_sweep(coef, grads, out_own, out_west, out_east, out_pack, levels):
    def block(r, carry):
        r8 = pl.multiple_of(r * 8, 8)
        rows = pl.ds(r8, 8)
        lane = lanes()
        group, off = lane // 8, lane % 8
        low, high = lane == 0, lane == BAND - 1
        ys = [[None] * EXT, [None] * EXT]
        packs = [None, None]
        for t in reversed(range(NT)):
            first, last = t + 1, 10 - t
            for var in (0, 1):
                for e in range(SLAB, 2 * SLAB):
                    g = grads[t, pl.ds(pl.multiple_of(var * levels + r8, 8), 8), pl.ds((e - SLAB) * BAND, BAND)]
                    ys[var][e] = g if ys[var][e] is None else ys[var][e] + g
            news = [[None] * EXT, [None] * EXT]
            tts = [jnp.zeros((8, 128), F32)] * 2
            mixes, pouts = [None, None], [None, None]
            if t < NT - 1:
                pu, pv = pack_coefficients(coef, t, rows, group)
                c0, up, um, vp, vm = factors(pu, pv)
                for var in (0, 1):
                    p = packs[var]
                    a, b = vp * p, vm * p
                    mixes[var] = jnp.where(off == 4, a, b)
                    pouts[var] = (c0 * p + turn(up * p, -8) + turn(um * p, 8), a, b)

            def put(var, e, x):
                news[var][e] = x if news[var][e] is None else news[var][e] + x

            for e in range(first, last + 1):
                c0, up, um, vp, vm = factors(*coefficients(coef, t, e, rows))
                for var in (0, 1):
                    y = ys[var][e]
                    if y is None:
                        continue
                    a, b = vp * y, vm * y
                    edge = 0.0 if mixes[var] is None else turn(mixes[var], -(8 * e + 4))
                    here = c0 * y + turn(jnp.where(low, edge, a), -1) + turn(jnp.where(high, edge, b), 1)
                    put(var, e, here)
                    put(var, e - 1, up * y)
                    put(var, e + 1, um * y)
                    mixed = turn(jnp.where(low, a, b), 8 * e + 4)
                    tts[var] = jnp.where((lane == 8 * e + 3) | (lane == 8 * e + 4), mixed, tts[var])
            for var in (0, 1):
                if pouts[var] is None:
                    packs[var] = turn(jnp.where(off == 4, tts[var], 0.0), -1) + turn(jnp.where(off == 3, tts[var], 0.0), 1)
                else:
                    rest, a, b = pouts[var]
                    packs[var] = rest + turn(jnp.where(off == 4, tts[var], a), -1) + turn(jnp.where(off == 3, tts[var], b), 1)
            ys = news
        for var in (0, 1):
            for e in range(SLAB):
                out_west[2 * e + var, rows] = ys[var][e]
                out_own[2 * e + var, rows] = ys[var][SLAB + e]
                out_east[2 * e + var, rows] = ys[var][2 * SLAB + e]
            out_west[2 * SLAB + var, rows] = packs[var]
            out_east[2 * SLAB + var, rows] = packs[var]
            out_pack[var, rows] = packs[var]
        return carry

    lax.fori_loop(0, levels // 8, block, 0)


def forward_sweep(coef, mains, smalls, fields, out_own, levels):
    def block(r, square):
        r8 = pl.multiple_of(r * 8, 8)
        rows = pl.ds(r8, 8)
        lane = lanes()
        group, off = lane // 8, lane % 8
        low, high = lane == 0, lane == BAND - 1
        rim = (lane < 4) | (lane >= BAND - 4)
        xs, packs = [[None] * EXT, [None] * EXT], [None, None]
        for var in (0, 1):
            pieces = [small[var, rows] for small in smalls]
            for e in range(EXT):
                source = (1, 0, 2)[e // SLAB]
                plane = mains[source][2 * (e % SLAB) + var, rows]
                fix = turn(pieces[source], -(8 * (SLAB + e % SLAB) + 4))
                xs[var][e] = plane + jnp.where(rim, fix, 0.0)
            p = jnp.where(group < 4, turn(pieces[1], -64), turn(pieces[0], -32))
            p = jnp.where(group < 8, p, pieces[2])
            packs[var] = jnp.where(group < 12, p, 0.0)
            for e in range(SLAB):
                x = xs[var][SLAB + e]
                out_own[2 * e + var, rows] = x
                square = square + x * x
        for t in range(NT):
            first, last = t + 1, 10 - t
            news = [[None] * EXT, [None] * EXT]
            tts = [jnp.zeros((8, 128), F32)] * 2
            for e in range(first, last + 1):
                c0, up, um, vp, vm = factors(*coefficients(coef, t, e, rows))
                for var in (0, 1):
                    x = xs[var][e]
                    edge = turn(packs[var], -(8 * e + 4))
                    news[var][e] = (
                        c0 * x
                        + up * xs[var][e - 1]
                        + um * xs[var][e + 1]
                        + vp * turn(jnp.where(high, edge, x), 1)
                        + vm * turn(jnp.where(low, edge, x), -1)
                    )
                    if t < NT - 1:
                        tts[var] = jnp.where((lane == 8 * e + 3) | (lane == 8 * e + 4), turn(x, 8 * e + 4), tts[var])
            if t < NT - 1:
                pu, pv = pack_coefficients(coef, t, rows, group)
                c0, up, um, vp, vm = factors(pu, pv)
                for var in (0, 1):
                    p = packs[var]
                    packs[var] = (
                        c0 * p
                        + up * turn(p, 8)
                        + um * turn(p, -8)
                        + vp * turn(jnp.where(off == 3, tts[var], p), 1)
                        + vm * turn(jnp.where(off == 4, tts[var], p), -1)
                    )
            xs = news
            for var in (0, 1):
                for e in range(SLAB, 2 * SLAB):
                    fields[t, pl.ds(pl.multiple_of(var * levels + r8, 8), 8), pl.ds((e - SLAB) * BAND, BAND)] = xs[var][e]
        return square

    return lax.fori_loop(0, levels // 8, block, jnp.zeros((8, 128), F32))


def halves(x):
    big = x.astype(BF16)
    return big, (x - big.astype(F32)).astype(BF16)


def dot(a, b):
    return jnp.dot(a, b, preferred_element_type=F32)


def split_dot(a_big, a_small, b):
    b_big, b_small = halves(b)
    return dot(a_big, b_big) + (dot(a_small, b_big) + dot(a_big, b_small))


def courant_kernel(levels, courant, own, to_west, to_east, edges):
    depth = courant.shape[0] // (2 * NT * SLAB)
    lane = lanes((levels, 128))
    for k in (0, 1):
        edge = jnp.zeros((levels, 128), F32)
        for t in range(NT):
            for l in range(SLAB):
                plane = 8 * t + 4 * k + l
                own[plane, pl.ds(levels - 8, 8)] = jnp.zeros((8, 128), F32)
                own[plane, pl.ds(0, depth)] = courant[pl.ds((2 * t + k) * depth * SLAB + l, depth, stride=SLAB)]
                x = own[plane]
                if t < NT - 1:
                    g = 4 * t + l
                    edge = jnp.where(lane // 8 == g, turn(x, 8 * g + 4), edge)
                    if l < NT - 1 - t:
                        to_west[2 * PLANES[t, l + 1] + k] = x
                    if l > t:
                        to_east[2 * PLANES[t, SLAB - l] + k] = x
        edges[k] = edge


def right_side_kernel(levels, cells, sent, index, weighting, *rest):
    coef, rest = rest[:6], rest[6:]
    out_own, out_west, out_east, out_pack, weights, grads = rest
    w_big, w_small = halves(weighting[...])
    count = index.shape[1]
    place = lax.broadcasted_iota(jnp.int32, (cells, count), 0)
    for t in range(NT):
        hit = jnp.where(place == index[pl.ds(t, 1), :], 1.0, 0.0).astype(BF16)
        a_big, a_small = halves(sent[t])
        b_big, b_small = halves(sent[NT + t])
        total = dot(hit, jnp.concatenate([a_big, b_big], 1)) + dot(hit, jnp.concatenate([a_small, b_small], 1))
        weights[t] = total[:, 128:].T
        grads[t] = split_dot(w_big, w_small, total[:, :128].T)
    adjoint_sweep(coef, grads, out_own, out_west, out_east, out_pack, levels)


def hessian_kernel(levels, mains, smalls, weights, weighting, columns, moments, *rest):
    coef, rest = rest[:6], rest[6:]
    out_own, out_west, out_east, out_pack, out_field, out_moments, fields = rest
    square = forward_sweep(coef, mains, smalls, fields, out_field, levels)
    w_big, w_small = halves(weighting[...])
    t_big, t_small = halves(columns[...])
    product = jnp.zeros((8, 128), F32)
    for t in range(NT):
        seen = split_dot(t_big, t_small, fields[t])
        weighed = weights[t] * seen
        product = product + jnp.sum((weighed * seen).reshape(-1, 8, SLAB, 128), axis=(0, 2))
        fields[t] = split_dot(w_big, w_small, weighed)
    lane = lanes(out_moments.shape)
    before = moments[pl.ds(0, 1), :]
    found = jnp.where(lane == 2, jnp.sum(square), jnp.where(lane == 3, jnp.sum(product), 0.0))
    out_moments[...] = jnp.where(lane < 2, turn(jnp.broadcast_to(before, lane.shape), -2), found)
    adjoint_sweep(coef, fields, out_own, out_west, out_east, out_pack, levels)


def hessian_entry(levels, own, west, east, s_own, s_west, s_east, *rest):
    hessian_kernel(levels, (own, west, east), (s_own, s_west, s_east), *rest)


def gather_kernel(own, pack, from_west, from_east, main, message, aligned):
    lane = lanes(pack.shape[1:])
    group = lane // 8
    for var in (0, 1):
        p = pack[var] + turn(from_east[2 * SLAB + var], 32) + turn(from_west[2 * SLAB + var], -32)
        out = jnp.where((group >= 4) & (group < 8), p, 0.0)
        for l in range(SLAB):
            k = 2 * l + var
            x = own[k] + from_west[k] + from_east[k]
            main[k] = x
            out = jnp.where(group == 8 + l, turn(x, 8 * (8 + l) + 4), out)
        message[var] = out
        aligned[var] = turn(p, 32)


def final_kernel(band, v0, v1, main, south, north, sums, solution, residual):
    total = jnp.sum(sums[...], axis=0, keepdims=True)
    lane = lanes(total.shape)
    m = [jnp.sum(jnp.where(lane == k, total, 0.0), axis=1, keepdims=True) for k in range(4)]
    a, c, d = m[1] / m[0], m[2] / m[0], m[3] / m[0]
    step0 = 1.0 / (1.0 + a)
    keep = a * step0
    ratio = (c - a * a) * step0 * step0
    p, s = keep + ratio, -step0
    curvature = p * p + 2.0 * p * s * a + s * s * c + (p * p * a + 2.0 * p * s * c + s * s * d)
    step1 = ratio / curvature
    depth = solution.shape[0] // (2 * SLAB)
    levels = main.shape[1]
    lane = lanes((levels, 128))
    rim, off = (lane < 4) | (lane >= BAND - 4), lane % 8
    where, bands = band[0], band[1]
    for var in (0, 1):
        fix = jnp.where(
            off < 4,
            jnp.where(where < bands - 1, north[var], 0.0),
            jnp.where(where > 0, south[var], 0.0),
        )
        for l in range(SLAB):
            k = 2 * l + var
            x0, x1 = v0[k], v1[k]
            x2 = main[k] + jnp.where(rim, turn(fix, -(8 * (SLAB + l) + 4)), 0.0)
            rows = pl.ds(var * depth * SLAB + l, depth, stride=SLAB)
            out = (step0 + step1 * p) * x0 + (step1 * s) * x1
            left = (keep - step1 * p) * x0 + (s - step1 * (p + s)) * x1 - (step1 * s) * x2
            solution[rows] = out[:depth]
            residual[rows] = left[:depth]


def shift(x, axis, by):
    n = lax.axis_size(axis)
    return lax.ppermute(x, axis, [(i, (i + by) % n) for i in range(n)])


def body(courant, slot_column_cells, column_counts, innovations, error_weight, weighting):
    depth = courant.shape[2]
    levels = -(-depth // 16) * 16
    owners = slot_column_cells.shape[2]
    capacity = slot_column_cells.shape[3]
    cells = SLAB * BAND
    channels = weighting.shape[1]
    bands = lax.axis_size("lat")
    band = lax.axis_index("lat")

    own, to_west, to_east, edges = call(
        functools.partial(courant_kernel, levels),
        [(2 * NT * SLAB, levels, 128), (12, levels, 128), (12, levels, 128), (2, levels, 128)],
        [courant.reshape(2 * NT * depth * SLAB, BAND)],
    )
    from_east, from_west = shift(to_west, "lon", -1), shift(to_east, "lon", 1)
    from_south, from_north = shift(edges, "lat", 1), shift(edges, "lat", -1)

    weights_here = error_weight[:, 0]
    sent = lax.all_to_all(
        jnp.concatenate([weights_here * innovations[:, 0], weights_here], 0),
        ("lon", "lat"),
        split_axis=1,
        concat_axis=1,
        tiled=True,
    ).reshape(2 * NT, owners * capacity, channels)
    slot = lax.broadcasted_iota(jnp.int32, (NT, owners, capacity), 2)
    index = jnp.where(slot < column_counts[:, 0, :, None], slot_column_cells[:, 0], -1).reshape(NT, owners * capacity)
    weighting_rows = jnp.pad(weighting.reshape(2, depth, channels), ((0, 0), (0, levels - depth), (0, 0))).reshape(
        2 * levels, channels
    )
    weighting_columns = weighting_rows.T

    lane = lanes((1, 1, 128))
    group, lower = lane // 8, lane % 8 < 4
    not_first, not_last = band > 0, band < bands - 1
    pack = jnp.where(
        lower,
        jnp.where(not_first, from_south, 0.0),
        jnp.where(not_last, from_north, 0.0),
    )
    coef = [own, from_west, from_east, pack, shift(pack, "lon", 1), shift(pack, "lon", -1)]

    planes, message = (2 * SLAB, levels, 128), (2 * SLAB + 2, levels, 128)
    small = (2, levels, 128)
    grads = pltpu.VMEM((NT, 2 * levels, cells), F32)

    def gathered(parts):
        mine, to_west, to_east, pack = parts
        return call(
            gather_kernel,
            [planes, small, small],
            [mine, pack, shift(to_east, "lon", 1), shift(to_west, "lon", -1)],
        )

    def hessian(state, weights, moments, rows):
        main, message_lat, aligned = state
        main_west, main_east = shift(main, "lon", 1), shift(main, "lon", -1)
        south, north = shift(message_lat, "lat", 1), shift(message_lat, "lat", -1)
        outer = aligned + jnp.where(lower, south, north)
        inner = jnp.where(lower, north, south)
        edge = jnp.where(
            (group >= 8) & (group < 12),
            jnp.where(jnp.where(lower, not_first, not_last), outer, 0.0),
            jnp.where(jnp.where(lower, not_last, not_first) & (group >= 4) & (group < 8), inner, 0.0),
        )
        return call(
            functools.partial(hessian_entry, levels),
            [planes, message, message, small, planes, (rows, 128)],
            [
                main, main_west, main_east, edge, shift(edge, "lon", 1), shift(edge, "lon", -1),
                weights, weighting_rows, weighting_columns, moments, *coef,
            ],
            [grads],
        )

    *parts, weights = call(
        functools.partial(right_side_kernel, levels, cells),
        [planes, message, message, small, (NT, channels, cells)],
        [sent, index, weighting_rows, *coef],
        [grads],
    )
    *parts, v0, moments = hessian(gathered(parts), weights, jnp.zeros((8, 128), F32), 8)
    *parts, v1, moments = hessian(gathered(parts), weights, moments, owners)
    sums = lax.all_to_all(moments, ("lon", "lat"), split_axis=0, concat_axis=0, tiled=True)
    main, message_lat, _ = gathered(parts)
    solution, residual = call(
        final_kernel,
        [(2 * depth * SLAB, BAND)] * 2,
        [
            jnp.stack([band, jnp.int32(bands)]).astype(jnp.int32),
            v0, v1, main, shift(message_lat, "lat", 1), shift(message_lat, "lat", -1), sums,
        ],
        specs=[SMEM] + [VMEM] * 6,
    )
    shape = (2, depth, SLAB, BAND)
    return solution.reshape(shape), residual.reshape(shape)


def solution(mesh):
    in_specs = (
        P(None, None, None, "lon", "lat"),
        P(None, ("lon", "lat"), None, None),
        P(None, ("lon", "lat"), None),
        P(None, ("lon", "lat"), None, None, None),
        P(None, ("lon", "lat"), None, None, None),
        P(),
    )
    out_specs = (P(None, None, "lon", "lat"), P(None, None, "lon", "lat"))
    return jax.shard_map(body, mesh=mesh, in_specs=in_specs, out_specs=out_specs, check_vma=False)
```

time: 1240 us -> 251 us (0.20)
  local copies, waits for them, and re-layouts: 331 us -> 18.2 us
  starting transfers between devices: 364 us -> 94.5 us
  other arithmetic: 211 us -> 4.67 us
  blocking collectives: 204 us -> 0 us
  Pallas kernels: 0 us -> 81.8 us
  matrix products: 31.1 us -> 0 us
  waiting for transfers between devices: 79.2 us -> 50.5 us
    psum x3 -> x0, blocking collectives: 204 us -> none  [the longest x2 133 us: squared_norm(): return lax.psum(jnp.sum(residual * residual), ('lon', 'lat'))]
    all_to_all x20 -> x2, starting transfers between devices: 173 us -> 29.1 us  [the longest x1 17.1 us: body(): lax.all_to_all(moments, ('lon', 'lat'), split_axis=0, concat_axis=0, tile...]
    ppermute x84 -> x26, starting transfers between devices: 190 us -> 65.4 us  [shift(): return lax.ppermute(x, axis, [(i, (i + by) % n) for i in range(n)])]
    slice x89 -> x0, local copies, waits for them, and re-layouts: 105 us -> none  [the longest x45 54.9 us: padded(): head = lax.slice_in_dim(cells, 0, width, axis=dim)]
    pallas_call x0 -> x8, Pallas kernels: none -> 81.8 us  [call(): pl.pallas_call(kernel, out_shape=[jax.ShapeDtypeStruct(s, F32) for s in s...]
    reshape x49 -> x2, local copies, waits for them, and re-layouts: 72.3 us -> 2.39 us  [the longest x1 1.58 us: body(): weighting.reshape(2, depth, channels)]
    ppermute x42 -> x0, local copies, waits for them, and re-layouts: 64.9 us -> none  [the longest x21 32.8 us: padded(): lax.ppermute(head, axis, [((i + 1) % count, i) for i in range(ends)])]
    all_to_all x20 -> x2, waiting for transfers between devices: 73.9 us -> 9.49 us  [the longest x1 9.49 us: body(): lax.all_to_all(moments, ('lon', 'lat'), split_axis=0, concat_axis=0, tile...]
  transfers between devices with their start and end apart: 104 -> 28, of which waited for: 12 -> 17; matrix products, arithmetic and copies ran while one was open for 38% -> 5% of each run, Pallas kernels for 0% -> 1%
where the time goes in v1:
time: 251 us
  starting transfers between devices  94.5 us (38%)
  Pallas kernels  81.8 us (33%)
  waiting for transfers between devices  50.5 us (20%)
  local copies, waits for them, and re-layouts  18.2 us (7%)
  other arithmetic  4.67 us (2%)
    pallas_call x8, Pallas kernels, call(): pl.pallas_call(kernel, out_shape=[jax.ShapeDtypeStruct(s, F32) for s in s...  81.8 us
    ppermute x26, starting transfers between devices, shift(): return lax.ppermute(x, axis, [(i, (i + by) % n) for i in range(n)])  65.4 us
    ppermute x26, waiting for transfers between devices, shift(): return lax.ppermute(x, axis, [(i, (i + by) % n) for i in range(n)])  41 us
    all_to_all x1, starting transfers between devices, body(): lax.all_to_all(moments, ('lon', 'lat'), split_axis=0, concat_axis=0, tile...  17.1 us
    all_to_all x1, starting transfers between devices, body(): lax.all_to_all(jnp.concatenate([weights_here * innovations[:, 0], weights...  12 us
    all_to_all x1, waiting for transfers between devices, body(): lax.all_to_all(moments, ('lon', 'lat'), split_axis=0, concat_axis=0, tile...  9.49 us
    unnamed x32, local copies, waits for them, and re-layouts  8.54 us
  transfers between devices with their start and end apart: 28, of which 17 were waited for; matrix products, arithmetic and copies ran while one was open for 5% of the time, Pallas kernels for 1%

profile of v1, /device:TPU:1, one launch (start us, length us, event | category | flops | bytes accessed | tf_op | source)
XLA Modules:
  0.0 250.5 jit_solution(3718313725243449302)
XLA Ops:
  0.6 1.6 copy.25
  2.8 1.9 pad_maximum_fusion
  4.7 12.0 %all-to-all-start = ((f32[8,128,4,128]{3,2,0,1:T(4,128)}), f32[8,128,4,128]{3,2,0,1:T(4,128)}, u32[]{:S(2)}, u32[]{:S(2)}) async-start(f32[8,128,4,128]{3,2,0,1:T(4,128)} %pad_maximum_fusion), calls=%async_computation | async-start | bytes 4194304 | tf_op jit(solution)/shard_map/all_to_all | solution.py:348
  16.7 1.6 copy-done.2
  18.3 1.8 shard_map.77
  20.1 1.6 collective-permute-start
  21.8 2.5 collective-permute-start.3
  24.9 1.6 reshape.104
  27.4 1.1 squeeze.11
  29.3 1.7 lt.82
  32.0 11.4 %collective-permute-done.3 = f32[2,144,128]{2,1,0:T(8,128)} collective-permute-done((f32[2,144,128]{2,1,0:T(8,128)S(1)}, f32[2,144,128]{2,1,0:T(8,128)}, u32[]{:S(2)}, u32[]{:S(2)}) %collective-permute-start.3) | collective-permute-done | bytes 147488 | tf_op jit(solution)/shard_map/ppermute | solution.py:326
  43.4 1.3 collective-permute-done.2
  46.6 1.2 collective-permute-start.4
  48.5 2.0 copy.17
  50.4 1.3 collective-permute-done.5.rest_5_.rest_9_
  51.7 1.0 collective-permute-done.4.rest_4_.rest_8_
  52.7 17.2 %shard_map.78 = (f32[8,144,128]{2,1,0:T(8,128)S(1)}, f32[10,144,128]{2,1,0:T(8,128)S(1)}, f32[10,144,128]{2,1,0:T(8,128)S(1)}, f32[2,144,128]{2,1,0:T(8,128)S(1)}, f32[4,128,512]{2,1,0:T(8,128)S(1)}) custom-call(f32[8,512,128]{2,1,0:T(8,128)S(1)} %bitcast.23, s32[4,512]{1,0:T(4,128)S(1)} %compare_select_fusion.index, f32[288,128]{1,0:T(8,128)S(1)} %bitcast.24, ...), custom_call_target="tpu_custom_call" | custom-call | bytes 6823936 | tf_op jit(solution)/shard_map/pallas_call | solution.py:23
  69.9 1.0 copy-done
  70.9 7.0 %collective-permute-start.7 = (f32[10,144,128]{2,1,0:T(8,128)S(1)}, f32[10,144,128]{2,1,0:T(8,128)S(1)}, u32[]{:S(2)}, u32[]{:S(2)}) collective-permute-start(f32[10,144,128]{2,1,0:T(8,128)S(1)} %get-tuple-element.40), channel_id=1, source_target_pairs={{0,124},{4,0},{8,4},{12,8},{16,12},{20,16},{24,20},{28,24},{32,28}... | collective-permute-start | bytes 2211848 | tf_op jit(solution)/shard_map/ppermute | solution.py:326
  77.9 1.7 collective-permute-done.6.from_west
  79.6 2.2 collective-permute-done.7.from_east
  81.8 1.1 shard_map.79
  82.8 2.4 collective-permute-start.11
  85.3 9.9 %collective-permute-start.9 = (f32[8,144,128]{2,1,0:T(8,128)}, f32[8,144,128]{2,1,0:T(8,128)}, u32[]{:S(2)}, u32[]{:S(2)}) collective-permute-start(f32[8,144,128]{2,1,0:T(8,128)} %get-tuple-element.41.own), channel_id=1, source_target_pairs={{0,124},{4,0},{8,4},{12,8},{16,12},{20,16},{24,20},{28,24},{32,28}... | collective-permute-start | bytes 1769480 | tf_op jit(solution)/shard_map/ppermute | solution.py:326
  95.9 4.8 %collective-permute-start.13 = (f32[2,144,128]{2,1,0:T(8,128)}, f32[2,144,128]{2,1,0:T(8,128)}, u32[]{:S(2)}, u32[]{:S(2)}) collective-permute-start(f32[2,144,128]{2,1,0:T(8,128)} %select_select_fusion.1.s_own), channel_id=1, source_target_pairs={{0,124},{4,0},{8,4},{12,8},{16,12},{20,16},{24,20},{28,24},{32,28}... | collective-permute-start | bytes 442376 | tf_op jit(solution)/shard_map/ppermute | solution.py:326
  102.1 4.6 %collective-permute-done.12.s_west = f32[2,144,128]{2,1,0:T(8,128)} collective-permute-done((f32[2,144,128]{2,1,0:T(8,128)}, f32[2,144,128]{2,1,0:T(8,128)}, u32[]{:S(2)}, u32[]{:S(2)}) %collective-permute-start.12) | collective-permute-done | bytes 147488 | tf_op jit(solution)/shard_map/ppermute | solution.py:326
  106.7 1.2 copy-done.1
  108.9 29.2 %shard_map.80 = (f32[8,144,128]{2,1,0:T(8,128)S(1)}, f32[10,144,128]{2,1,0:T(8,128)S(1)}, f32[10,144,128]{2,1,0:T(8,128)S(1)}, f32[2,144,128]{2,1,0:T(8,128)S(1)...) custom-call(f32[8,144,128]{2,1,0:T(8,128)} %get-tuple-element.41.own, f32[8,144,128]{2,1,0:T(8,128)} %collective-permute-done.8.west, ...), custom_call_target="tpu_custom_call" | custom-call | bytes 8130560 | tf_op jit(solution)/shard_map/pallas_call | solution.py:23
  138.2 7.6 %collective-permute-start.15 = (f32[10,144,128]{2,1,0:T(8,128)S(1)}, f32[10,144,128]{2,1,0:T(8,128)S(1)}, u32[]{:S(2)}, u32[]{:S(2)}) collective-permute-start(f32[10,144,128]{2,1,0:T(8,128)S(1)} %get-tuple-element.49), channel_id=1, source_target_pairs={{0,124},{4,0},{8,4},{12,8},{16,12},{20,16},{24,20},{28,24},{32,28}... | collective-permute-start | bytes 2211848 | tf_op jit(solution)/shard_map/ppermute | solution.py:326
  145.8 1.6 collective-permute-done.14.from_west
  147.4 1.8 collective-permute-done.15.from_east
  149.5 10.8 %collective-permute-start.17 = (f32[8,144,128]{2,1,0:T(8,128)S(1)}, f32[8,144,128]{2,1,0:T(8,128)S(1)}, u32[]{:S(2)}, u32[]{:S(2)}) collective-permute-start(f32[8,144,128]{2,1,0:T(8,128)S(1)} %get-tuple-element.50.own), channel_id=1, source_target_pairs={{0,124},{4,0},{8,4},{12,8},{16,12},{20,16},{24,20},{28,24},{32,28}... | collective-permute-start | bytes 1769480 | tf_op jit(solution)/shard_map/ppermute | solution.py:326
  160.3 1.5 collective-permute-start.19
  161.8 2.5 %collective-permute-done.19 = f32[2,144,128]{2,1,0:T(8,128)S(1)} collective-permute-done((f32[2,144,128]{2,1,0:T(8,128)S(1)}, f32[2,144,128]{2,1,0:T(8,128)S(1)}, u32[]{:S(2)}, u32[]{:S(2)}) %collective-permute-start.19) | collective-permute-done | bytes 147488 | tf_op jit(solution)/shard_map/ppermute | solution.py:326
  164.3 2.7 %collective-permute-done.18 = f32[2,144,128]{2,1,0:T(8,128)S(1)} collective-permute-done((f32[2,144,128]{2,1,0:T(8,128)S(1)}, f32[2,144,128]{2,1,0:T(8,128)S(1)}, u32[]{:S(2)}, u32[]{:S(2)}) %collective-permute-start.18) | collective-permute-done | bytes 147488 | tf_op jit(solution)/shard_map/ppermute | solution.py:326
  167.0 6.6 %collective-permute-start.21 = (f32[2,144,128]{2,1,0:T(8,128)S(1)}, f32[2,144,128]{2,1,0:T(8,128)S(1)}, u32[]{:S(2)}, u32[]{:S(2)}) collective-permute-start(f32[2,144,128]{2,1,0:T(8,128)S(1)} %select_select_fusion.s_own), channel_id=1, source_target_pairs={{0,124},{4,0},{8,4},{12,8},{16,12},{20,16},{24,20},{28,24},{32,28}... | collective-permute-start | bytes 442376 | tf_op jit(solution)/shard_map/ppermute | solution.py:326
  173.6 1.0 collective-permute-done.21.s_east
  174.6 3.5 %collective-permute-done.20.s_west = f32[2,144,128]{2,1,0:T(8,128)S(1)} collective-permute-done((f32[2,144,128]{2,1,0:T(8,128)S(1)}, f32[2,144,128]{2,1,0:T(8,128)S(1)}, u32[]{:S(2)}, u32[]{:S(2)}) %collective-permute-start.20) | collective-permute-done | bytes 147488 | tf_op jit(solution)/shard_map/ppermute | solution.py:326
  178.1 29.3 %shard_map.82 = (f32[8,144,128]{2,1,0:T(8,128)S(1)}, f32[10,144,128]{2,1,0:T(8,128)S(1)}, f32[10,144,128]{2,1,0:T(8,128)S(1)}, f32[2,144,128]{2,1,0:T(8,128)S(1)...) custom-call(f32[8,144,128]{2,1,0:T(8,128)S(1)} %get-tuple-element.50.own, ...), custom_call_target="tpu_custom_call" | custom-call | bytes 8130560 | tf_op jit(solution)/shard_map/pallas_call | solution.py:23
  207.5 7.0 %collective-permute-start.23 = (f32[10,144,128]{2,1,0:T(8,128)S(1)}, f32[10,144,128]{2,1,0:T(8,128)S(1)}, u32[]{:S(2)}, u32[]{:S(2)}) collective-permute-start(f32[10,144,128]{2,1,0:T(8,128)S(1)} %get-tuple-element.58), channel_id=1, source_target_pairs={{0,124},{4,0},{8,4},{12,8},{16,12},{20,16},{24,20},{28,24},{32,28}... | collective-permute-start | bytes 2211848 | tf_op jit(solution)/shard_map/ppermute | solution.py:326
  214.5 1.6 collective-permute-done.22.from_west
  216.1 2.2 collective-permute-done.23.from_east
  218.4 1.0 shard_map.83
  219.4 1.5 collective-permute-start.24
  220.9 17.1 %all-to-all-start.1 = ((f32[128,1,128]{2,1,0:T(1,128)}), f32[128,1,128]{2,1,0:T(1,128)S(1)}, u32[]{:S(2)}, u32[]{:S(2)}) async-start(f32[128,1,128]{2,1,0:T(1,128)} %bitcast.9), calls=%async_computation.1 | async-start | bytes 131072 | tf_op jit(solution)/shard_map/all_to_all | solution.py:413
  238.1 9.5 %all-to-all-done.1 = f32[128,1,128]{2,1,0:T(1,128)S(1)} async-done(((f32[128,1,128]{2,1,0:T(1,128)}), f32[128,1,128]{2,1,0:T(1,128)S(1)}, u32[]{:S(2)}, u32[]{:S(2)}) %all-to-all-start.1) | async-done | bytes 65568 | tf_op jit(solution)/shard_map/all_to_all | solution.py:413
  247.6 1.1 copy-done.8
  248.6 1.9 shard_map.84
  (68 shorter events, 10.1 us)
Async XLA Ops:
  0.6 1.6 copy-start.9
  0.6 1.8 copy-start.10
  4.7 43.8 %all-to-all-start = ((f32[8,128,4,128]{3,2,0,1:T(4,128)}), f32[8,128,4,128]{3,2,0,1:T(4,128)}, u32[]{:S(2)}, u32[]{:S(2)}) async-start(f32[8,128,4,128]{3,2,0,1:T(4,128)} %pad_maximum_fusion), calls=%async_computation | async-start | bytes 4194304 | tf_op jit(solution)/shard_map/all_to_all | solution.py:348
  16.7 1.6 copy-start.2
  18.3 8.2 %copy-start.11 = (s32[4,1,128,4]{2,3,1,0:T(4,128)S(1)}, s32[4,1,128,4]{2,3,1,0:T(4,128)}, u32[]{:S(2)}) copy-start(s32[4,1,128,4]{2,3,1,0:T(4,128)} %param.7) | copy-start | bytes 24580
  18.3 10.2 %copy-start.14 = (s32[4,1,128]{2,1,0:T(1,128)S(1)}, s32[4,1,128]{2,1,0:T(1,128)}, u32[]{:S(2)}) copy-start(s32[4,1,128]{2,1,0:T(1,128)} %param.8) | copy-start | bytes 6148
  20.1 32.6 %collective-permute-start = (f32[12,144,128]{2,1,0:T(8,128)}, f32[12,144,128]{2,1,0:T(8,128)S(1)}, u32[]{:S(2)}, u32[]{:S(2)}) collective-permute-start(f32[12,144,128]{2,1,0:T(8,128)} %get-tuple-element.34), channel_id=1, source_target_pairs={{0,4},{4,8},{8,12},{12,16},{16,20},{20,24},{24,28},{28,32},{32,36}... | collective-permute-start | bytes 2654216 | tf_op jit(solution)/shard_map/ppermute | solution.py:326
  21.8 30.9 %collective-permute-start.1 = (f32[12,144,128]{2,1,0:T(8,128)}, f32[12,144,128]{2,1,0:T(8,128)}, u32[]{:S(2)}, u32[]{:S(2)}) collective-permute-start(f32[12,144,128]{2,1,0:T(8,128)} %get-tuple-element.35), channel_id=1, source_target_pairs={{0,124},{4,0},{8,4},{12,8},{16,12},{20,16},{24,20},{28,24},{32,28}... | collective-permute-start | bytes 2654216 | tf_op jit(solution)/shard_map/ppermute | solution.py:326
  21.8 21.7 %collective-permute-start.3 = (f32[2,144,128]{2,1,0:T(8,128)S(1)}, f32[2,144,128]{2,1,0:T(8,128)}, u32[]{:S(2)}, u32[]{:S(2)}) collective-permute-start(f32[2,144,128]{2,1,0:T(8,128)S(1)} %get-tuple-element.36), channel_id=1, source_target_pairs={{0,3},{1,0},{2,1},{3,2},{4,7},{5,4},{6,5},{7,6},{8,11},{9,8},{10,9... | collective-permute-start | bytes 442376 | tf_op jit(solution)/shard_map/ppermute | solution.py:326
  24.2 20.5 %collective-permute-start.2 = (f32[2,144,128]{2,1,0:T(8,128)S(1)}, f32[2,144,128]{2,1,0:T(8,128)}, u32[]{:S(2)}, u32[]{:S(2)}) collective-permute-start(f32[2,144,128]{2,1,0:T(8,128)S(1)} %get-tuple-element.36), channel_id=1, source_target_pairs={{0,1},{1,2},{2,3},{3,0},{4,5},{5,6},{6,7},{7,4},{8,9},{9,10},{10,1... | collective-permute-start | bytes 442376 | tf_op jit(solution)/shard_map/ppermute | solution.py:326
  32.0 14.6 %copy-start.12 = (pred[128]{0:T(512)(128)(4,1)}, pred[128]{0:T(512)(128)(4,1)S(1)}, u32[]{:S(2)}) copy-start(pred[128]{0:T(512)(128)(4,1)S(1)} %fusion) | copy-start | bytes 388
  45.6 6.0 %collective-permute-start.5 = (f32[2,144,128]{2,1,0:T(8,128)S(1)}, f32[2,144,128]{2,1,0:T(8,128)}, u32[]{:S(2)}, u32[]{:S(2)}) collective-permute-start(f32[2,144,128]{2,1,0:T(8,128)S(1)} %select_select_fusion.2.rest_3_.rest_7_), channel_id=1, source_target_pairs={{0,124},{4,0},{8,4},{12,8},{16,12},{20,16},{24,20},{28,24},{32,28}... | collective-permute-start | bytes 442376 | tf_op jit(solution)/shard_map/ppermute | solution.py:326
  46.6 6.1 %collective-permute-start.4 = (f32[2,144,128]{2,1,0:T(8,128)S(1)}, f32[2,144,128]{2,1,0:T(8,128)}, u32[]{:S(2)}, u32[]{:S(2)}) collective-permute-start(f32[2,144,128]{2,1,0:T(8,128)S(1)} %select_select_fusion.2.rest_3_.rest_7_), channel_id=1, source_target_pairs={{0,4},{4,8},{8,12},{12,16},{16,20},{20,24},{24,28},{28,32},{32,36}... | collective-permute-start | bytes 442376 | tf_op jit(solution)/shard_map/ppermute | solution.py:326
  69.9 1.0 copy-start
  70.9 24.4 %copy-start.13 = (pred[128]{0:T(512)(128)(4,1)S(1)}, pred[128]{0:T(512)(128)(4,1)}, u32[]{:S(2)}) copy-start(pred[128]{0:T(512)(128)(4,1)} %copy-done.12) | copy-start | bytes 388
  70.9 8.7 %collective-permute-start.6 = (f32[10,144,128]{2,1,0:T(8,128)S(1)}, f32[10,144,128]{2,1,0:T(8,128)S(1)}, u32[]{:S(2)}, u32[]{:S(2)}) collective-permute-start(f32[10,144,128]{2,1,0:T(8,128)S(1)} %get-tuple-element.39), channel_id=1, source_target_pairs={{0,4},{4,8},{8,12},{12,16},{16,20},{20,24},{24,28},{28,32},{32,36}... | collective-permute-start | bytes 2211848 | tf_op jit(solution)/shard_map/ppermute | solution.py:326
  70.9 10.9 %collective-permute-start.7 = (f32[10,144,128]{2,1,0:T(8,128)S(1)}, f32[10,144,128]{2,1,0:T(8,128)S(1)}, u32[]{:S(2)}, u32[]{:S(2)}) collective-permute-start(f32[10,144,128]{2,1,0:T(8,128)S(1)} %get-tuple-element.40), channel_id=1, source_target_pairs={{0,124},{4,0},{8,4},{12,8},{16,12},{20,16},{24,20},{28,24},{32,28}... | collective-permute-start | bytes 2211848 | tf_op jit(solution)/shard_map/ppermute | solution.py:326
  82.8 12.4 %collective-permute-start.11 = (f32[2,144,128]{2,1,0:T(8,128)S(1)}, f32[2,144,128]{2,1,0:T(8,128)S(1)}, u32[]{:S(2)}, u32[]{:S(2)}) collective-permute-start(f32[2,144,128]{2,1,0:T(8,128)S(1)} %get-tuple-element.43), channel_id=1, source_target_pairs={{0,3},{1,0},{2,1},{3,2},{4,7},{5,4},{6,5},{7,6},{8,11},{9,8},{10,9... | collective-permute-start | bytes 442376 | tf_op jit(solution)/shard_map/ppermute | solution.py:326
  85.3 10.0 %collective-permute-start.10 = (f32[2,144,128]{2,1,0:T(8,128)S(1)}, f32[2,144,128]{2,1,0:T(8,128)S(1)}, u32[]{:S(2)}, u32[]{:S(2)}) collective-permute-start(f32[2,144,128]{2,1,0:T(8,128)S(1)} %get-tuple-element.43), channel_id=1, source_target_pairs={{0,1},{1,2},{2,3},{3,0},{4,5},{5,6},{6,7},{7,4},{8,9},{9,10},{10,1... | collective-permute-start | bytes 442376 | tf_op jit(solution)/shard_map/ppermute | solution.py:326
  85.3 21.5 %collective-permute-start.9 = (f32[8,144,128]{2,1,0:T(8,128)}, f32[8,144,128]{2,1,0:T(8,128)}, u32[]{:S(2)}, u32[]{:S(2)}) collective-permute-start(f32[8,144,128]{2,1,0:T(8,128)} %get-tuple-element.41.own), channel_id=1, source_target_pairs={{0,124},{4,0},{8,4},{12,8},{16,12},{20,16},{24,20},{28,24},{32,28}... | collective-permute-start | bytes 1769480 | tf_op jit(solution)/shard_map/ppermute | solution.py:326
  95.2 11.5 %collective-permute-start.8 = (f32[8,144,128]{2,1,0:T(8,128)}, f32[8,144,128]{2,1,0:T(8,128)}, u32[]{:S(2)}, u32[]{:S(2)}) collective-permute-start(f32[8,144,128]{2,1,0:T(8,128)} %get-tuple-element.41.own), channel_id=1, source_target_pairs={{0,4},{4,8},{8,12},{12,16},{16,20},{20,24},{24,28},{28,32},{32,36}... | collective-permute-start | bytes 1769480 | tf_op jit(solution)/shard_map/ppermute | solution.py:326
  95.9 6.2 %collective-permute-start.13 = (f32[2,144,128]{2,1,0:T(8,128)}, f32[2,144,128]{2,1,0:T(8,128)}, u32[]{:S(2)}, u32[]{:S(2)}) collective-permute-start(f32[2,144,128]{2,1,0:T(8,128)} %select_select_fusion.1.s_own), channel_id=1, source_target_pairs={{0,124},{4,0},{8,4},{12,8},{16,12},{20,16},{24,20},{28,24},{32,28}... | collective-permute-start | bytes 442376 | tf_op jit(solution)/shard_map/ppermute | solution.py:326
  100.8 5.9 %collective-permute-start.12 = (f32[2,144,128]{2,1,0:T(8,128)}, f32[2,144,128]{2,1,0:T(8,128)}, u32[]{:S(2)}, u32[]{:S(2)}) collective-permute-start(f32[2,144,128]{2,1,0:T(8,128)} %select_select_fusion.1.s_own), channel_id=1, source_target_pairs={{0,4},{4,8},{8,12},{12,16},{16,20},{20,24},{24,28},{28,32},{32,36}... | collective-permute-start | bytes 442376 | tf_op jit(solution)/shard_map/ppermute | solution.py:326
  106.7 1.2 copy-start.1
  108.0 0.9 copy-start.3
  138.1 40.0 %copy-start.5 = (f32[8,144,128]{2,1,0:T(8,128)}, f32[8,144,128]{2,1,0:T(8,128)S(1)}, u32[]{:S(2)}) copy-start(f32[8,144,128]{2,1,0:T(8,128)S(1)} %get-tuple-element.45.v0) | copy-start | bytes 1769476
  138.1 40.0 %copy-start.4 = (f32[288,128]{0,1:T(8,128)S(1)}, f32[288,128]{0,1:T(8,128)}, u32[]{:S(2)}) copy-start(f32[288,128]{0,1:T(8,128)} %copy.19) | copy-start | bytes 442372
  138.1 9.3 %collective-permute-start.14 = (f32[10,144,128]{2,1,0:T(8,128)S(1)}, f32[10,144,128]{2,1,0:T(8,128)S(1)}, u32[]{:S(2)}, u32[]{:S(2)}) collective-permute-start(f32[10,144,128]{2,1,0:T(8,128)S(1)} %get-tuple-element.48), channel_id=1, source_target_pairs={{0,4},{4,8},{8,12},{12,16},{16,20},{20,24},{24,28},{28,32},{32,36}... | collective-permute-start | bytes 2211848 | tf_op jit(solution)/shard_map/ppermute | solution.py:326
  138.2 11.0 %collective-permute-start.15 = (f32[10,144,128]{2,1,0:T(8,128)S(1)}, f32[10,144,128]{2,1,0:T(8,128)S(1)}, u32[]{:S(2)}, u32[]{:S(2)}) collective-permute-start(f32[10,144,128]{2,1,0:T(8,128)S(1)} %get-tuple-element.49), channel_id=1, source_target_pairs={{0,124},{4,0},{8,4},{12,8},{16,12},{20,16},{24,20},{28,24},{32,28}... | collective-permute-start | bytes 2211848 | tf_op jit(solution)/shard_map/ppermute | solution.py:326
  149.5 28.6 %collective-permute-start.17 = (f32[8,144,128]{2,1,0:T(8,128)S(1)}, f32[8,144,128]{2,1,0:T(8,128)S(1)}, u32[]{:S(2)}, u32[]{:S(2)}) collective-permute-start(f32[8,144,128]{2,1,0:T(8,128)S(1)} %get-tuple-element.50.own), channel_id=1, source_target_pairs={{0,124},{4,0},{8,4},{12,8},{16,12},{20,16},{24,20},{28,24},{32,28}... | collective-permute-start | bytes 1769480 | tf_op jit(solution)/shard_map/ppermute | solution.py:326
  160.3 17.8 %collective-permute-start.16 = (f32[8,144,128]{2,1,0:T(8,128)S(1)}, f32[8,144,128]{2,1,0:T(8,128)S(1)}, u32[]{:S(2)}, u32[]{:S(2)}) collective-permute-start(f32[8,144,128]{2,1,0:T(8,128)S(1)} %get-tuple-element.50.own), channel_id=1, source_target_pairs={{0,4},{4,8},{8,12},{12,16},{16,20},{20,24},{24,28},{28,32},{32,36}... | collective-permute-start | bytes 1769480 | tf_op jit(solution)/shard_map/ppermute | solution.py:326
  160.3 4.0 %collective-permute-start.19 = (f32[2,144,128]{2,1,0:T(8,128)S(1)}, f32[2,144,128]{2,1,0:T(8,128)S(1)}, u32[]{:S(2)}, u32[]{:S(2)}) collective-permute-start(f32[2,144,128]{2,1,0:T(8,128)S(1)} %get-tuple-element.52), channel_id=1, source_target_pairs={{0,3},{1,0},{2,1},{3,2},{4,7},{5,4},{6,5},{7,6},{8,11},{9,8},{10,9... | collective-permute-start | bytes 442376 | tf_op jit(solution)/shard_map/ppermute | solution.py:326
  161.8 5.2 %collective-permute-start.18 = (f32[2,144,128]{2,1,0:T(8,128)S(1)}, f32[2,144,128]{2,1,0:T(8,128)S(1)}, u32[]{:S(2)}, u32[]{:S(2)}) collective-permute-start(f32[2,144,128]{2,1,0:T(8,128)S(1)} %get-tuple-element.52), channel_id=1, source_target_pairs={{0,1},{1,2},{2,3},{3,0},{4,5},{5,6},{6,7},{7,4},{8,9},{9,10},{10,1... | collective-permute-start | bytes 442376 | tf_op jit(solution)/shard_map/ppermute | solution.py:326
  167.0 7.6 %collective-permute-start.21 = (f32[2,144,128]{2,1,0:T(8,128)S(1)}, f32[2,144,128]{2,1,0:T(8,128)S(1)}, u32[]{:S(2)}, u32[]{:S(2)}) collective-permute-start(f32[2,144,128]{2,1,0:T(8,128)S(1)} %select_select_fusion.s_own), channel_id=1, source_target_pairs={{0,124},{4,0},{8,4},{12,8},{16,12},{20,16},{24,20},{28,24},{32,28}... | collective-permute-start | bytes 442376 | tf_op jit(solution)/shard_map/ppermute | solution.py:326
  173.6 4.5 %collective-permute-start.20 = (f32[2,144,128]{2,1,0:T(8,128)S(1)}, f32[2,144,128]{2,1,0:T(8,128)S(1)}, u32[]{:S(2)}, u32[]{:S(2)}) collective-permute-start(f32[2,144,128]{2,1,0:T(8,128)S(1)} %select_select_fusion.s_own), channel_id=1, source_target_pairs={{0,4},{4,8},{8,12},{12,16},{16,20},{20,24},{24,28},{28,32},{32,36}... | collective-permute-start | bytes 442376 | tf_op jit(solution)/shard_map/ppermute | solution.py:326
  207.4 12.0 %copy-start.7 = (f32[8,144,128]{2,1,0:T(8,128)}, f32[8,144,128]{2,1,0:T(8,128)S(1)}, u32[]{:S(2)}) copy-start(f32[8,144,128]{2,1,0:T(8,128)S(1)} %get-tuple-element.54.v1) | copy-start | bytes 1769476
  207.4 40.2 %copy-start.6 = (f32[8,144,128]{2,1,0:T(8,128)S(1)}, f32[8,144,128]{2,1,0:T(8,128)}, u32[]{:S(2)}) copy-start(f32[8,144,128]{2,1,0:T(8,128)} %copy-done.5) | copy-start | bytes 1769476
  207.4 8.7 %collective-permute-start.22 = (f32[10,144,128]{2,1,0:T(8,128)S(1)}, f32[10,144,128]{2,1,0:T(8,128)S(1)}, u32[]{:S(2)}, u32[]{:S(2)}) collective-permute-start(f32[10,144,128]{2,1,0:T(8,128)S(1)} %get-tuple-element.57), channel_id=1, source_target_pairs={{0,4},{4,8},{8,12},{12,16},{16,20},{20,24},{24,28},{28,32},{32,36}... | collective-permute-start | bytes 2211848 | tf_op jit(solution)/shard_map/ppermute | solution.py:326
  207.5 10.9 %collective-permute-start.23 = (f32[10,144,128]{2,1,0:T(8,128)S(1)}, f32[10,144,128]{2,1,0:T(8,128)S(1)}, u32[]{:S(2)}, u32[]{:S(2)}) collective-permute-start(f32[10,144,128]{2,1,0:T(8,128)S(1)} %get-tuple-element.58), channel_id=1, source_target_pairs={{0,124},{4,0},{8,4},{12,8},{16,12},{20,16},{24,20},{28,24},{32,28}... | collective-permute-start | bytes 2211848 | tf_op jit(solution)/shard_map/ppermute | solution.py:326
  219.4 28.2 %collective-permute-start.25 = (f32[2,144,128]{2,1,0:T(8,128)S(1)}, f32[2,144,128]{2,1,0:T(8,128)S(1)}, u32[]{:S(2)}, u32[]{:S(2)}) collective-permute-start(f32[2,144,128]{2,1,0:T(8,128)S(1)} %get-tuple-element.60), channel_id=1, source_target_pairs={{0,3},{1,0},{2,1},{3,2},{4,7},{5,4},{6,5},{7,6},{8,11},{9,8},{10,9... | collective-permute-start | bytes 442376 | tf_op jit(solution)/shard_map/ppermute | solution.py:326
  219.4 28.2 %collective-permute-start.24 = (f32[2,144,128]{2,1,0:T(8,128)S(1)}, f32[2,144,128]{2,1,0:T(8,128)S(1)}, u32[]{:S(2)}, u32[]{:S(2)}) collective-permute-start(f32[2,144,128]{2,1,0:T(8,128)S(1)} %get-tuple-element.60), channel_id=1, source_target_pairs={{0,1},{1,2},{2,3},{3,0},{4,5},{5,6},{6,7},{7,4},{8,9},{9,10},{10,1... | collective-permute-start | bytes 442376 | tf_op jit(solution)/shard_map/ppermute | solution.py:326
  220.9 26.7 %all-to-all-start.1 = ((f32[128,1,128]{2,1,0:T(1,128)}), f32[128,1,128]{2,1,0:T(1,128)S(1)}, u32[]{:S(2)}, u32[]{:S(2)}) async-start(f32[128,1,128]{2,1,0:T(1,128)} %bitcast.9), calls=%async_computation.1 | async-start | bytes 131072 | tf_op jit(solution)/shard_map/all_to_all | solution.py:413
  247.6 1.1 copy-start.8

commit v2 on v1

v2 whole, which is shorter than its diff:
```python
import functools

import jax
import jax.numpy as jnp
from jax import lax
from jax.experimental import pallas as pl
from jax.experimental.pallas import tpu as pltpu
from jax.sharding import PartitionSpec as P

F32 = jnp.float32
BF16 = jnp.bfloat16
NT = 4
SLAB = 4
BAND = 128
EXT = 3 * SLAB
SLOTS = 4
PLANES = {(0, 1): 0, (0, 2): 1, (0, 3): 2, (1, 1): 3, (1, 2): 4, (2, 1): 5}
VMEM = pl.BlockSpec(memory_space=pltpu.VMEM)
HBM = pl.BlockSpec(memory_space=pltpu.HBM)
SMEM = pl.BlockSpec(memory_space=pltpu.SMEM)


def call(kernel, shapes, inputs, scratch=(), flops=0, hbm_in=(), hbm_out=()):
    nbytes = sum(x.size * x.dtype.itemsize for x in inputs)
    return pl.pallas_call(
        kernel,
        out_shape=[jax.ShapeDtypeStruct(s, F32) for s in shapes],
        in_specs=[SMEM] + [HBM if i in hbm_in else VMEM for i in range(1, len(inputs))],
        out_specs=[HBM if i in hbm_out else VMEM for i in range(len(shapes))],
        scratch_shapes=list(scratch),
        compiler_params=pltpu.CompilerParams(vmem_limit_bytes=28 << 20),
        cost_estimate=pl.CostEstimate(flops=flops, bytes_accessed=nbytes, transcendentals=0),
    )(*inputs)


def turn(x, shift):
    shift %= 128
    return pltpu.roll(x, shift, x.ndim - 1) if shift else x


def lanes(shape=(8, 128)):
    return lax.broadcasted_iota(jnp.int32, shape, len(shape) - 1)


def flip(x, group):
    lane = lanes(x.shape)
    return jnp.take_along_axis(x, (8 * group + 3 - lane) & 127, axis=1, mode="promise_in_bounds")


def sides(odd, near, far):
    return jnp.where(odd, near, far), jnp.where(odd, far, near)


def parts(u):
    plus = jnp.maximum(u, 0.0)
    return plus, plus - u


def factors(u, v):
    up, um = parts(u)
    vp, vm = parts(v)
    return 1.0 - (up + um) - (vp + vm), up, um, vp, vm


def coefficients(odd, refs, t, e, rows):
    own, near, far = refs[:3]
    if SLAB <= e < 2 * SLAB:
        k = 8 * t + e - SLAB
        return own[k, rows], own[k + SLAB, rows]
    k = 2 * PLANES[t, SLAB - e if e < SLAB else e - 2 * SLAB + 1]
    side = 0 if e < SLAB else 1
    return tuple(sides(odd, near[k + i, rows], far[k + i, rows])[side] for i in (0, 1))


def pack_coefficients(odd, refs, t, rows, group):
    own, near, far = refs[3:]
    out = []
    for k in (0, 1):
        west, east = sides(odd, near[k, rows], far[k, rows])
        p = jnp.where(group < 4, turn(west, -32 * t), turn(own[k, rows], 32 - 32 * t))
        p = jnp.where(group < 8, p, turn(east, 64 - 32 * t))
        out.append(jnp.where(group < 12, p, 0.0))
    return out


def adjoint_sweep(odd, coef, grads, out_own, out_near, out_far, out_pack, levels):
    def block(r, carry):
        r8 = pl.multiple_of(r * 8, 8)
        rows = pl.ds(r8, 8)
        lane = lanes()
        group, off = lane // 8, lane % 8
        low, high = lane == 0, lane == BAND - 1
        ys = [[None] * EXT, [None] * EXT]
        packs = [None, None]
        for t in reversed(range(NT)):
            first, last = t + 1, 10 - t
            for var in (0, 1):
                for e in range(SLAB, 2 * SLAB):
                    g = grads[t, pl.ds(pl.multiple_of(var * levels + r8, 8), 8), pl.ds((e - SLAB) * BAND, BAND)]
                    ys[var][e] = g if ys[var][e] is None else ys[var][e] + g
            news = [[None] * EXT, [None] * EXT]
            tts = [jnp.zeros((8, 128), F32)] * 2
            mixes, pouts = [None, None], [None, None]
            if t < NT - 1:
                pu, pv = pack_coefficients(odd, coef, t, rows, group)
                c0, up, um, vp, vm = factors(pu, pv)
                for var in (0, 1):
                    p = packs[var]
                    a, b = vp * p, vm * p
                    mixes[var] = jnp.where(off == 3, a, b)
                    pouts[var] = (c0 * p + turn(up * p, -8) + turn(um * p, 8), turn(a, 1), turn(b, -1))

            def put(var, e, x):
                news[var][e] = x if news[var][e] is None else news[var][e] + x

            for e in range(first, last + 1):
                c0, up, um, vp, vm = factors(*coefficients(odd, coef, t, e, rows))
                for var in (0, 1):
                    y = ys[var][e]
                    a, b = vp * y, vm * y
                    edge = 0.0 if mixes[var] is None else turn(mixes[var], -(8 * e + 4))
                    put(var, e, c0 * y + jnp.where(high, edge, turn(a, -1)) + jnp.where(low, edge, turn(b, 1)))
                    put(var, e - 1, up * y)
                    put(var, e + 1, um * y)
                    mixed = turn(jnp.where(low, a, b), 8 * e + 4)
                    tts[var] = jnp.where((lane == 8 * e + 3) | (lane == 8 * e + 4), mixed, tts[var])
            for var in (0, 1):
                rest, a, b = (0.0, 0.0, 0.0) if pouts[var] is None else pouts[var]
                packs[var] = rest + (jnp.where(off == 4, tts[var], a) + jnp.where(off == 3, tts[var], b))
            ys = news
        for var in (0, 1):
            for e in range(SLAB):
                k = 2 * e + var
                west, east = ys[var][e], ys[var][2 * SLAB + e]
                out_own[k, rows] = ys[var][SLAB + e]
                out_near[k, rows] = jnp.where(odd, west, east)
                out_far[k, rows] = jnp.where(odd, east, west)
            out_pack[var, rows] = packs[var]
        both = jnp.where((group & 4) == 0, packs[0], turn(packs[1], 32))
        out_near[2 * SLAB, rows] = both
        out_far[2 * SLAB, rows] = both
        return carry

    lax.fori_loop(0, levels // 8, block, 0, unroll=2)


def forward_sweep(odd, coef, mains, smalls, fields, out_own, levels):
    def block(r, square):
        r8 = pl.multiple_of(r * 8, 8)
        rows = pl.ds(r8, 8)
        lane = lanes()
        group, off = lane // 8, lane % 8
        low, high = lane == 0, lane == BAND - 1
        rim = (lane < 4) | (lane >= BAND - 4)
        xs, packs = [[None] * EXT, [None] * EXT], [None, None]
        pieces = (smalls[0][rows], *sides(odd, smalls[1][rows], smalls[2][rows]))
        for var in (0, 1):
            for l in range(SLAB):
                k = 2 * l + var
                planes = (mains[0][k, rows], *sides(odd, mains[1][k, rows], mains[2][k, rows]))
                for part, e in ((0, SLAB + l), (1, l), (2, 2 * SLAB + l)):
                    xs[var][e] = planes[part] + jnp.where(rim, flip(pieces[part], 8 * var + l), 0.0)
            p = jnp.where(group < 4, turn(pieces[1], -64 * var - 32), turn(pieces[0], -64 * var))
            p = jnp.where(group < 8, p, turn(pieces[2], 32 - 64 * var))
            packs[var] = jnp.where(group < 12, p, 0.0)
            for l in range(SLAB):
                x = xs[var][SLAB + l]
                out_own[2 * l + var, rows] = x
                square = square + x * x
        for t in range(NT):
            first, last = t + 1, 10 - t
            news = [[None] * EXT, [None] * EXT]
            tts = [jnp.zeros((8, 128), F32)] * 2
            for e in range(first, last + 1):
                c0, up, um, vp, vm = factors(*coefficients(odd, coef, t, e, rows))
                for var in (0, 1):
                    x = xs[var][e]
                    edge = turn(packs[var], -(8 * e + 4))
                    news[var][e] = (
                        c0 * x
                        + up * xs[var][e - 1]
                        + um * xs[var][e + 1]
                        + vp * jnp.where(low, edge, turn(x, 1))
                        + vm * jnp.where(high, edge, turn(x, -1))
                    )
                    if t < NT - 1:
                        tts[var] = jnp.where((lane == 8 * e + 3) | (lane == 8 * e + 4), turn(x, 8 * e + 4), tts[var])
            if t < NT - 1:
                pu, pv = pack_coefficients(odd, coef, t, rows, group)
                c0, up, um, vp, vm = factors(pu, pv)
                for var in (0, 1):
                    p = packs[var]
                    packs[var] = (
                        c0 * p
                        + up * turn(p, 8)
                        + um * turn(p, -8)
                        + vp * jnp.where(off == 3, tts[var], turn(p, -1))
                        + vm * jnp.where(off == 4, tts[var], turn(p, 1))
                    )
            xs = news
            for var in (0, 1):
                for e in range(SLAB, 2 * SLAB):
                    fields[t, pl.ds(pl.multiple_of(var * levels + r8, 8), 8), pl.ds((e - SLAB) * BAND, BAND)] = xs[var][e]
        return square

    return lax.fori_loop(0, levels // 8, block, jnp.zeros((8, 128), F32), unroll=2)


def halves(x):
    big = x.astype(BF16)
    return big, (x - big.astype(F32)).astype(BF16)


def dot(a, b):
    return jnp.dot(a, b, preferred_element_type=F32)


def split_dot(a_big, a_small, b):
    b_big, b_small = halves(b)
    return dot(a_big, b_big) + (dot(a_small, b_big) + dot(a_big, b_small))


def message_kernel(flags, given_weight, given, sent, error_weight, innovations, message, done):
    copies = [
        pltpu.make_async_copy(source, target, done.at[i])
        for i, (source, target) in enumerate(((given_weight, error_weight), (given, innovations)))
    ]
    for copy in copies:
        copy.start()
    for copy in copies:
        copy.wait()
    owners = error_weight.shape[0] // (NT * SLOTS)
    for t in range(NT):
        for c in range(SLOTS):
            here = pl.ds((t * owners) * SLOTS + c, owners, stride=SLOTS)
            weight = error_weight[here]
            message[pl.ds(t * SLOTS + c, owners, stride=2 * NT * SLOTS)] = weight * innovations[here]
            message[pl.ds((NT + t) * SLOTS + c, owners, stride=2 * NT * SLOTS)] = weight
    send = pltpu.make_async_copy(message, sent, done.at[2])
    send.start()
    send.wait()


def prepare_kernel(levels, flags, courant, weighting, *outs):
    own, to_near, to_far, edges, table, columns = outs
    depth = courant.shape[0] // (2 * NT * SLAB)
    odd = flags[0] == 1
    lane = lanes((levels, 128))
    for k in (0, 1):
        edge = jnp.zeros((levels, 128), F32)
        for t in range(NT):
            xs = []
            for l in range(SLAB):
                plane = 8 * t + 4 * k + l
                own[plane, pl.ds(levels - 8, 8)] = jnp.zeros((8, 128), F32)
                own[plane, pl.ds(0, depth)] = courant[pl.ds((2 * t + k) * depth * SLAB + l, depth, stride=SLAB)]
                xs.append(own[plane])
                if t < NT - 1:
                    g = 4 * t + l
                    edge = jnp.where(lane // 8 == g, flip(xs[l], g), edge)
            for d in range(1, NT - t):
                west, east = xs[d - 1], xs[SLAB - d]
                to_near[2 * PLANES[t, d] + k] = jnp.where(odd, west, east)
                to_far[2 * PLANES[t, d] + k] = jnp.where(odd, east, west)
        edges[k] = edge
        table[pl.ds(levels * (k + 1) - 8, 8)] = jnp.zeros((8, 128), F32)
        table[pl.ds(levels * k, depth)] = weighting[pl.ds(depth * k, depth)]
    columns[...] = table[...].T


def pack_kernel(flags, south, north, pack):
    lane = lanes(pack.shape)
    inside = jnp.where(flags[1] < flags[2] - 1, north[...], 0.0)
    pack[...] = jnp.where(lane % 8 < 4, inside, jnp.where(flags[1] > 0, south[...], 0.0))


def edge_kernel(flags, aligned, south, north, edge):
    lane = lanes(edge.shape)
    upper = lane % 8 < 4
    fix = jnp.where(
        upper,
        jnp.where(flags[1] > 0, south[...], 0.0),
        jnp.where(flags[1] < flags[2] - 1, north[...], 0.0),
    )
    halo = jnp.where(
        upper,
        jnp.where(flags[1] < flags[2] - 1, aligned[...] + north[...], 0.0),
        jnp.where(flags[1] > 0, aligned[...] + south[...], 0.0),
    )
    edge[...] = jnp.where(lane % 64 < 32, fix, halo)


def slots_kernel(cells, flags, sent, index, counts, table, weights, grads):
    w_big, w_small = halves(table[...])
    owners = counts.shape[1]
    place = lax.broadcasted_iota(jnp.int32, (cells, owners), 0)
    for t in range(NT):
        hits, bigs, smalls = [], [], []
        for c in range(SLOTS):
            slot = jnp.where(c < counts[pl.ds(t, 1), :], index[t, pl.ds(c, 1), :], -1)
            hits.append(jnp.where(place == slot, 1.0, 0.0).astype(BF16))
            both = [sent[pl.ds((i * NT + t) * SLOTS + c, owners, stride=2 * NT * SLOTS)] for i in (0, 1)]
            big, small = halves(jnp.concatenate(both, 1))
            bigs.append(big)
            smalls.append(small)
        hit = jnp.concatenate(hits, 1)
        total = dot(hit, jnp.concatenate(bigs, 0)) + dot(hit, jnp.concatenate(smalls, 0))
        weights[t] = total[:, 128:].T
        grads[t] = split_dot(w_big, w_small, total[:, :128].T)


def right_side_kernel(levels, flags, grads, *rest):
    coef, outs = rest[:6], rest[6:]
    adjoint_sweep(flags[0] == 1, coef, grads, *outs, levels)


def hessian_kernel(levels, flags, own, near, far, s_own, s_near, s_far, weights, table, columns, moments, *rest):
    coef, rest = rest[:6], rest[6:]
    out_own, out_near, out_far, out_pack, out_field, out_moments, fields = rest
    odd = flags[0] == 1
    square = forward_sweep(odd, coef, (own, near, far), (s_own, s_near, s_far), fields, out_field, levels)
    w_big, w_small = halves(table[...])
    t_big, t_small = halves(columns[...])
    product = jnp.zeros((8, 128), F32)
    for t in range(NT):
        seen = split_dot(t_big, t_small, fields[t])
        weighed = weights[t] * seen
        product = product + jnp.sum((weighed * seen).reshape(-1, 8, SLAB, 128), axis=(0, 2))
        fields[t] = split_dot(w_big, w_small, weighed)
    lane = lanes(out_moments.shape)
    before = moments[pl.ds(0, 1), :]
    found = jnp.where(lane == 2, jnp.sum(square), jnp.where(lane == 3, jnp.sum(product), 0.0))
    out_moments[...] = jnp.where(lane < 2, turn(jnp.broadcast_to(before, lane.shape), -2), found)
    adjoint_sweep(odd, coef, fields, out_own, out_near, out_far, out_pack, levels)


def gather_kernel(flags, own, pack, near, far, *rest):
    main, message, aligned = rest[-3:]
    lane = lanes(message.shape)
    group = lane // 8
    odd = flags[0] == 1
    west, east = sides(odd, near[2 * SLAB], far[2 * SLAB])
    out, left = jnp.zeros(message.shape, F32), jnp.zeros(message.shape, F32)
    for var in (0, 1):
        p = pack[var] + turn(east, 32 - 32 * var) + turn(west, -32 - 32 * var)
        out = jnp.where(group // 4 == 2 * var, turn(p, 64 * var - 32), out)
        left = jnp.where(group // 4 == 2 * var + 1, turn(p, 64 * var), left)
        for l in range(SLAB):
            k = 2 * l + var
            x = own[k] + (near[k] + far[k])
            main[k] = x
            g = 8 * var + SLAB + l
            out = jnp.where(group == g, flip(x, g), out)
    message[...] = out
    aligned[...] = left


def final_kernel(flags, v0, v1, main, south, north, sums, solution, residual):
    total = jnp.sum(sums[...], axis=0, keepdims=True)
    lane = lanes(total.shape)
    m = [jnp.sum(jnp.where(lane == k, total, 0.0), axis=1, keepdims=True) for k in range(4)]
    a, c, d = m[1] / m[0], m[2] / m[0], m[3] / m[0]
    step0 = 1.0 / (1.0 + a)
    keep = a * step0
    ratio = (c - a * a) * step0 * step0
    p, s = keep + ratio, -step0
    curvature = p * p + 2.0 * p * s * a + s * s * c + (p * p * a + 2.0 * p * s * c + s * s * d)
    step1 = ratio / curvature
    depth = solution.shape[0] // (2 * SLAB)
    lane = lanes(south.shape)
    rim = (lane < 4) | (lane >= BAND - 4)
    fix = jnp.where(
        lane % 8 < 4,
        jnp.where(flags[1] > 0, south[...], 0.0),
        jnp.where(flags[1] < flags[2] - 1, north[...], 0.0),
    )
    for var in (0, 1):
        for l in range(SLAB):
            k = 2 * l + var
            x0, x1 = v0[k], v1[k]
            x2 = main[k] + jnp.where(rim, flip(fix, 8 * var + l), 0.0)
            rows = pl.ds(var * depth * SLAB + l, depth, stride=SLAB)
            out = (step0 + step1 * p) * x0 + (step1 * s) * x1
            left = (keep - step1 * p) * x0 + (s - step1 * (p + s)) * x1 - (step1 * s) * x2
            solution[rows] = out[:depth]
            residual[rows] = left[:depth]


def shift(x, axis, by):
    n = lax.axis_size(axis)
    return lax.ppermute(x, axis, [(i, (i + by) % n) for i in range(n)])


def far_swap(x):
    n = lax.axis_size("lon")
    return lax.ppermute(x, "lon", [(i, (i + 1 if i % 2 else i - 1) % n) for i in range(n)])


def near_swap(x):
    return lax.ppermute(x, "lon", [(i, i ^ 1) for i in range(lax.axis_size("lon"))])


def body(courant, slot_column_cells, column_counts, innovations, error_weight, weighting):
    depth = courant.shape[2]
    levels = -(-depth // 16) * 16
    owners = slot_column_cells.shape[2]
    cells = SLAB * BAND
    channels = weighting.shape[1]
    flags = jnp.stack([lax.axis_index("lon") % 2, lax.axis_index("lat"), jnp.int32(lax.axis_size("lat"))]).astype(jnp.int32)
    slots = owners * SLOTS

    (message,) = call(
        message_kernel,
        [(2 * NT * slots, channels)],
        [flags, error_weight.reshape(NT * slots, channels), innovations.reshape(NT * slots, channels)],
        [
            pltpu.VMEM((NT * slots, channels), F32), pltpu.VMEM((NT * slots, channels), F32),
            pltpu.VMEM((2 * NT * slots, channels), F32), pltpu.SemaphoreType.DMA((3,)),
        ],
        hbm_in=(1, 2),
        hbm_out=(0,),
    )
    sent = lax.all_to_all(
        message.reshape(owners, 2 * NT * SLOTS, channels), ("lon", "lat"), split_axis=0, concat_axis=0, tiled=True
    ).reshape(2 * NT * slots, channels)
    own, to_near, to_far, edges, table, columns = call(
        functools.partial(prepare_kernel, levels),
        [
            (2 * NT * SLAB, levels, 128), (12, levels, 128), (12, levels, 128), (2, levels, 128),
            (2 * levels, channels), (channels, 2 * levels),
        ],
        [flags, courant.reshape(2 * NT * depth * SLAB, BAND), weighting],
    )
    c_far, c_near = far_swap(to_far), near_swap(to_near)
    (pack,) = call(pack_kernel, [(2, levels, 128)], [flags, shift(edges, "lat", 1), shift(edges, "lat", -1)])
    index = jnp.swapaxes(slot_column_cells[:, 0], 1, 2)
    coef = [own, c_near, c_far, pack, near_swap(pack), far_swap(pack)]

    planes, parcel = (2 * SLAB, levels, 128), (2 * SLAB + 1, levels, 128)
    small = (levels, 128)
    grads = pltpu.VMEM((NT, 2 * levels, cells), F32)
    pieces = [planes, parcel, parcel, (2, levels, 128)]

    def gathered(parts, *more):
        mine, to_near, to_far, pack = parts
        return call(
            gather_kernel, [planes, small, small], [flags, mine, pack, near_swap(to_near), far_swap(to_far), *more]
        )

    def hessian(state, weights, moments, rows):
        main, message, aligned = state
        (edge,) = call(edge_kernel, [small], [flags, aligned, shift(message, "lat", 1), shift(message, "lat", -1)])
        return call(
            functools.partial(hessian_kernel, levels),
            [*pieces, planes, (rows, 128)],
            [
                flags, main, near_swap(main), far_swap(main), edge, near_swap(edge), far_swap(edge),
                weights, table, columns, moments, *coef,
            ],
            [grads],
        )

    weights, right = call(
        functools.partial(slots_kernel, cells),
        [(NT, channels, cells), (NT, 2 * levels, cells)],
        [flags, sent, index, column_counts[:, 0], table],
    )
    parts = call(functools.partial(right_side_kernel, levels), pieces, [flags, right, *coef])
    *parts, v0, moments = hessian(gathered(parts), weights, jnp.zeros((8, 128), F32), 8)
    *parts, v1, moments = hessian(gathered(parts), weights, moments, owners)
    sums = lax.all_to_all(moments, ("lon", "lat"), split_axis=0, concat_axis=0, tiled=True)
    main, message, _ = gathered(parts, sums)
    solution, residual = call(
        final_kernel,
        [(2 * depth * SLAB, BAND)] * 2,
        [flags, v0, v1, main, shift(message, "lat", 1), shift(message, "lat", -1), sums],
    )
    shape = (2, depth, SLAB, BAND)
    return solution.reshape(shape), residual.reshape(shape)


def solution(mesh):
    in_specs = (
        P(None, None, None, "lon", "lat"),
        P(None, ("lon", "lat"), None, None),
        P(None, ("lon", "lat"), None),
        P(None, ("lon", "lat"), None, None, None),
        P(None, ("lon", "lat"), None, None, None),
        P(),
    )
    out_specs = (P(None, None, "lon", "lat"), P(None, None, "lon", "lat"))
    return jax.shard_map(body, mesh=mesh, in_specs=in_specs, out_specs=out_specs, check_vma=False)
```

time: 251 us -> 205 us (0.82)
  starting transfers between devices: 94.5 us -> 51.3 us
  blocking collectives: 0 us -> 15.7 us
  local copies, waits for them, and re-layouts: 18.2 us -> 4.78 us
  Pallas kernels: 81.8 us -> 76.9 us
  other arithmetic: 4.67 us -> 0.08 us
  waiting for transfers between devices: 50.5 us -> 53.9 us
    ppermute x26 -> x8, starting transfers between devices: 65.4 us -> 6.86 us  [shift(): return lax.ppermute(x, axis, [(i, (i + by) % n) for i in range(n)])]
    ppermute x0 -> x18, starting transfers between devices: none -> 32.5 us  [the longest x9 29.5 us: near_swap(): lax.ppermute(x, 'lon', [(i, i ^ 1) for i in range(lax.axis_size('lon'))])]
    ppermute x0 -> x18, waiting for transfers between devices: none -> 23.8 us  [the longest x9 19.2 us: far_swap(): lax.ppermute(x, 'lon', [(i, (i + 1 if i % 2 else i - 1) % n) for i in ran...]
    all_to_all x2 -> x1, starting transfers between devices: 29.1 us -> 12 us  [body(): lax.all_to_all(message.reshape(owners, 2 * NT * SLOTS, channels), ('lon',...]
    all_to_all x0 -> x1, blocking collectives: none -> 15.7 us  [body(): lax.all_to_all(moments, ('lon', 'lat'), split_axis=0, concat_axis=0, tile...]
    ppermute x26 -> x8, waiting for transfers between devices: 41 us -> 30.1 us  [shift(): return lax.ppermute(x, axis, [(i, (i + by) % n) for i in range(n)])]
    all_to_all x2 -> x1, waiting for transfers between devices: 9.49 us -> 0.01 us  [body(): lax.all_to_all(message.reshape(owners, 2 * NT * SLOTS, channels), ('lon',...]
    pallas_call x8 -> x13, Pallas kernels: 81.8 us -> 76.9 us  [call(): pl.pallas_call(kernel, out_shape=[jax.ShapeDtypeStruct(s, F32) for s in s...]
  transfers between devices with their start and end apart: 28 -> 27, of which waited for: 17 -> 15; matrix products, arithmetic and copies ran while one was open for 5% -> 0% of each run, Pallas kernels for 1% -> 5%
where the time goes in v2:
time: 205 us; the launch traced here: 204 us
  Pallas kernels  76.9 us (38%)
  waiting for transfers between devices  53.9 us (26%)
  starting transfers between devices  51.3 us (25%)
  blocking collectives  15.7 us (8%)
  local copies, waits for them, and re-layouts  4.78 us (2%)
    pallas_call x13, Pallas kernels, call(): pl.pallas_call(kernel, out_shape=[jax.ShapeDtypeStruct(s, F32) for s in s...  76.9 us
    ppermute x8, waiting for transfers between devices, shift(): return lax.ppermute(x, axis, [(i, (i + by) % n) for i in range(n)])  30.1 us
    ppermute x9, starting transfers between devices, near_swap(): lax.ppermute(x, 'lon', [(i, i ^ 1) for i in range(lax.axis_size('lon'))])  29.5 us
    ppermute x9, waiting for transfers between devices, far_swap(): lax.ppermute(x, 'lon', [(i, (i + 1 if i % 2 else i - 1) % n) for i in ran...  19.2 us
    all_to_all x1, blocking collectives, body(): lax.all_to_all(moments, ('lon', 'lat'), split_axis=0, concat_axis=0, tile...  15.7 us
    all_to_all x1, starting transfers between devices, body(): lax.all_to_all(message.reshape(owners, 2 * NT * SLOTS, channels), ('lon',...  12 us
    ppermute x8, starting transfers between devices, shift(): return lax.ppermute(x, axis, [(i, (i + by) % n) for i in range(n)])  6.86 us
    unnamed x16, local copies, waits for them, and re-layouts  4.77 us
  transfers between devices with their start and end apart: 27, of which 15 were waited for; matrix products, arithmetic and copies ran while one was open for 0% of the time, Pallas kernels for 5%

profile of v2, /device:TPU:1, one launch (start us, length us, event | category | flops | bytes accessed | tf_op | source)
XLA Modules:
  0.0 203.7 jit_solution(10144063968098606119)
XLA Ops:
  0.7 1.2 copy-done.1
  1.9 1.2 copy-done.2
  3.2 3.8 %shard_map.77 = f32[4096,128]{1,0:T(8,128)} custom-call(s32[3]{0:T(128)S(1)} %pad_add_fusion.flags, f32[2048,128]{1,0:T(8,128)S(1)} %bitcast.18, f32[2048,128]{1,0:T(8,128)S(1)} %bitcast.19), custom_call_target="tpu_custom_call" | custom-call | bytes 2097164 | tf_op jit(solution)/shard_map/pallas_call | solution.py:25
  7.0 12.0 %all-to-all-start = ((f32[128,32,128]{2,1,0:T(8,128)}), f32[128,32,128]{2,1,0:T(8,128)}, u32[]{:S(2)}, u32[]{:S(2)}) async-start(f32[128,32,128]{2,1,0:T(8,128)} %bitcast.4), calls=%async_computation | async-start | bytes 4194304 | tf_op jit(solution)/shard_map/all_to_all | solution.py:423
  18.9 1.6 copy-done
  20.6 2.4 %shard_map.78 = (f32[32,144,128]{2,1,0:T(8,128)S(1)}, f32[12,144,128]{2,1,0:T(8,128)}, f32[12,144,128]{2,1,0:T(8,128)}, f32[2,144,128]{2,1,0:T(8,128)S(1)}, f32[...) custom-call(s32[3]{0:T(128)S(1)} %pad_add_fusion.flags, f32[4384,128]{1,0:T(8,128)S(1)} %bitcast.17, f32[274,128]{1,0:T(8,128)S(1)} %copy-done.5), custom_call_target="tpu_custom_call" | custom-call | bytes 2384908 | tf_op jit(solution)/shard_map/pallas_call | solution.py:25
  23.0 0.7 copy-done.3
  23.7 1.1 collective-permute-start
  24.8 0.6 collective-permute-start.1
  25.5 2.5 %collective-permute-start.3 = (f32[2,144,128]{2,1,0:T(8,128)S(1)}, f32[2,144,128]{2,1,0:T(8,128)S(1)}, u32[]{:S(2)}, u32[]{:S(2)}) collective-permute-start(f32[2,144,128]{2,1,0:T(8,128)S(1)} %get-tuple-element.41), channel_id=1, source_target_pairs={{0,3},{1,0},{2,1},{3,2},{4,7},{5,4},{6,5},{7,6},{8,11},{9,8},{10,9... | collective-permute-start | bytes 442376 | tf_op jit(solution)/shard_map/ppermute | solution.py:391
  28.0 17.7 %collective-permute-done.3.north = f32[2,144,128]{2,1,0:T(8,128)S(1)} collective-permute-done((f32[2,144,128]{2,1,0:T(8,128)S(1)}, f32[2,144,128]{2,1,0:T(8,128)S(1)}, u32[]{:S(2)}, u32[]{:S(2)}) %collective-permute-start.3) | collective-permute-done | bytes 147488 | tf_op jit(solution)/shard_map/ppermute | solution.py:391
  45.7 1.3 collective-permute-done.2.south
  47.0 0.6 shard_map.80.rest_3_
  47.6 1.9 collective-permute-start.5
  49.5 4.0 %collective-permute-start.4 = (f32[2,144,128]{2,1,0:T(8,128)S(1)}, f32[2,144,128]{2,1,0:T(8,128)}, u32[]{:S(2)}, u32[]{:S(2)}) collective-permute-start(f32[2,144,128]{2,1,0:T(8,128)S(1)} %shard_map.80.rest_3_), channel_id=1, source_target_pairs={{0,4},{4,0},{8,12},{12,8},{16,20},{20,16},{24,28},{28,24},{32,36},... | collective-permute-start | bytes 442376 | tf_op jit(solution)/shard_map/ppermute | solution.py:400
  53.5 6.2 %shard_map.79 = (f32[4,128,512]{2,1,0:T(8,128)S(1)}, f32[4,288,512]{2,1,0:T(8,128)S(1)}) custom-call(s32[3]{0:T(128)S(1)} %pad_add_fusion.flags, f32[4096,128]{1,0:T(8,128)} %bitcast.5.sent, s32[4,4,128]{2,1,0:T(4,128)S(1)} %bitcast.23, s32[4,128]{1,0:T(4,128)S(1)} %bitcast.24, f32[288,128]{1,0:T(8,128)S(1)} %get-tuple-element.36.table), custom_call_target="tpu_custom_call" | custom-call | bytes 2254860 | tf_op jit(solution)/shard_map/pallas_call | solution.py:25
  59.8 10.1 %shard_map.81 = (f32[8,144,128]{2,1,0:T(8,128)S(1)}, f32[9,144,128]{2,1,0:T(8,128)S(1)}, f32[9,144,128]{2,1,0:T(8,128)S(1)}, f32[2,144,128]{2,1,0:T(8,128)S(1)}) custom-call(s32[3]{0:T(128)S(1)} %pad_add_fusion.flags, f32[4,288,512]{2,1,0:T(8,128)S(1)} %get-tuple-element.37.grads, f32[32,144,128]{2,1,0:T(8,128)S(1)} %get-tuple-element.38.rest_0_, ...), custom_call_target="tpu_custom_call" | custom-call | bytes 6930444 | tf_op jit(solution)/shard_map/pallas_call | solution.py:25
  70.2 2.0 collective-permute-done.6.near
  72.2 8.4 %collective-permute-done.7.far = f32[9,144,128]{2,1,0:T(8,128)S(1)} collective-permute-done((f32[9,144,128]{2,1,0:T(8,128)S(1)}, f32[9,144,128]{2,1,0:T(8,128)S(1)}, u32[]{:S(2)}, u32[]{:S(2)}) %collective-permute-start.7) | collective-permute-done | bytes 663584 | tf_op jit(solution)/shard_map/ppermute | solution.py:396
  80.5 1.0 shard_map.82
  81.6 4.7 %collective-permute-start.8 = (f32[8,144,128]{2,1,0:T(8,128)S(1)}, f32[8,144,128]{2,1,0:T(8,128)S(1)}, u32[]{:S(2)}, u32[]{:S(2)}) collective-permute-start(f32[8,144,128]{2,1,0:T(8,128)S(1)} %get-tuple-element.46.own), channel_id=1, source_target_pairs={{0,4},{4,0},{8,12},{12,8},{16,20},{20,16},{24,28},{28,24},{32,36},... | collective-permute-start | bytes 1769480 | tf_op jit(solution)/shard_map/ppermute | solution.py:400
  86.3 0.4 collective-permute-start.11
  86.8 1.0 collective-permute-start.10
  87.8 2.4 %collective-permute-done.11.north = f32[144,128]{1,0:T(8,128)S(1)} collective-permute-done((f32[144,128]{1,0:T(8,128)S(1)}, f32[144,128]{1,0:T(8,128)S(1)}, u32[]{:S(2)}, u32[]{:S(2)}) %collective-permute-start.11) | collective-permute-done | bytes 73760 | tf_op jit(solution)/shard_map/ppermute | solution.py:391
  90.2 1.3 collective-permute-done.10.south
  91.6 0.6 shard_map.83.s_own
  92.2 4.0 %collective-permute-start.12 = (f32[144,128]{1,0:T(8,128)S(1)}, f32[144,128]{1,0:T(8,128)S(1)}, u32[]{:S(2)}, u32[]{:S(2)}) collective-permute-start(f32[144,128]{1,0:T(8,128)S(1)} %shard_map.83.s_own), channel_id=1, source_target_pairs={{0,4},{4,0},{8,12},{12,8},{16,20},{20,16},{24,28},{28,24},{32,36},... | collective-permute-start | bytes 221192 | tf_op jit(solution)/shard_map/ppermute | solution.py:400
  96.3 0.8 collective-permute-done.12.s_near
  97.2 23.6 %shard_map.84 = (f32[8,144,128]{2,1,0:T(8,128)S(1)}, f32[9,144,128]{2,1,0:T(8,128)S(1)}, f32[9,144,128]{2,1,0:T(8,128)S(1)}, f32[2,144,128]{2,1,0:T(8,128)S(1)},...) custom-call(s32[3]{0:T(128)S(1)} %pad_add_fusion.flags, f32[8,144,128]{2,1,0:T(8,128)S(1)} %get-tuple-element.46.own, ...), custom_call_target="tpu_custom_call" | custom-call | bytes 7909388 | tf_op jit(solution)/shard_map/pallas_call | solution.py:25
  120.8 3.4 %collective-permute-start.14 = (f32[9,144,128]{2,1,0:T(8,128)S(1)}, f32[9,144,128]{2,1,0:T(8,128)S(1)}, u32[]{:S(2)}, u32[]{:S(2)}) collective-permute-start(f32[9,144,128]{2,1,0:T(8,128)S(1)} %get-tuple-element.54), channel_id=1, source_target_pairs={{0,4},{4,0},{8,12},{12,8},{16,20},{20,16},{24,28},{28,24},{32,36},... | collective-permute-start | bytes 1990664 | tf_op jit(solution)/shard_map/ppermute | solution.py:400
  124.2 1.7 collective-permute-done.14.near
  125.9 8.7 %collective-permute-done.15.far = f32[9,144,128]{2,1,0:T(8,128)S(1)} collective-permute-done((f32[9,144,128]{2,1,0:T(8,128)S(1)}, f32[9,144,128]{2,1,0:T(8,128)S(1)}, u32[]{:S(2)}, u32[]{:S(2)}) %collective-permute-start.15) | collective-permute-done | bytes 663584 | tf_op jit(solution)/shard_map/ppermute | solution.py:396
  134.6 1.0 shard_map.85
  135.7 6.0 %collective-permute-start.16 = (f32[8,144,128]{2,1,0:T(8,128)S(1)}, f32[8,144,128]{2,1,0:T(8,128)S(1)}, u32[]{:S(2)}, u32[]{:S(2)}) collective-permute-start(f32[8,144,128]{2,1,0:T(8,128)S(1)} %get-tuple-element.56.own), channel_id=1, source_target_pairs={{0,4},{4,0},{8,12},{12,8},{16,20},{20,16},{24,28},{28,24},{32,36},... | collective-permute-start | bytes 1769480 | tf_op jit(solution)/shard_map/ppermute | solution.py:400
  141.7 1.5 collective-permute-start.18
  143.1 2.4 %collective-permute-done.19.north = f32[144,128]{1,0:T(8,128)S(1)} collective-permute-done((f32[144,128]{1,0:T(8,128)S(1)}, f32[144,128]{1,0:T(8,128)S(1)}, u32[]{:S(2)}, u32[]{:S(2)}) %collective-permute-start.19) | collective-permute-done | bytes 73760 | tf_op jit(solution)/shard_map/ppermute | solution.py:391
  145.6 0.9 collective-permute-done.18.south
  146.5 0.6 shard_map.86.s_own
  147.1 1.8 collective-permute-start.20
  148.9 2.1 %collective-permute-done.21.s_far = f32[144,128]{1,0:T(8,128)S(1)} collective-permute-done((f32[144,128]{1,0:T(8,128)S(1)}, f32[144,128]{1,0:T(8,128)S(1)}, u32[]{:S(2)}, u32[]{:S(2)}) %collective-permute-start.21) | collective-permute-done | bytes 73760 | tf_op jit(solution)/shard_map/ppermute | solution.py:396
  151.0 23.6 %shard_map.87 = (f32[8,144,128]{2,1,0:T(8,128)S(1)}, f32[9,144,128]{2,1,0:T(8,128)S(1)}, f32[9,144,128]{2,1,0:T(8,128)S(1)}, f32[2,144,128]{2,1,0:T(8,128)S(1)},...) custom-call(s32[3]{0:T(128)S(1)} %pad_add_fusion.flags, f32[8,144,128]{2,1,0:T(8,128)S(1)} %get-tuple-element.56.own, ...), custom_call_target="tpu_custom_call" | custom-call | bytes 7909388 | tf_op jit(solution)/shard_map/pallas_call | solution.py:25
  174.7 4.4 %collective-permute-start.22 = (f32[9,144,128]{2,1,0:T(8,128)S(1)}, f32[9,144,128]{2,1,0:T(8,128)S(1)}, u32[]{:S(2)}, u32[]{:S(2)}) collective-permute-start(f32[9,144,128]{2,1,0:T(8,128)S(1)} %get-tuple-element.63), channel_id=1, source_target_pairs={{0,4},{4,0},{8,12},{12,8},{16,20},{20,16},{24,28},{28,24},{32,36},... | collective-permute-start | bytes 1990664 | tf_op jit(solution)/shard_map/ppermute | solution.py:400
  179.1 15.7 %all_to_all.16 = f32[128,1,128]{2,1,0:T(1,128)S(1)} all-to-all(f32[128,1,128]{2,1,0:T(1,128)S(1)} %bitcast.22), channel_id=1, replica_groups=mesh['lon'=32,'lat'=4] {'lon','lat'}, dimensions={0} | all-to-all | bytes 131072 | tf_op jit(solution)/shard_map/all_to_all | solution.py:471
  194.8 1.5 shard_map.88
  196.3 1.0 collective-permute-start.25
  197.8 1.7 collective-permute-done.25.north
  199.5 2.3 %collective-permute-done.24.south = f32[144,128]{1,0:T(8,128)S(1)} collective-permute-done((f32[144,128]{1,0:T(8,128)S(1)}, f32[144,128]{1,0:T(8,128)S(1)}, u32[]{:S(2)}, u32[]{:S(2)}) %collective-permute-start.24) | collective-permute-done | bytes 73760 | tf_op jit(solution)/shard_map/ppermute | solution.py:391
  201.8 1.9 shard_map.89
  (38 shorter events, 1.2 us)
Async XLA Ops:
  0.7 1.2 copy-start.1
  1.9 1.2 copy-start.2
  6.9 12.0 %copy-start.5 = (f32[274,128]{1,0:T(8,128)S(1)}, f32[274,128]{1,0:T(8,128)}, u32[]{:S(2)}) copy-start(f32[274,128]{1,0:T(8,128)} %weighting.1) | copy-start | bytes 420868
  7.0 46.6 %all-to-all-start = ((f32[128,32,128]{2,1,0:T(8,128)}), f32[128,32,128]{2,1,0:T(8,128)}, u32[]{:S(2)}, u32[]{:S(2)}) async-start(f32[128,32,128]{2,1,0:T(8,128)} %bitcast.4), calls=%async_computation | async-start | bytes 4194304 | tf_op jit(solution)/shard_map/all_to_all | solution.py:423
  18.9 1.6 copy-start
  20.6 33.0 %copy-start.6 = (s32[4,1,128,4]{2,3,1,0:T(4,128)S(1)}, s32[4,1,128,4]{2,3,1,0:T(4,128)}, u32[]{:S(2)}) copy-start(s32[4,1,128,4]{2,3,1,0:T(4,128)} %param.7) | copy-start | bytes 24580
  20.6 33.0 %copy-start.7 = (s32[4,1,128]{2,1,0:T(1,128)S(1)}, s32[4,1,128]{2,1,0:T(1,128)}, u32[]{:S(2)}) copy-start(s32[4,1,128]{2,1,0:T(1,128)} %param.8) | copy-start | bytes 6148
  23.0 0.7 copy-start.3
  23.7 36.1 %collective-permute-start = (f32[12,144,128]{2,1,0:T(8,128)}, f32[12,144,128]{2,1,0:T(8,128)S(1)}, u32[]{:S(2)}, u32[]{:S(2)}) collective-permute-start(f32[12,144,128]{2,1,0:T(8,128)} %get-tuple-element.39), channel_id=1, source_target_pairs={{0,4},{4,0},{8,12},{12,8},{16,20},{20,16},{24,28},{28,24},{32,36},... | collective-permute-start | bytes 2654216 | tf_op jit(solution)/shard_map/ppermute | solution.py:400
  24.8 35.0 %collective-permute-start.1 = (f32[12,144,128]{2,1,0:T(8,128)}, f32[12,144,128]{2,1,0:T(8,128)}, u32[]{:S(2)}, u32[]{:S(2)}) collective-permute-start(f32[12,144,128]{2,1,0:T(8,128)} %get-tuple-element.40), channel_id=1, source_target_pairs={{0,124},{4,8},{8,4},{12,16},{16,12},{20,24},{24,20},{28,32},{32,28... | collective-permute-start | bytes 2654216 | tf_op jit(solution)/shard_map/ppermute | solution.py:396
  25.5 20.2 %collective-permute-start.3 = (f32[2,144,128]{2,1,0:T(8,128)S(1)}, f32[2,144,128]{2,1,0:T(8,128)S(1)}, u32[]{:S(2)}, u32[]{:S(2)}) collective-permute-start(f32[2,144,128]{2,1,0:T(8,128)S(1)} %get-tuple-element.41), channel_id=1, source_target_pairs={{0,3},{1,0},{2,1},{3,2},{4,7},{5,4},{6,5},{7,6},{8,11},{9,8},{10,9... | collective-permute-start | bytes 442376 | tf_op jit(solution)/shard_map/ppermute | solution.py:391
  27.9 19.0 %collective-permute-start.2 = (f32[2,144,128]{2,1,0:T(8,128)S(1)}, f32[2,144,128]{2,1,0:T(8,128)S(1)}, u32[]{:S(2)}, u32[]{:S(2)}) collective-permute-start(f32[2,144,128]{2,1,0:T(8,128)S(1)} %get-tuple-element.41), channel_id=1, source_target_pairs={{0,1},{1,2},{2,3},{3,0},{4,5},{5,6},{6,7},{7,4},{8,9},{9,10},{10,1... | collective-permute-start | bytes 442376 | tf_op jit(solution)/shard_map/ppermute | solution.py:391
  47.6 12.2 %collective-permute-start.5 = (f32[2,144,128]{2,1,0:T(8,128)S(1)}, f32[2,144,128]{2,1,0:T(8,128)}, u32[]{:S(2)}, u32[]{:S(2)}) collective-permute-start(f32[2,144,128]{2,1,0:T(8,128)S(1)} %shard_map.80.rest_3_), channel_id=1, source_target_pairs={{0,124},{4,8},{8,4},{12,16},{16,12},{20,24},{24,20},{28,32},{32,28... | collective-permute-start | bytes 442376 | tf_op jit(solution)/shard_map/ppermute | solution.py:396
  49.5 10.3 %collective-permute-start.4 = (f32[2,144,128]{2,1,0:T(8,128)S(1)}, f32[2,144,128]{2,1,0:T(8,128)}, u32[]{:S(2)}, u32[]{:S(2)}) collective-permute-start(f32[2,144,128]{2,1,0:T(8,128)S(1)} %shard_map.80.rest_3_), channel_id=1, source_target_pairs={{0,4},{4,0},{8,12},{12,8},{16,20},{20,16},{24,28},{28,24},{32,36},... | collective-permute-start | bytes 442376 | tf_op jit(solution)/shard_map/ppermute | solution.py:400
  70.0 27.2 %copy-start.4 = (f32[128,288]{1,0:T(8,128)S(1)}, f32[128,288]{1,0:T(8,128)}, u32[]{:S(2)}) copy-start(f32[128,288]{1,0:T(8,128)} %copy-done.3) | copy-start | bytes 442372
  70.0 2.2 %collective-permute-start.6 = (f32[9,144,128]{2,1,0:T(8,128)S(1)}, f32[9,144,128]{2,1,0:T(8,128)S(1)}, u32[]{:S(2)}, u32[]{:S(2)}) collective-permute-start(f32[9,144,128]{2,1,0:T(8,128)S(1)} %get-tuple-element.44), channel_id=1, source_target_pairs={{0,4},{4,0},{8,12},{12,8},{16,20},{20,16},{24,28},{28,24},{32,36},... | collective-permute-start | bytes 1990664 | tf_op jit(solution)/shard_map/ppermute | solution.py:400
  70.1 10.5 %collective-permute-start.7 = (f32[9,144,128]{2,1,0:T(8,128)S(1)}, f32[9,144,128]{2,1,0:T(8,128)S(1)}, u32[]{:S(2)}, u32[]{:S(2)}) collective-permute-start(f32[9,144,128]{2,1,0:T(8,128)S(1)} %get-tuple-element.45), channel_id=1, source_target_pairs={{0,124},{4,8},{8,4},{12,16},{16,12},{20,24},{24,20},{28,32},{32,28... | collective-permute-start | bytes 1990664 | tf_op jit(solution)/shard_map/ppermute | solution.py:396
  81.5 15.6 %collective-permute-start.9 = (f32[8,144,128]{2,1,0:T(8,128)S(1)}, f32[8,144,128]{2,1,0:T(8,128)S(1)}, u32[]{:S(2)}, u32[]{:S(2)}) collective-permute-start(f32[8,144,128]{2,1,0:T(8,128)S(1)} %get-tuple-element.46.own), channel_id=1, source_target_pairs={{0,124},{4,8},{8,4},{12,16},{16,12},{20,24},{24,20},{28,32},{32,28... | collective-permute-start | bytes 1769480 | tf_op jit(solution)/shard_map/ppermute | solution.py:396
  81.6 15.5 %collective-permute-start.8 = (f32[8,144,128]{2,1,0:T(8,128)S(1)}, f32[8,144,128]{2,1,0:T(8,128)S(1)}, u32[]{:S(2)}, u32[]{:S(2)}) collective-permute-start(f32[8,144,128]{2,1,0:T(8,128)S(1)} %get-tuple-element.46.own), channel_id=1, source_target_pairs={{0,4},{4,0},{8,12},{12,8},{16,20},{20,16},{24,28},{28,24},{32,36},... | collective-permute-start | bytes 1769480 | tf_op jit(solution)/shard_map/ppermute | solution.py:400
  86.3 3.9 %collective-permute-start.11 = (f32[144,128]{1,0:T(8,128)S(1)}, f32[144,128]{1,0:T(8,128)S(1)}, u32[]{:S(2)}, u32[]{:S(2)}) collective-permute-start(f32[144,128]{1,0:T(8,128)S(1)} %get-tuple-element.48), channel_id=1, source_target_pairs={{0,3},{1,0},{2,1},{3,2},{4,7},{5,4},{6,5},{7,6},{8,11},{9,8},{10,9... | collective-permute-start | bytes 221192 | tf_op jit(solution)/shard_map/ppermute | solution.py:391
  86.8 4.8 %collective-permute-start.10 = (f32[144,128]{1,0:T(8,128)S(1)}, f32[144,128]{1,0:T(8,128)S(1)}, u32[]{:S(2)}, u32[]{:S(2)}) collective-permute-start(f32[144,128]{1,0:T(8,128)S(1)} %get-tuple-element.48), channel_id=1, source_target_pairs={{0,1},{1,2},{2,3},{3,0},{4,5},{5,6},{6,7},{7,4},{8,9},{9,10},{10,1... | collective-permute-start | bytes 221192 | tf_op jit(solution)/shard_map/ppermute | solution.py:391
  92.1 4.2 %collective-permute-start.13 = (f32[144,128]{1,0:T(8,128)S(1)}, f32[144,128]{1,0:T(8,128)S(1)}, u32[]{:S(2)}, u32[]{:S(2)}) collective-permute-start(f32[144,128]{1,0:T(8,128)S(1)} %shard_map.83.s_own), channel_id=1, source_target_pairs={{0,124},{4,8},{8,4},{12,16},{16,12},{20,24},{24,20},{28,32},{32,28... | collective-permute-start | bytes 221192 | tf_op jit(solution)/shard_map/ppermute | solution.py:396
  92.2 4.9 %collective-permute-start.12 = (f32[144,128]{1,0:T(8,128)S(1)}, f32[144,128]{1,0:T(8,128)S(1)}, u32[]{:S(2)}, u32[]{:S(2)}) collective-permute-start(f32[144,128]{1,0:T(8,128)S(1)} %shard_map.83.s_own), channel_id=1, source_target_pairs={{0,4},{4,0},{8,12},{12,8},{16,20},{20,16},{24,28},{28,24},{32,36},... | collective-permute-start | bytes 221192 | tf_op jit(solution)/shard_map/ppermute | solution.py:400
  120.8 5.1 %collective-permute-start.14 = (f32[9,144,128]{2,1,0:T(8,128)S(1)}, f32[9,144,128]{2,1,0:T(8,128)S(1)}, u32[]{:S(2)}, u32[]{:S(2)}) collective-permute-start(f32[9,144,128]{2,1,0:T(8,128)S(1)} %get-tuple-element.54), channel_id=1, source_target_pairs={{0,4},{4,0},{8,12},{12,8},{16,20},{20,16},{24,28},{28,24},{32,36},... | collective-permute-start | bytes 1990664 | tf_op jit(solution)/shard_map/ppermute | solution.py:400
  124.2 10.4 %collective-permute-start.15 = (f32[9,144,128]{2,1,0:T(8,128)S(1)}, f32[9,144,128]{2,1,0:T(8,128)S(1)}, u32[]{:S(2)}, u32[]{:S(2)}) collective-permute-start(f32[9,144,128]{2,1,0:T(8,128)S(1)} %get-tuple-element.55), channel_id=1, source_target_pairs={{0,124},{4,8},{8,4},{12,16},{16,12},{20,24},{24,20},{28,32},{32,28... | collective-permute-start | bytes 1990664 | tf_op jit(solution)/shard_map/ppermute | solution.py:396
  135.6 15.4 %collective-permute-start.17 = (f32[8,144,128]{2,1,0:T(8,128)S(1)}, f32[8,144,128]{2,1,0:T(8,128)S(1)}, u32[]{:S(2)}, u32[]{:S(2)}) collective-permute-start(f32[8,144,128]{2,1,0:T(8,128)S(1)} %get-tuple-element.56.own), channel_id=1, source_target_pairs={{0,124},{4,8},{8,4},{12,16},{16,12},{20,24},{24,20},{28,32},{32,28... | collective-permute-start | bytes 1769480 | tf_op jit(solution)/shard_map/ppermute | solution.py:396
  135.7 15.3 %collective-permute-start.16 = (f32[8,144,128]{2,1,0:T(8,128)S(1)}, f32[8,144,128]{2,1,0:T(8,128)S(1)}, u32[]{:S(2)}, u32[]{:S(2)}) collective-permute-start(f32[8,144,128]{2,1,0:T(8,128)S(1)} %get-tuple-element.56.own), channel_id=1, source_target_pairs={{0,4},{4,0},{8,12},{12,8},{16,20},{20,16},{24,28},{28,24},{32,36},... | collective-permute-start | bytes 1769480 | tf_op jit(solution)/shard_map/ppermute | solution.py:400
  141.7 3.9 %collective-permute-start.19 = (f32[144,128]{1,0:T(8,128)S(1)}, f32[144,128]{1,0:T(8,128)S(1)}, u32[]{:S(2)}, u32[]{:S(2)}) collective-permute-start(f32[144,128]{1,0:T(8,128)S(1)} %get-tuple-element.58), channel_id=1, source_target_pairs={{0,3},{1,0},{2,1},{3,2},{4,7},{5,4},{6,5},{7,6},{8,11},{9,8},{10,9... | collective-permute-start | bytes 221192 | tf_op jit(solution)/shard_map/ppermute | solution.py:391
  141.7 4.8 %collective-permute-start.18 = (f32[144,128]{1,0:T(8,128)S(1)}, f32[144,128]{1,0:T(8,128)S(1)}, u32[]{:S(2)}, u32[]{:S(2)}) collective-permute-start(f32[144,128]{1,0:T(8,128)S(1)} %get-tuple-element.58), channel_id=1, source_target_pairs={{0,1},{1,2},{2,3},{3,0},{4,5},{5,6},{6,7},{7,4},{8,9},{9,10},{10,1... | collective-permute-start | bytes 221192 | tf_op jit(solution)/shard_map/ppermute | solution.py:391
  147.0 3.9 %collective-permute-start.21 = (f32[144,128]{1,0:T(8,128)S(1)}, f32[144,128]{1,0:T(8,128)S(1)}, u32[]{:S(2)}, u32[]{:S(2)}) collective-permute-start(f32[144,128]{1,0:T(8,128)S(1)} %shard_map.86.s_own), channel_id=1, source_target_pairs={{0,124},{4,8},{8,4},{12,16},{16,12},{20,24},{24,20},{28,32},{32,28... | collective-permute-start | bytes 221192 | tf_op jit(solution)/shard_map/ppermute | solution.py:396
  147.1 3.9 %collective-permute-start.20 = (f32[144,128]{1,0:T(8,128)S(1)}, f32[144,128]{1,0:T(8,128)S(1)}, u32[]{:S(2)}, u32[]{:S(2)}) collective-permute-start(f32[144,128]{1,0:T(8,128)S(1)} %shard_map.86.s_own), channel_id=1, source_target_pairs={{0,4},{4,0},{8,12},{12,8},{16,20},{20,16},{24,28},{28,24},{32,36},... | collective-permute-start | bytes 221192 | tf_op jit(solution)/shard_map/ppermute | solution.py:400
  174.7 20.2 %collective-permute-start.22 = (f32[9,144,128]{2,1,0:T(8,128)S(1)}, f32[9,144,128]{2,1,0:T(8,128)S(1)}, u32[]{:S(2)}, u32[]{:S(2)}) collective-permute-start(f32[9,144,128]{2,1,0:T(8,128)S(1)} %get-tuple-element.63), channel_id=1, source_target_pairs={{0,4},{4,0},{8,12},{12,8},{16,20},{20,16},{24,28},{28,24},{32,36},... | collective-permute-start | bytes 1990664 | tf_op jit(solution)/shard_map/ppermute | solution.py:400
  179.1 15.8 %collective-permute-start.23 = (f32[9,144,128]{2,1,0:T(8,128)S(1)}, f32[9,144,128]{2,1,0:T(8,128)S(1)}, u32[]{:S(2)}, u32[]{:S(2)}) collective-permute-start(f32[9,144,128]{2,1,0:T(8,128)S(1)} %get-tuple-element.64), channel_id=1, source_target_pairs={{0,124},{4,8},{8,4},{12,16},{16,12},{20,24},{24,20},{28,32},{32,28... | collective-permute-start | bytes 1990664 | tf_op jit(solution)/shard_map/ppermute | solution.py:396
  196.3 3.2 %collective-permute-start.25 = (f32[144,128]{1,0:T(8,128)S(1)}, f32[144,128]{1,0:T(8,128)S(1)}, u32[]{:S(2)}, u32[]{:S(2)}) collective-permute-start(f32[144,128]{1,0:T(8,128)S(1)} %get-tuple-element.67), channel_id=1, source_target_pairs={{0,3},{1,0},{2,1},{3,2},{4,7},{5,4},{6,5},{7,6},{8,11},{9,8},{10,9... | collective-permute-start | bytes 221192 | tf_op jit(solution)/shard_map/ppermute | solution.py:391
  197.4 4.4 %collective-permute-start.24 = (f32[144,128]{1,0:T(8,128)S(1)}, f32[144,128]{1,0:T(8,128)S(1)}, u32[]{:S(2)}, u32[]{:S(2)}) collective-permute-start(f32[144,128]{1,0:T(8,128)S(1)} %get-tuple-element.67), channel_id=1, source_target_pairs={{0,1},{1,2},{2,3},{3,0},{4,5},{5,6},{6,7},{7,4},{8,9},{9,10},{10,1... | collective-permute-start | bytes 221192 | tf_op jit(solution)/shard_map/ppermute | solution.py:391

commit v3 on v0

v3 whole, which is shorter than its diff:
```python
import functools

import jax
import jax.numpy as jnp
from jax import lax
from jax.experimental import pallas as pl
from jax.experimental.pallas import tpu as pltpu
from jax.sharding import PartitionSpec as P

F32 = jnp.float32
BF16 = jnp.bfloat16
NT = 4
SLAB = 4
BAND = 128
EXT = 3 * SLAB
SLOTS = 4
TILES = 17
ROWS = 8 * TILES
REST = 9
SHARE = SLAB * REST
BASE = (0, 10, 18, 24)
PLANES = {(0, 1): 0, (0, 2): 1, (0, 3): 2, (1, 1): 3, (1, 2): 4, (2, 1): 5}
VMEM = pl.BlockSpec(memory_space=pltpu.VMEM)
HBM = pl.BlockSpec(memory_space=pltpu.HBM)
SMEM = pl.BlockSpec(memory_space=pltpu.SMEM)


def call(kernel, shapes, inputs, scratch=(), flops=0, hbm_in=(), hbm_out=()):
    nbytes = sum(x.size * x.dtype.itemsize for x in inputs)
    return pl.pallas_call(
        kernel,
        out_shape=[jax.ShapeDtypeStruct(s, F32) for s in shapes],
        in_specs=[SMEM] + [HBM if i in hbm_in else VMEM for i in range(1, len(inputs))],
        out_specs=[HBM if i in hbm_out else VMEM for i in range(len(shapes))],
        scratch_shapes=list(scratch),
        compiler_params=pltpu.CompilerParams(vmem_limit_bytes=32 << 20),
        cost_estimate=pl.CostEstimate(flops=flops, bytes_accessed=nbytes, transcendentals=0),
    )(*inputs)


def turn(x, shift):
    shift %= 128
    return pltpu.roll(x, shift, 1) if shift else x


def drop(x, by):
    return pltpu.roll(x, by % 8, 0)


def lanes(shape=(8, 128)):
    return lax.broadcasted_iota(jnp.int32, shape, len(shape) - 1)


def depths():
    return lax.broadcasted_iota(jnp.int32, (8, 128), 0)


def tile(m):
    return pl.ds(8 * m, 8)


def parts(u):
    plus = jnp.maximum(u, 0.0)
    return plus, plus - u


def factors(u, v):
    up, um = parts(u)
    vp, vm = parts(v)
    return 1.0 - (up + um) - (vp + vm), up, um, vp, vm


def forward_sweep(main_c, left_c, xs, lefts):
    for t in range(NT):
        src, dst, low, high = xs[t], xs[t + 1], t + 1, 10 - t

        def longitude(e, carry, src=src, dst=dst, first=2 * (1 + BASE[t] - low)):
            k = first + 2 * e
            here = [src[var * EXT + e, tile(0)] for var in (0, 1)]
            start = here
            before = [drop(src[var * EXT + e, tile(TILES - 1)], 1) for var in (0, 1)]
            for m in range(TILES):
                c0, up, um, vp, vm = factors(main_c[k, tile(m)], main_c[k + 1, tile(m)])
                after = [src[var * EXT + e, tile(m + 1)] if m < TILES - 1 else drop(start[var], -1) for var in (0, 1)]
                for var in (0, 1):
                    p = var * EXT + e
                    dst[p, tile(m)] = (
                        c0 * here[var]
                        + (up * src[p - 1, tile(m)] + um * src[p + 1, tile(m)])
                        + (vp * before[var] + vm * after[var])
                    )
                before, here = here, after
            return carry

        lax.fori_loop(low, high + 1, longitude, 0)
        for m in range(TILES):
            c0, up, um, vp, vm = factors(left_c[2 * t, tile(m)], left_c[2 * t + 1, tile(m)])
            for var in (0, 1):
                x = lefts[t][var, tile(m)]
                before = lefts[t][var, tile(m - 1)] if m else drop(lefts[t][var, tile(TILES - 1)], 1)
                after = lefts[t][var, tile(m + 1)] if m < TILES - 1 else drop(lefts[t][var, tile(0)], -1)
                lefts[t + 1][var, tile(m)] = (
                    c0 * x + (up * turn(x, REST) + um * turn(x, -REST)) + (vp * before + vm * after)
                )


def adjoint_lats(terms, write):
    stay0, down0, up0 = terms(0)
    last, up_last, first = None, None, None
    pending, rising = stay0, up0
    for m in range(1, TILES):
        stay, down, up = terms(m)
        done = pending + down
        if m == 1:
            first = done
        else:
            write(m - 1, done)
        pending, rising = stay + rising, up
    write(TILES - 1, pending + drop(down0, -1))
    write(0, first + drop(rising, 1))


def adjoint_sweep(main_c, left_c, grads, ys, lefts):
    for t in reversed(range(NT)):
        src, dst, low, high = ys[t + 1], ys[t], t + 1, 10 - t
        for var in (0, 1):
            for l in range(SLAB):
                g = grads[10 * t + 2 * l + var]
                own = var * EXT + SLAB + l
                src[own] = g if t == NT - 1 else src[own] + g
            g = grads[10 * t + 8 + var]
            lefts[t + 1][var] = g if t == NT - 1 else lefts[t + 1][var] + g
            for e in (low - 1, high + 1):
                src[var * EXT + e] = jnp.zeros((ROWS, 128), F32)

        first_plane = 2 * (1 + BASE[t] - low)

        def longitude(e, carry, src=src, dst=dst, first=first_plane):
            k = first + 2 * e
            both = [{}, {}]

            def shared(m):
                if m not in both[0]:
                    from_east = jnp.maximum(main_c[k + 2, tile(m)], 0.0)
                    from_west = jnp.maximum(-main_c[k - 2, tile(m)], 0.0)
                    both[0][m] = (*factors(main_c[k, tile(m)], main_c[k + 1, tile(m)]), from_east, from_west)
                return both[0][m]

            state = [None, None]
            for m in range(TILES):
                c0, _, _, vp, vm, from_east, from_west = shared(m)
                for var in (0, 1):
                    p = var * EXT + e
                    y = src[p, tile(m)]
                    stay = c0 * y + (from_east * src[p + 1, tile(m)] + from_west * src[p - 1, tile(m)])
                    down, up = vp * y, vm * y
                    if m == 0:
                        state[var] = (down, None, stay, up)
                        continue
                    down0, first, pending, rising = state[var]
                    done = pending + down
                    if m == 1:
                        first = done
                    else:
                        dst[p, tile(m - 1)] = done
                    state[var] = (down0, first, stay + rising, up)
            for var in (0, 1):
                down0, first, pending, rising = state[var]
                dst[var * EXT + e, tile(TILES - 1)] = pending + drop(down0, -1)
                dst[var * EXT + e, tile(0)] = first + drop(rising, 1)
            return carry

        lax.fori_loop(low, high + 1, longitude, 0)
        for m in range(TILES):
            west = jnp.maximum(main_c[first_plane + 2 * low, tile(m)], 0.0)
            east = jnp.maximum(-main_c[first_plane + 2 * high, tile(m)], 0.0)
            for var in (0, 1):
                dst[var * EXT + low - 1, tile(m)] = west * src[var * EXT + low, tile(m)]
                dst[var * EXT + high + 1, tile(m)] = east * src[var * EXT + high, tile(m)]
        for var in (0, 1):

            def terms(m, var=var, t=t):
                c0, up, um, vp, vm = factors(left_c[2 * t, tile(m)], left_c[2 * t + 1, tile(m)])
                y = lefts[t + 1][var, tile(m)]
                return c0 * y + (turn(up * y, -REST) + turn(um * y, REST)), vp * y, vm * y

            def write(m, x, var=var, t=t):
                lefts[t][var, tile(m)] = x

            adjoint_lats(terms, write)


def adjoint_outputs(odd, y, left, out_own, out_near, out_far):
    for var in (0, 1):
        for l in range(SLAB):
            k, p = 2 * l + var, var * EXT + l
            west, east = y[p], y[p + 2 * SLAB]
            out_own[k] = y[p + SLAB]
            out_near[k] = jnp.where(odd, west, east)
            out_far[k] = jnp.where(odd, east, west)
        out_own[2 * SLAB + var] = left[var]
    lane = lanes((ROWS, 128))
    west = jnp.where(lane < SHARE, left[0], turn(left[1], SHARE))
    east = jnp.where(lane < SHARE, turn(left[0], -2 * SHARE), turn(left[1], -SHARE))
    out_near[2 * SLAB] = jnp.where(odd, west, east)
    out_far[2 * SLAB] = jnp.where(odd, east, west)


def with_rim(x, m, rim, plane):
    if m < 8:
        return jnp.where(depths() == 0, rim[plane, pl.ds(m, 1)], x)
    if m > 8:
        return jnp.where(depths() == 7, rim[plane, pl.ds(m - 1, 1)], x)
    return x


def inside(m):
    return depths() != (0 if m < 4 else 7 if m >= TILES - 4 else -1)


def halves(x):
    big = x.astype(BF16)
    return big, (x - big.astype(F32)).astype(BF16)


def dot(a, b, across=False):
    dims = (((1,), (1 if across else 0,)), ((), ()))
    return lax.dot_general(a, b, dims, preferred_element_type=F32)


def split_dot(a, b_big, b_small, across=False):
    a_big, a_small = halves(a)
    return dot(a_big, b_big, across) + (dot(a_small, b_big, across) + dot(a_big, b_small, across))


def spread(values, table, others, grads, t):
    main = split_dot(values, *table, True)
    rest = split_dot(jnp.concatenate([values[l * ROWS : (l + 1) * ROWS] for l in range(SLAB)], 1), *others, True)
    for var in (0, 1):
        for l in range(SLAB):
            grads[10 * t + 2 * l + var] = main[l * ROWS : (l + 1) * ROWS, 128 * var : 128 * (var + 1)]
        grads[10 * t + 8 + var] = rest[:, 128 * var : 128 * (var + 1)]


def observe(x, left, table, others):
    rows = [jnp.concatenate([x[SLAB + l], x[EXT + SLAB + l]], 1) for l in range(SLAB)]
    main = split_dot(jnp.concatenate(rows, 0), *table)
    rest = split_dot(jnp.concatenate([left[0], left[1]], 1), *others)
    return main + jnp.concatenate([rest[:, 128 * l : 128 * (l + 1)] for l in range(SLAB)], 0)


def message_kernel(flags, given_weight, given, sent, error_weight, innovations, message, done):
    copies = [
        pltpu.make_async_copy(source, target, done.at[i])
        for i, (source, target) in enumerate(((given_weight, error_weight), (given, innovations)))
    ]
    for copy in copies:
        copy.start()
    for copy in copies:
        copy.wait()
    owners = error_weight.shape[0] // (NT * SLOTS)
    for t in range(NT):
        for c in range(SLOTS):
            here = pl.ds((t * owners) * SLOTS + c, owners, stride=SLOTS)
            weight = error_weight[here]
            message[pl.ds(t * SLOTS + c, owners, stride=2 * NT * SLOTS)] = weight * innovations[here]
            message[pl.ds((NT + t) * SLOTS + c, owners, stride=2 * NT * SLOTS)] = weight
    send = pltpu.make_async_copy(message, sent, done.at[2])
    send.start()
    send.wait()


def prepare_kernel(flags, courant, weighting, own, own_left, to_near, to_far, edges, table, others, lay, mine, packed):
    depth = courant.shape[0] // (2 * NT * SLAB)
    main = depth - REST
    odd = flags[0] == 1
    lay[...] = jnp.zeros(lay.shape, F32)
    mine[...] = jnp.zeros(mine.shape, F32)
    packed[...] = jnp.zeros(packed.shape, F32)

    def place(x, target, plane, edge):
        if edge is not None:
            edges[edge, pl.ds(0, 4)] = x[:4]
            edges[edge, pl.ds(4, 4)] = x[BAND - 4 :]
        lay[pl.ds(4, BAND)] = x
        for m in range(TILES):
            target[plane, tile(m)] = lay[pl.ds(m, 8, stride=TILES)]

    for k in (0, 1):
        for t in range(NT):
            for l in range(SLAB):
                start = (2 * t + k) * depth * SLAB + l
                x = courant[pl.ds(start, main, stride=SLAB)]
                place(x.T, own, 8 * t + 4 * k + l, 2 * (4 * t + l) + k if t < NT - 1 else None)
                x = courant[pl.ds(start + main * SLAB, REST, stride=SLAB)]
                mine[pl.ds((SLAB + l) * REST, REST)] = x
                if t < NT - 1:
                    packed[pl.ds(t * SHARE + l * REST, REST)] = x
            place(mine[...].T, own_left, 2 * t + k, None)
            for d in range(1, NT - t):
                west, east = own[8 * t + 4 * k + d - 1], own[8 * t + 4 * k + SLAB - d]
                to_near[2 * PLANES[t, d] + k] = jnp.where(odd, west, east)
                to_far[2 * PLANES[t, d] + k] = jnp.where(odd, east, west)
        place(packed[...].T, to_near, 12 + k, 24 + k)
        to_far[12 + k] = to_near[12 + k]
    others[...] = jnp.zeros(others.shape, F32)
    for var in (0, 1):
        table[pl.ds(128 * var, main)] = weighting[pl.ds(depth * var, main)]
        rest = weighting[pl.ds(depth * var + main, REST)]
        for l in range(SLAB):
            others[pl.ds(128 * var + (SLAB + l) * REST, REST), pl.ds(128 * l, 128)] = rest


def halo_kernel(flags, south, north, halo):
    row = lax.broadcasted_iota(jnp.int32, south.shape[1:], 0)
    for k in range(south.shape[0]):
        below = jnp.where(flags[1] > 0, drop(south[k], 4), 0.0)
        above = jnp.where(flags[1] < flags[2] - 1, drop(north[k], 4), 0.0)
        halo[k] = jnp.where(row < 4, below, above)


def complete(flags, mine, south, north, k):
    has_south, has_north = flags[1] > 0, flags[1] < flags[2] - 1
    low = jnp.where(has_south, south[k, pl.ds(8, 8)], 0.0) + mine[k, pl.ds(0, 8)]
    high = jnp.where(has_north, north[k, pl.ds(0, 8)], 0.0) + mine[k, pl.ds(8, 8)]
    row = depths()
    return (
        jnp.where(row < 4, jnp.where(has_south, low, 0.0), low),
        jnp.where(row < 4, high, jnp.where(has_north, high, 0.0)),
    )


def edge_kernel(flags, mine, south, north, edge):
    for k in range(edge.shape[0]):
        low, high = complete(flags, mine, south, north, k)
        edge[k, pl.ds(0, 8)] = low
        edge[k, pl.ds(8, 8)] = high


def slots_kernel(flags, sent, index, counts, table, others, weights, grads):
    table, others = halves(table[...]), halves(others[...])
    owners = counts.shape[1]
    shape = (SLAB, TILES, 8, owners)
    l, m, s = (lax.broadcasted_iota(jnp.int32, shape, axis) for axis in range(3))
    latitude = TILES * s + m - 4
    cell = jnp.where((latitude >= 0) & (latitude < BAND), l * BAND + latitude, -2).reshape(SLAB * ROWS, owners)
    for t in range(NT):
        hits, bigs, smalls = [], [], []
        for c in range(SLOTS):
            slot = jnp.where(c < counts[pl.ds(t, 1), :], index[t, pl.ds(c, 1), :], -1)
            hits.append(jnp.where(cell == slot, 1.0, 0.0).astype(BF16))
            both = [sent[pl.ds((i * NT + t) * SLOTS + c, owners, stride=2 * NT * SLOTS)] for i in (0, 1)]
            big, small = halves(jnp.concatenate(both, 1))
            bigs.append(big)
            smalls.append(small)
        hit = jnp.concatenate(hits, 1)
        total = dot(hit, jnp.concatenate(bigs, 0)) + dot(hit, jnp.concatenate(smalls, 0))
        weights[t] = total[:, 128:]
        spread(total[:, :128], table, others, grads, t)


def right_side_kernel(flags, grads, own, own_left, packed, near, far, halo, halo_near, halo_far, *rest):
    out_own, out_near, out_far, main_c, left_c, whole, *scratch = rest
    odd = flags[0] == 1
    lane, row = lanes(), depths()

    def tiles(target, plane, tile_of, halo_of):
        for m in range(TILES):
            x = tile_of(m)
            if halo_of is not None and m < 4:
                x = jnp.where(row == 0, halo_of(m), x)
            if halo_of is not None and m >= TILES - 4:
                x = jnp.where(row == 7, halo_of(m - (TILES - 8)), x)
            target[plane, tile(m)] = x

    for k in (0, 1):
        main_c[k] = jnp.zeros((ROWS, 128), F32)
        main_c[58 + k] = jnp.zeros((ROWS, 128), F32)
        for t in range(NT):
            for e in range(t + 1, 11 - t):
                plane = 2 * (1 + BASE[t] + e - t - 1) + k
                strip = 2 * (4 * t + e % SLAB) + k
                if SLAB <= e < 2 * SLAB:
                    source = 8 * t + 4 * k + e - SLAB
                    tiles(
                        main_c, plane, lambda m, p=source: own[p, tile(m)],
                        (lambda i, p=strip: halo[p, pl.ds(i, 1)]) if t < NT - 1 else None,
                    )
                    continue
                source = 2 * PLANES[t, SLAB - e if e < SLAB else e - 2 * SLAB + 1] + k
                a, b, ha, hb = (near, far, halo_near, halo_far) if e < SLAB else (far, near, halo_far, halo_near)
                tiles(
                    main_c, plane,
                    lambda m, p=source, a=a, b=b: jnp.where(odd, a[p, tile(m)], b[p, tile(m)]),
                    lambda i, p=strip, a=ha, b=hb: jnp.where(odd, a[p, pl.ds(i, 1)], b[p, pl.ds(i, 1)]),
                )
        tiles(whole, 0, lambda m: packed[k, tile(m)], lambda i: halo[24 + k, pl.ds(i, 1)])
        for part, (a, b, ha, hb) in ((1, (near, far, halo_near, halo_far)), (2, (far, near, halo_far, halo_near))):
            tiles(
                whole, part,
                lambda m, a=a, b=b: jnp.where(odd, a[12 + k, tile(m)], b[12 + k, tile(m)]),
                lambda i, a=ha, b=hb: jnp.where(odd, a[24 + k, pl.ds(i, 1)], b[24 + k, pl.ds(i, 1)]),
            )
        for t in range(NT):
            for m in range(TILES):
                if t == NT - 1:
                    left_c[2 * t + k, tile(m)] = own_left[2 * t + k, tile(m)]
                    continue
                mid, west, east = (whole[i, tile(m)] for i in range(3))
                x = jnp.where(lane < SHARE, turn(west, -SHARE * t), turn(mid, SHARE - SHARE * t))
                x = jnp.where(lane < 2 * SHARE, x, turn(east, 2 * SHARE - SHARE * t))
                left_c[2 * t + k, tile(m)] = jnp.where(lane < 3 * SHARE, x, 0.0)
    ys, lefts = scratch[: NT + 1], scratch[NT + 1 :]
    adjoint_sweep(main_c, left_c, grads, ys, lefts)
    adjoint_outputs(odd, ys[0], lefts[0], out_own, out_near, out_far)


def hessian_kernel(flags, own, near, far, e_own, e_near, e_far, weights, table, others, moments, main_c, left_c, *rest):
    out_own, out_near, out_far, out_field, out_moments, grads, *scratch = rest
    xs, lefts = scratch[: NT + 1], scratch[NT + 1 :]
    odd = flags[0] == 1
    lane = lanes()
    square = jnp.zeros((8, 128), F32)
    for m in range(TILES):
        for k in range(2 * SLAB + 1):
            a = with_rim(own[k, tile(m)], m, e_own, k)
            b = with_rim(near[k, tile(m)], m, e_near, k)
            c = with_rim(far[k, tile(m)], m, e_far, k)
            west, east = jnp.where(odd, b, c), jnp.where(odd, c, b)
            out_field[k, tile(m)] = a
            counted = inside(m)
            if k < 2 * SLAB:
                p = (k % 2) * EXT + k // 2
                for i, x in enumerate((west, a, east)):
                    xs[0][p + SLAB * i, tile(m)] = x
            else:
                counted = counted & (lane >= SHARE) & (lane < 3 * SHARE)
                for var in (0, 1):
                    x = jnp.where(lane < SHARE, turn(west, -SHARE * (1 + var)), turn(a, -SHARE * var))
                    x = jnp.where(lane < 2 * SHARE, x, turn(east, SHARE - SHARE * var))
                    lefts[0][var, tile(m)] = jnp.where(lane < 3 * SHARE, x, 0.0)
            square = square + jnp.where(counted, a * a, 0.0)
    forward_sweep(main_c, left_c, xs, lefts)
    table, others = halves(table[...]), halves(others[...])
    product = jnp.zeros((8, 128), F32)
    for t in range(NT):
        seen = observe(xs[t + 1], lefts[t + 1], table, others)
        weighed = weights[t] * seen
        product = product + jnp.sum((weighed * seen).reshape(-1, 8, 128), axis=0)
        spread(weighed, table, others, grads, t)
    lane = lanes(out_moments.shape)
    before = moments[pl.ds(0, 1), :]
    found = jnp.where(lane == 2, jnp.sum(square), jnp.where(lane == 3, jnp.sum(product), 0.0))
    out_moments[...] = jnp.where(lane < 2, turn(jnp.broadcast_to(before, lane.shape), -2), found)
    adjoint_sweep(main_c, left_c, grads, xs, lefts)
    adjoint_outputs(odd, xs[0], lefts[0], out_own, out_near, out_far)


def gather_kernel(flags, own, near, far, *rest):
    main, rim = rest[-2:]
    lane = lanes()
    for k in range(2 * SLAB + 1):
        for m in range(TILES):
            if k < 2 * SLAB:
                x = own[k, tile(m)] + (near[k, tile(m)] + far[k, tile(m)])
            else:
                more = near[k, tile(m)] + far[k, tile(m)]
                first = own[k, tile(m)] + turn(more, SHARE)
                second = own[k + 1, tile(m)] + more
                x = jnp.where(lane < 2 * SHARE, first, turn(second, SHARE))
                x = jnp.where((lane >= SHARE) & (lane < 3 * SHARE), x, 0.0)
            main[k, tile(m)] = x
        for m in range(8):
            rim[k, pl.ds(m, 1)] = main[k, pl.ds(8 * m, 1)]
            rim[k, pl.ds(m + 8, 1)] = main[k, pl.ds(8 * (m + 9) + 7, 1)]


def final_kernel(flags, v0, v1, main, mine, south, north, sums, solution, residual, edge, lay_s, lay_r):
    total = jnp.sum(sums[...], axis=0, keepdims=True)
    lane = lanes(total.shape)
    m = [jnp.sum(jnp.where(lane == k, total, 0.0), axis=1, keepdims=True) for k in range(4)]
    a, c, d = m[1] / m[0], m[2] / m[0], m[3] / m[0]
    step0 = 1.0 / (1.0 + a)
    keep = a * step0
    ratio = (c - a * a) * step0 * step0
    p, s = keep + ratio, -step0
    curvature = p * p + 2.0 * p * s * a + s * s * c + (p * p * a + 2.0 * p * s * c + s * s * d)
    step1 = ratio / curvature
    for_s = (step0 + step1 * p, step1 * s)
    for_r = (keep - step1 * p, s - step1 * (p + s), -(step1 * s))
    depth = solution.shape[0] // (2 * SLAB)
    edge_kernel(flags, mine, south, north, edge)
    for k in range(2 * SLAB + 1):
        for m in range(TILES):
            x0, x1 = v0[k, tile(m)], v1[k, tile(m)]
            x2 = with_rim(main[k, tile(m)], m, edge, k)
            lay_s[pl.ds(m, 8, stride=TILES)] = for_s[0] * x0 + for_s[1] * x1
            lay_r[pl.ds(m, 8, stride=TILES)] = for_r[0] * x0 + for_r[1] * x1 + for_r[2] * x2
        for lay, out in ((lay_s, solution), (lay_r, residual)):
            x = lay[pl.ds(4, BAND)].T
            if k < 2 * SLAB:
                out[pl.ds((k % 2) * depth * SLAB + k // 2, 128, stride=SLAB)] = x
                continue
            for var in (0, 1):
                for l in range(SLAB):
                    row = SHARE * (1 + var) + REST * l
                    out[pl.ds((var * depth + 128) * SLAB + l, REST, stride=SLAB)] = x[row : row + REST]


def shift(x, axis, by):
    n = lax.axis_size(axis)
    return lax.ppermute(x, axis, [(i, (i + by) % n) for i in range(n)])


def far_swap(x):
    n = lax.axis_size("lon")
    return lax.ppermute(x, "lon", [(i, (i + 1 if i % 2 else i - 1) % n) for i in range(n)])


def near_swap(x):
    return lax.ppermute(x, "lon", [(i, i ^ 1) for i in range(lax.axis_size("lon"))])


def body(courant, slot_column_cells, column_counts, innovations, error_weight, weighting):
    depth = courant.shape[2]
    owners = slot_column_cells.shape[2]
    channels = weighting.shape[1]
    flags = jnp.stack([lax.axis_index("lon") % 2, lax.axis_index("lat"), jnp.int32(lax.axis_size("lat"))]).astype(jnp.int32)
    slots = owners * SLOTS

    (message,) = call(
        message_kernel,
        [(2 * NT * slots, channels)],
        [flags, error_weight.reshape(NT * slots, channels), innovations.reshape(NT * slots, channels)],
        [
            pltpu.VMEM((NT * slots, channels), F32), pltpu.VMEM((NT * slots, channels), F32),
            pltpu.VMEM((2 * NT * slots, channels), F32), pltpu.SemaphoreType.DMA((3,)),
        ],
        hbm_in=(1, 2),
        hbm_out=(0,),
    )
    sent = lax.all_to_all(
        message.reshape(owners, 2 * NT * SLOTS, channels), ("lon", "lat"), split_axis=0, concat_axis=0, tiled=True
    ).reshape(2 * NT * slots, channels)
    own, own_left, to_near, to_far, edges, table, others = call(
        prepare_kernel,
        [
            (2 * NT * SLAB, ROWS, 128), (2 * NT, ROWS, 128), (14, ROWS, 128), (14, ROWS, 128), (26, 8, 128),
            (256, channels), (256, SLAB * channels),
        ],
        [flags, courant.reshape(2 * NT * depth * SLAB, BAND), weighting],
        [pltpu.VMEM((ROWS, 128), F32), pltpu.VMEM((128, 128), F32), pltpu.VMEM((128, 128), F32)],
    )
    c_far, c_near = far_swap(to_far), near_swap(to_near)
    (halo,) = call(halo_kernel, [(26, 8, 128)], [flags, shift(edges, "lat", 1), shift(edges, "lat", -1)])
    index = jnp.swapaxes(slot_column_cells[:, 0], 1, 2)

    parcel = (2 * SLAB + 1, ROWS, 128)
    rim = (2 * SLAB + 1, 16, 128)
    pieces = [(2 * SLAB + 2, ROWS, 128), parcel, parcel]
    steps = [pltpu.VMEM((2 * EXT, ROWS, 128), F32)] * (NT + 1) + [pltpu.VMEM((2, ROWS, 128), F32)] * (NT + 1)

    def gathered(parts, *more):
        mine, to_near, to_far = parts
        return call(gather_kernel, [parcel, rim], [flags, mine, near_swap(to_near), far_swap(to_far), *more])

    def hessian(state, moments, rows):
        main, mine = state
        (edge,) = call(edge_kernel, [rim], [flags, mine, shift(mine, "lat", 1), shift(mine, "lat", -1)])
        return call(
            hessian_kernel,
            [*pieces, parcel, (rows, 128)],
            [
                flags, main, near_swap(main), far_swap(main), edge, near_swap(edge), far_swap(edge),
                weights, table, others, moments, main_c, left_c,
            ],
            [pltpu.VMEM((10 * NT, ROWS, 128), F32), *steps],
        )

    weights, right = call(
        slots_kernel,
        [(NT, SLAB * ROWS, channels), (10 * NT, ROWS, 128)],
        [flags, sent, index, column_counts[:, 0], table, others],
    )
    *parts, main_c, left_c = call(
        right_side_kernel,
        [*pieces, (60, ROWS, 128), (2 * NT, ROWS, 128)],
        [flags, right, own, own_left, to_near[12:], c_near, c_far, halo, near_swap(halo), far_swap(halo)],
        [pltpu.VMEM((3, ROWS, 128), F32), *steps],
    )
    *parts, v0, moments = hessian(gathered(parts), jnp.zeros((8, 128), F32), 8)
    *parts, v1, moments = hessian(gathered(parts), moments, owners)
    sums = lax.all_to_all(moments, ("lon", "lat"), split_axis=0, concat_axis=0, tiled=True)
    main, mine = gathered(parts, sums)
    solution, residual = call(
        final_kernel,
        [(2 * depth * SLAB, BAND)] * 2,
        [flags, v0, v1, main, mine, shift(mine, "lat", 1), shift(mine, "lat", -1), sums],
        [pltpu.VMEM(rim, F32), pltpu.VMEM((ROWS, 128), F32), pltpu.VMEM((ROWS, 128), F32)],
    )
    shape = (2, depth, SLAB, BAND)
    return solution.reshape(shape), residual.reshape(shape)


def solution(mesh):
    in_specs = (
        P(None, None, None, "lon", "lat"),
        P(None, ("lon", "lat"), None, None),
        P(None, ("lon", "lat"), None),
        P(None, ("lon", "lat"), None, None, None),
        P(None, ("lon", "lat"), None, None, None),
        P(),
    )
    out_specs = (P(None, None, "lon", "lat"), P(None, None, "lon", "lat"))
    return jax.shard_map(body, mesh=mesh, in_specs=in_specs, out_specs=out_specs, check_vma=False)
```

time: 1240 us -> 173 us (0.14)
  local copies, waits for them, and re-layouts: 331 us -> 10.6 us
  starting transfers between devices: 364 us -> 52.1 us
  other arithmetic: 211 us -> 0.08 us
  blocking collectives: 204 us -> 18.1 us
  Pallas kernels: 0 us -> 41.5 us
  matrix products: 31.1 us -> 0 us
  waiting for transfers between devices: 79.2 us -> 48.8 us
    psum x3 -> x0, blocking collectives: 204 us -> none  [the longest x2 133 us: squared_norm(): return lax.psum(jnp.sum(residual * residual), ('lon', 'lat'))]
    all_to_all x20 -> x1, starting transfers between devices: 173 us -> 11.5 us  [body(): lax.all_to_all(message.reshape(owners, 2 * NT * SLOTS, channels), ('lon',...]
    ppermute x84 -> x26, starting transfers between devices: 190 us -> 40.6 us  [the longest x9 26.6 us: near_swap(): lax.ppermute(x, 'lon', [(i, i ^ 1) for i in range(lax.axis_size('lon'))])]
    slice x89 -> x1, local copies, waits for them, and re-layouts: 105 us -> 0.92 us  [body(): to_near[12:]]
    all_to_all x20 -> x1, waiting for transfers between devices: 73.9 us -> 0.01 us  [body(): lax.all_to_all(message.reshape(owners, 2 * NT * SLOTS, channels), ('lon',...]
    reshape x49 -> x0, local copies, waits for them, and re-layouts: 72.3 us -> none  [the longest x12 26.5 us: deposit(): masked.reshape(owner_devices * slot_capacity, column_depth)]
    ppermute x42 -> x0, local copies, waits for them, and re-layouts: 64.9 us -> none  [the longest x21 32.8 us: padded(): lax.ppermute(head, axis, [((i + 1) % count, i) for i in range(ends)])]
    scatter-add x12 -> x0, other arithmetic: 53.9 us -> none  [deposit(): flattened.at[:, slot_lookup[time_moment]]]
  transfers between devices with their start and end apart: 104 -> 27, of which waited for: 12 -> 11; matrix products, arithmetic and copies ran while one was open for 38% -> 1% of each run, Pallas kernels for 0% -> 5%
where the time goes in v3:
time: 173 us; the launch traced here: 172 us
  starting transfers between devices  52.1 us (30%)
  waiting for transfers between devices  48.8 us (28%)
  Pallas kernels  41.5 us (24%)
  blocking collectives  18.1 us (10%)
  local copies, waits for them, and re-layouts  10.6 us (6%)
    pallas_call x13, Pallas kernels, call(): pl.pallas_call(kernel, out_shape=[jax.ShapeDtypeStruct(s, F32) for s in s...  41.5 us
    ppermute x9, starting transfers between devices, near_swap(): lax.ppermute(x, 'lon', [(i, i ^ 1) for i in range(lax.axis_size('lon'))])  26.6 us
    ppermute x9, waiting for transfers between devices, far_swap(): lax.ppermute(x, 'lon', [(i, (i + 1 if i % 2 else i - 1) % n) for i in ran...  22.7 us
    ppermute x8, waiting for transfers between devices, shift(): return lax.ppermute(x, axis, [(i, (i + by) % n) for i in range(n)])  21.9 us
    all_to_all x1, blocking collectives, body(): lax.all_to_all(moments, ('lon', 'lat'), split_axis=0, concat_axis=0, tile...  18.1 us
    all_to_all x1, starting transfers between devices, body(): lax.all_to_all(message.reshape(owners, 2 * NT * SLOTS, channels), ('lon',...  11.5 us
    ppermute x8, starting transfers between devices, shift(): return lax.ppermute(x, axis, [(i, (i + by) % n) for i in range(n)])  11.1 us
    unnamed x26, local copies, waits for them, and re-layouts  9.68 us
  transfers between devices with their start and end apart: 27, of which 11 were waited for; matrix products, arithmetic and copies ran while one was open for 1% of the time, Pallas kernels for 5%

profile of v3, /device:TPU:1, one launch (start us, length us, event | category | flops | bytes accessed | tf_op | source)
XLA Modules:
  0.0 172.0 jit_solution(5758891733391844937)
XLA Ops:
  0.7 1.2 copy-done.4
  1.9 1.2 copy-done.5
  3.2 2.6 %shard_map.77 = f32[4096,128]{1,0:T(8,128)S(1)} custom-call(s32[3]{0:T(128)S(1)} %pad_add_fusion.flags, f32[2048,128]{1,0:T(8,128)S(1)} %bitcast.20, f32[2048,128]{1,0:T(8,128)S(1)} %bitcast.21), custom_call_target="tpu_custom_call" | custom-call | bytes 2097164 | tf_op jit(solution)/shard_map/pallas_call | solution.py:30
  5.8 1.4 copy-done
  7.2 11.5 %all-to-all-start = ((f32[128,32,128]{2,1,0:T(8,128)}), f32[128,32,128]{2,1,0:T(8,128)S(1)}, u32[]{:S(2)}, u32[]{:S(2)}) async-start(f32[128,32,128]{2,1,0:T(8,128)} %bitcast.18), calls=%async_computation | async-start | bytes 4194304 | tf_op jit(solution)/shard_map/all_to_all | solution.py:542
  18.7 1.6 copy-done.1
  20.3 2.9 %shard_map.78 = (f32[32,136,128]{2,1,0:T(8,128)S(1)}, f32[8,136,128]{2,1,0:T(8,128)S(1)}, f32[14,136,128]{2,1,0:T(8,128)}, f32[14,136,128]{2,1,0:T(8,128)}, f32[...) custom-call(s32[3]{0:T(128)S(1)} %pad_add_fusion.flags, f32[4384,128]{1,0:T(8,128)S(1)} %bitcast.19, ...), custom_call_target="tpu_custom_call" | custom-call | bytes 2384908 | tf_op jit(solution)/shard_map/pallas_call | solution.py:30
  23.2 1.4 copy-done.2
  24.6 1.1 collective-permute-start
  25.7 0.7 collective-permute-start.1
  26.4 1.2 collective-permute-start.2
  27.6 1.5 collective-permute-start.3
  29.0 16.6 %collective-permute-done.2.south = f32[26,8,128]{2,1,0:T(8,128)S(1)} collective-permute-done((f32[26,8,128]{2,1,0:T(8,128)S(1)}, f32[26,8,128]{2,1,0:T(8,128)S(1)}, u32[]{:S(2)}, u32[]{:S(2)}) %collective-permute-start.2) | collective-permute-done | bytes 106528 | tf_op jit(solution)/shard_map/ppermute | solution.py:512
  46.9 1.3 collective-permute-start.4
  48.2 1.4 collective-permute-start.5
  49.5 0.9 slice.3.packed
  50.5 0.8 copy-done.9
  51.3 0.7 copy-done.11
  52.7 4.7 %shard_map.79 = (f32[4,544,128]{2,1,0:T(8,128)S(1)}, f32[40,136,128]{2,1,0:T(8,128)S(1)}) custom-call(s32[3]{0:T(128)S(1)} %copy-done.9, f32[4096,128]{1,0:T(8,128)S(1)} %bitcast.17, s32[4,4,128]{2,1,0:T(4,128)S(1)} %bitcast.25, s32[4,128]{1,0:T(4,128)S(1)} %bitcast.26, f32[256,128]{1,0:T(8,128)S(1)} %get-tuple-element.34.table, ...), custom_call_target="tpu_custom_call" | custom-call | bytes 2762764 | tf_op jit(solution)/shard_map/pallas_call | solution.py:30
  57.5 5.3 %shard_map.81 = (f32[10,136,128]{2,1,0:T(8,128)S(1)}, f32[9,136,128]{2,1,0:T(8,128)S(1)}, f32[9,136,128]{2,1,0:T(8,128)S(1)}, f32[60,136,128]{2,1,0:T(8,128)S(1)}, f32[8,136,128]{2,1,0:T(8,128)S(1)}) custom-call(s32[3]{0:T(128)S(1)} %copy-done.9, f32[40,136,128]{2,1,0:T(8,128)S(1)} %get-tuple-element.36.grads, f32[32,136,128]{2,1,0:T(8,128)S(1)} %copy-done.3, ...), custom_call_target="tpu_custom_call" | custom-call | bytes 7979020 | tf_op jit(solution)/shard_map/pallas_call | solution.py:30
  62.8 4.7 %collective-permute-start.6 = (f32[9,136,128]{2,1,0:T(8,128)S(1)}, f32[9,136,128]{2,1,0:T(8,128)S(1)}, u32[]{:S(2)}, u32[]{:S(2)}) collective-permute-start(f32[9,136,128]{2,1,0:T(8,128)S(1)} %get-tuple-element.43), channel_id=1, source_target_pairs={{0,4},{4,0},{8,12},{12,8},{16,20},{20,16},{24,28},{28,24},{32,36},... | collective-permute-start | bytes 1880072 | tf_op jit(solution)/shard_map/ppermute | solution.py:521
  67.5 1.7 collective-permute-done.6.near
  69.1 8.3 %collective-permute-done.7.far = f32[9,136,128]{2,1,0:T(8,128)S(1)} collective-permute-done((f32[9,136,128]{2,1,0:T(8,128)S(1)}, f32[9,136,128]{2,1,0:T(8,128)S(1)}, u32[]{:S(2)}, u32[]{:S(2)}) %collective-permute-start.7) | collective-permute-done | bytes 626720 | tf_op jit(solution)/shard_map/ppermute | solution.py:517
  77.5 0.7 shard_map.82
  78.2 3.2 %collective-permute-start.8 = (f32[9,136,128]{2,1,0:T(8,128)S(1)}, f32[9,136,128]{2,1,0:T(8,128)S(1)}, u32[]{:S(2)}, u32[]{:S(2)}) collective-permute-start(f32[9,136,128]{2,1,0:T(8,128)S(1)} %get-tuple-element.45.own), channel_id=1, source_target_pairs={{0,4},{4,0},{8,12},{12,8},{16,20},{20,16},{24,28},{28,24},{32,36},... | collective-permute-start | bytes 1880072 | tf_op jit(solution)/shard_map/ppermute | solution.py:521
  81.4 2.7 %collective-permute-start.11 = (f32[9,16,128]{2,1,0:T(8,128)S(1)}, f32[9,16,128]{2,1,0:T(8,128)S(1)}, u32[]{:S(2)}, u32[]{:S(2)}) collective-permute-start(f32[9,16,128]{2,1,0:T(8,128)S(1)} %get-tuple-element.46.mine), channel_id=1, source_target_pairs={{0,3},{1,0},{2,1},{3,2},{4,7},{5,4},{6,5},{7,6},{8,11},{9,8},{10,9... | collective-permute-start | bytes 221192 | tf_op jit(solution)/shard_map/ppermute | solution.py:512
  84.1 1.7 %collective-permute-done.10.south = f32[9,16,128]{2,1,0:T(8,128)S(1)} collective-permute-done((f32[9,16,128]{2,1,0:T(8,128)S(1)}, f32[9,16,128]{2,1,0:T(8,128)S(1)}, u32[]{:S(2)}, u32[]{:S(2)}) %collective-permute-start.10) | collective-permute-done | bytes 73760 | tf_op jit(solution)/shard_map/ppermute | solution.py:512
  86.4 2.2 %collective-permute-start.12 = (f32[9,16,128]{2,1,0:T(8,128)S(1)}, f32[9,16,128]{2,1,0:T(8,128)S(1)}, u32[]{:S(2)}, u32[]{:S(2)}) collective-permute-start(f32[9,16,128]{2,1,0:T(8,128)S(1)} %shard_map.83.e_own), channel_id=1, source_target_pairs={{0,4},{4,0},{8,12},{12,8},{16,20},{20,16},{24,28},{28,24},{32,36},... | collective-permute-start | bytes 221192 | tf_op jit(solution)/shard_map/ppermute | solution.py:521
  88.6 0.9 collective-permute-start.13
  89.5 3.2 %collective-permute-done.13.e_far = f32[9,16,128]{2,1,0:T(8,128)S(1)} collective-permute-done((f32[9,16,128]{2,1,0:T(8,128)S(1)}, f32[9,16,128]{2,1,0:T(8,128)S(1)}, u32[]{:S(2)}, u32[]{:S(2)}) %collective-permute-start.13) | collective-permute-done | bytes 73760 | tf_op jit(solution)/shard_map/ppermute | solution.py:517
  92.7 9.8 %shard_map.84 = (f32[10,136,128]{2,1,0:T(8,128)S(1)}, f32[9,136,128]{2,1,0:T(8,128)S(1)}, f32[9,136,128]{2,1,0:T(8,128)S(1)}, f32[9,136,128]{2,1,0:T(8,128)S(1)}, f32[8,128]{1,0:T(8,128)S(1)}) custom-call(s32[3]{0:T(128)S(1)} %copy-done.10, f32[9,136,128]{2,1,0:T(8,128)S(1)} %get-tuple-element.45.own, f32[9,136,128]{2,1,0:T(8,128)S(1)} %collective-permute-done.8.near, ...), custom_call_target="tpu_custom_call" | custom-call | bytes 8609804 | tf_op jit(solution)/shard_map/pallas_call | solution.py:30
  102.5 3.2 %collective-permute-start.14 = (f32[9,136,128]{2,1,0:T(8,128)S(1)}, f32[9,136,128]{2,1,0:T(8,128)S(1)}, u32[]{:S(2)}, u32[]{:S(2)}) collective-permute-start(f32[9,136,128]{2,1,0:T(8,128)S(1)} %get-tuple-element.52), channel_id=1, source_target_pairs={{0,4},{4,0},{8,12},{12,8},{16,20},{20,16},{24,28},{28,24},{32,36},... | collective-permute-start | bytes 1880072 | tf_op jit(solution)/shard_map/ppermute | solution.py:521
  105.7 1.7 collective-permute-done.14.near
  107.4 8.3 %collective-permute-done.15.far = f32[9,136,128]{2,1,0:T(8,128)S(1)} collective-permute-done((f32[9,136,128]{2,1,0:T(8,128)S(1)}, f32[9,136,128]{2,1,0:T(8,128)S(1)}, u32[]{:S(2)}, u32[]{:S(2)}) %collective-permute-start.15) | collective-permute-done | bytes 626720 | tf_op jit(solution)/shard_map/ppermute | solution.py:517
  115.7 0.8 shard_map.85
  116.4 3.2 %collective-permute-start.16 = (f32[9,136,128]{2,1,0:T(8,128)S(1)}, f32[9,136,128]{2,1,0:T(8,128)S(1)}, u32[]{:S(2)}, u32[]{:S(2)}) collective-permute-start(f32[9,136,128]{2,1,0:T(8,128)S(1)} %get-tuple-element.54.own), channel_id=1, source_target_pairs={{0,4},{4,0},{8,12},{12,8},{16,20},{20,16},{24,28},{28,24},{32,36},... | collective-permute-start | bytes 1880072 | tf_op jit(solution)/shard_map/ppermute | solution.py:521
  119.6 3.0 %collective-permute-start.19 = (f32[9,16,128]{2,1,0:T(8,128)S(1)}, f32[9,16,128]{2,1,0:T(8,128)S(1)}, u32[]{:S(2)}, u32[]{:S(2)}) collective-permute-start(f32[9,16,128]{2,1,0:T(8,128)S(1)} %get-tuple-element.55.mine), channel_id=1, source_target_pairs={{0,3},{1,0},{2,1},{3,2},{4,7},{5,4},{6,5},{7,6},{8,11},{9,8},{10,9... | collective-permute-start | bytes 221192 | tf_op jit(solution)/shard_map/ppermute | solution.py:512
  122.6 1.7 %collective-permute-done.18.south = f32[9,16,128]{2,1,0:T(8,128)S(1)} collective-permute-done((f32[9,16,128]{2,1,0:T(8,128)S(1)}, f32[9,16,128]{2,1,0:T(8,128)S(1)}, u32[]{:S(2)}, u32[]{:S(2)}) %collective-permute-start.18) | collective-permute-done | bytes 73760 | tf_op jit(solution)/shard_map/ppermute | solution.py:512
  124.9 4.1 %collective-permute-start.20 = (f32[9,16,128]{2,1,0:T(8,128)S(1)}, f32[9,16,128]{2,1,0:T(8,128)S(1)}, u32[]{:S(2)}, u32[]{:S(2)}) collective-permute-start(f32[9,16,128]{2,1,0:T(8,128)S(1)} %shard_map.86.e_own), channel_id=1, source_target_pairs={{0,4},{4,0},{8,12},{12,8},{16,20},{20,16},{24,28},{28,24},{32,36},... | collective-permute-start | bytes 221192 | tf_op jit(solution)/shard_map/ppermute | solution.py:521
  129.0 0.9 collective-permute-done.20.e_near
  129.9 2.9 %collective-permute-done.21.e_far = f32[9,16,128]{2,1,0:T(8,128)S(1)} collective-permute-done((f32[9,16,128]{2,1,0:T(8,128)S(1)}, f32[9,16,128]{2,1,0:T(8,128)S(1)}, u32[]{:S(2)}, u32[]{:S(2)}) %collective-permute-start.21) | collective-permute-done | bytes 73760 | tf_op jit(solution)/shard_map/ppermute | solution.py:517
  132.8 9.8 %shard_map.87 = (f32[10,136,128]{2,1,0:T(8,128)S(1)}, f32[9,136,128]{2,1,0:T(8,128)S(1)}, f32[9,136,128]{2,1,0:T(8,128)S(1)}, f32[9,136,128]{2,1,0:T(8,128)S(1)}, f32[128,128]{1,0:T(8,128)S(1)}) custom-call(s32[3]{0:T(128)S(1)} %copy-done.10, f32[9,136,128]{2,1,0:T(8,128)S(1)} %get-tuple-element.54.own, f32[9,136,128]{2,1,0:T(8,128)S(1)} %collective-permute-done.16.near, ...), custom_call_target="tpu_custom_call" | custom-call | bytes 8609804 | tf_op jit(solution)/shard_map/pallas_call | solution.py:30
  142.6 3.7 %collective-permute-start.22 = (f32[9,136,128]{2,1,0:T(8,128)S(1)}, f32[9,136,128]{2,1,0:T(8,128)S(1)}, u32[]{:S(2)}, u32[]{:S(2)}) collective-permute-start(f32[9,136,128]{2,1,0:T(8,128)S(1)} %get-tuple-element.59), channel_id=1, source_target_pairs={{0,4},{4,0},{8,12},{12,8},{16,20},{20,16},{24,28},{28,24},{32,36},... | collective-permute-start | bytes 1880072 | tf_op jit(solution)/shard_map/ppermute | solution.py:521
  146.3 18.1 %all_to_all.16 = f32[128,1,128]{2,1,0:T(1,128)S(1)} all-to-all(f32[128,1,128]{2,1,0:T(1,128)S(1)} %bitcast.24), channel_id=1, replica_groups=mesh['lon'=32,'lat'=4] {'lon','lat'}, dimensions={0} | all-to-all | bytes 131072 | tf_op jit(solution)/shard_map/all_to_all | solution.py:593
  164.4 0.7 shard_map.88
  165.6 2.3 %collective-permute-start.25 = (f32[9,16,128]{2,1,0:T(8,128)S(1)}, f32[9,16,128]{2,1,0:T(8,128)S(1)}, u32[]{:S(2)}, u32[]{:S(2)}) collective-permute-start(f32[9,16,128]{2,1,0:T(8,128)S(1)} %get-tuple-element.63.mine), channel_id=1, source_target_pairs={{0,3},{1,0},{2,1},{3,2},{4,7},{5,4},{6,5},{7,6},{8,11},{9,8},{10,9... | collective-permute-start | bytes 221192 | tf_op jit(solution)/shard_map/ppermute | solution.py:512
  167.9 1.7 %collective-permute-done.24.south = f32[9,16,128]{2,1,0:T(8,128)S(1)} collective-permute-done((f32[9,16,128]{2,1,0:T(8,128)S(1)}, f32[9,16,128]{2,1,0:T(8,128)S(1)}, u32[]{:S(2)}, u32[]{:S(2)}) %collective-permute-start.24) | collective-permute-done | bytes 73760 | tf_op jit(solution)/shard_map/ppermute | solution.py:512
  169.6 2.4 %shard_map.89 = (f32[1096,128]{1,0:T(8,128)}, f32[1096,128]{1,0:T(8,128)}) custom-call(s32[3]{0:T(128)S(1)} %copy-done.10, f32[9,136,128]{2,1,0:T(8,128)S(1)} %get-tuple-element.50.v0, f32[9,136,128]{2,1,0:T(8,128)S(1)} %get-tuple-element.57.v1, f32[9,136,128]{2,1,0:T(8,128)S(1)} %get-tuple-element.62.main, f32[9,16,128]{2,1,0:T(8,128)S(1)} %get-tuple-element.63.mine, ...), custom_call_target="tpu_custom_call" | custom-call | bytes 2166796 | tf_op jit(solution)/shard_map/pallas_call | solution.py:30
  (49 shorter events, 3.6 us)
Async XLA Ops:
  0.7 17.9 %copy-start.7 = (s32[3]{0:T(128)}, s32[3]{0:T(128)S(1)}, u32[]{:S(2)}) copy-start(s32[3]{0:T(128)S(1)} %pad_add_fusion.flags) | copy-start | bytes 40
  0.7 1.2 copy-start.4
  1.9 1.2 copy-start.5
  5.8 1.4 copy-start
  7.2 11.5 %copy-start.6 = (f32[274,128]{1,0:T(8,128)S(1)}, f32[274,128]{1,0:T(8,128)}, u32[]{:S(2)}) copy-start(f32[274,128]{1,0:T(8,128)} %weighting.1) | copy-start | bytes 420868
  7.2 43.3 %all-to-all-start = ((f32[128,32,128]{2,1,0:T(8,128)}), f32[128,32,128]{2,1,0:T(8,128)S(1)}, u32[]{:S(2)}, u32[]{:S(2)}) async-start(f32[128,32,128]{2,1,0:T(8,128)} %bitcast.18), calls=%async_computation | async-start | bytes 4194304 | tf_op jit(solution)/shard_map/all_to_all | solution.py:542
  18.7 1.6 copy-start.1
  23.2 1.4 copy-start.2
  24.6 32.8 %collective-permute-start = (f32[14,136,128]{2,1,0:T(8,128)}, f32[14,136,128]{2,1,0:T(8,128)}, u32[]{:S(2)}, u32[]{:S(2)}) collective-permute-start(f32[14,136,128]{2,1,0:T(8,128)} %get-tuple-element.39), channel_id=1, source_target_pairs={{0,4},{4,0},{8,12},{12,8},{16,20},{20,16},{24,28},{28,24},{32,36},... | collective-permute-start | bytes 2924552 | tf_op jit(solution)/shard_map/ppermute | solution.py:521
  25.7 31.8 %collective-permute-start.1 = (f32[14,136,128]{2,1,0:T(8,128)}, f32[14,136,128]{2,1,0:T(8,128)}, u32[]{:S(2)}, u32[]{:S(2)}) collective-permute-start(f32[14,136,128]{2,1,0:T(8,128)} %get-tuple-element.40), channel_id=1, source_target_pairs={{0,124},{4,8},{8,4},{12,16},{16,12},{20,24},{24,20},{28,32},{32,28... | collective-permute-start | bytes 2924552 | tf_op jit(solution)/shard_map/ppermute | solution.py:517
  26.4 19.3 %collective-permute-start.2 = (f32[26,8,128]{2,1,0:T(8,128)S(1)}, f32[26,8,128]{2,1,0:T(8,128)S(1)}, u32[]{:S(2)}, u32[]{:S(2)}) collective-permute-start(f32[26,8,128]{2,1,0:T(8,128)S(1)} %get-tuple-element.41), channel_id=1, source_target_pairs={{0,1},{1,2},{2,3},{3,0},{4,5},{5,6},{6,7},{7,4},{8,9},{9,10},{10,1... | collective-permute-start | bytes 319496 | tf_op jit(solution)/shard_map/ppermute | solution.py:512
  27.6 18.1 %collective-permute-start.3 = (f32[26,8,128]{2,1,0:T(8,128)S(1)}, f32[26,8,128]{2,1,0:T(8,128)S(1)}, u32[]{:S(2)}, u32[]{:S(2)}) collective-permute-start(f32[26,8,128]{2,1,0:T(8,128)S(1)} %get-tuple-element.41), channel_id=1, source_target_pairs={{0,3},{1,0},{2,1},{3,2},{4,7},{5,4},{6,5},{7,6},{8,11},{9,8},{10,9... | collective-permute-start | bytes 319496 | tf_op jit(solution)/shard_map/ppermute | solution.py:512
  45.7 0.7 copy-start.8
  46.9 10.5 %collective-permute-start.4 = (f32[26,8,128]{2,1,0:T(8,128)S(1)}, f32[26,8,128]{2,1,0:T(8,128)}, u32[]{:S(2)}, u32[]{:S(2)}) collective-permute-start(f32[26,8,128]{2,1,0:T(8,128)S(1)} %shard_map.80.halo), channel_id=1, source_target_pairs={{0,4},{4,0},{8,12},{12,8},{16,20},{20,16},{24,28},{28,24},{32,36},... | collective-permute-start | bytes 319496 | tf_op jit(solution)/shard_map/ppermute | solution.py:521
  48.2 9.2 %collective-permute-start.5 = (f32[26,8,128]{2,1,0:T(8,128)S(1)}, f32[26,8,128]{2,1,0:T(8,128)}, u32[]{:S(2)}, u32[]{:S(2)}) collective-permute-start(f32[26,8,128]{2,1,0:T(8,128)S(1)} %shard_map.80.halo), channel_id=1, source_target_pairs={{0,124},{4,8},{8,4},{12,16},{16,12},{20,24},{24,20},{28,32},{32,28... | collective-permute-start | bytes 319496 | tf_op jit(solution)/shard_map/ppermute | solution.py:517
  50.5 7.0 %copy-start.3 = (f32[32,136,128]{2,1,0:T(8,128)S(1)}, f32[32,136,128]{2,1,0:T(8,128)}, u32[]{:S(2)}) copy-start(f32[32,136,128]{2,1,0:T(8,128)} %copy-done.2) | copy-start | bytes 6684676
  50.5 0.8 copy-start.9
  51.3 0.7 copy-start.11
  52.0 0.7 copy-start.12
  57.5 20.0 %copy-start.10 = (s32[3]{0:T(128)S(1)}, s32[3]{0:T(128)}, u32[]{:S(2)}) copy-start(s32[3]{0:T(128)} %copy-done.7) | copy-start | bytes 40
  62.8 6.3 %collective-permute-start.6 = (f32[9,136,128]{2,1,0:T(8,128)S(1)}, f32[9,136,128]{2,1,0:T(8,128)S(1)}, u32[]{:S(2)}, u32[]{:S(2)}) collective-permute-start(f32[9,136,128]{2,1,0:T(8,128)S(1)} %get-tuple-element.43), channel_id=1, source_target_pairs={{0,4},{4,0},{8,12},{12,8},{16,20},{20,16},{24,28},{28,24},{32,36},... | collective-permute-start | bytes 1880072 | tf_op jit(solution)/shard_map/ppermute | solution.py:521
  67.5 10.0 %collective-permute-start.7 = (f32[9,136,128]{2,1,0:T(8,128)S(1)}, f32[9,136,128]{2,1,0:T(8,128)S(1)}, u32[]{:S(2)}, u32[]{:S(2)}) collective-permute-start(f32[9,136,128]{2,1,0:T(8,128)S(1)} %get-tuple-element.44), channel_id=1, source_target_pairs={{0,124},{4,8},{8,4},{12,16},{16,12},{20,24},{24,20},{28,32},{32,28... | collective-permute-start | bytes 1880072 | tf_op jit(solution)/shard_map/ppermute | solution.py:517
  78.2 14.4 %collective-permute-start.8 = (f32[9,136,128]{2,1,0:T(8,128)S(1)}, f32[9,136,128]{2,1,0:T(8,128)S(1)}, u32[]{:S(2)}, u32[]{:S(2)}) collective-permute-start(f32[9,136,128]{2,1,0:T(8,128)S(1)} %get-tuple-element.45.own), channel_id=1, source_target_pairs={{0,4},{4,0},{8,12},{12,8},{16,20},{20,16},{24,28},{28,24},{32,36},... | collective-permute-start | bytes 1880072 | tf_op jit(solution)/shard_map/ppermute | solution.py:521
  81.4 11.2 %collective-permute-start.9 = (f32[9,136,128]{2,1,0:T(8,128)S(1)}, f32[9,136,128]{2,1,0:T(8,128)S(1)}, u32[]{:S(2)}, u32[]{:S(2)}) collective-permute-start(f32[9,136,128]{2,1,0:T(8,128)S(1)} %get-tuple-element.45.own), channel_id=1, source_target_pairs={{0,124},{4,8},{8,4},{12,16},{16,12},{20,24},{24,20},{28,32},{32,28... | collective-permute-start | bytes 1880072 | tf_op jit(solution)/shard_map/ppermute | solution.py:517
  81.4 4.4 %collective-permute-start.10 = (f32[9,16,128]{2,1,0:T(8,128)S(1)}, f32[9,16,128]{2,1,0:T(8,128)S(1)}, u32[]{:S(2)}, u32[]{:S(2)}) collective-permute-start(f32[9,16,128]{2,1,0:T(8,128)S(1)} %get-tuple-element.46.mine), channel_id=1, source_target_pairs={{0,1},{1,2},{2,3},{3,0},{4,5},{5,6},{6,7},{7,4},{8,9},{9,10},{10,1... | collective-permute-start | bytes 221192 | tf_op jit(solution)/shard_map/ppermute | solution.py:512
  81.4 4.4 %collective-permute-start.11 = (f32[9,16,128]{2,1,0:T(8,128)S(1)}, f32[9,16,128]{2,1,0:T(8,128)S(1)}, u32[]{:S(2)}, u32[]{:S(2)}) collective-permute-start(f32[9,16,128]{2,1,0:T(8,128)S(1)} %get-tuple-element.46.mine), channel_id=1, source_target_pairs={{0,3},{1,0},{2,1},{3,2},{4,7},{5,4},{6,5},{7,6},{8,11},{9,8},{10,9... | collective-permute-start | bytes 221192 | tf_op jit(solution)/shard_map/ppermute | solution.py:512
  86.4 3.1 %collective-permute-start.12 = (f32[9,16,128]{2,1,0:T(8,128)S(1)}, f32[9,16,128]{2,1,0:T(8,128)S(1)}, u32[]{:S(2)}, u32[]{:S(2)}) collective-permute-start(f32[9,16,128]{2,1,0:T(8,128)S(1)} %shard_map.83.e_own), channel_id=1, source_target_pairs={{0,4},{4,0},{8,12},{12,8},{16,20},{20,16},{24,28},{28,24},{32,36},... | collective-permute-start | bytes 221192 | tf_op jit(solution)/shard_map/ppermute | solution.py:521
  88.6 4.1 %collective-permute-start.13 = (f32[9,16,128]{2,1,0:T(8,128)S(1)}, f32[9,16,128]{2,1,0:T(8,128)S(1)}, u32[]{:S(2)}, u32[]{:S(2)}) collective-permute-start(f32[9,16,128]{2,1,0:T(8,128)S(1)} %shard_map.83.e_own), channel_id=1, source_target_pairs={{0,124},{4,8},{8,4},{12,16},{16,12},{20,24},{24,20},{28,32},{32,28... | collective-permute-start | bytes 221192 | tf_op jit(solution)/shard_map/ppermute | solution.py:517
  102.5 4.9 %collective-permute-start.14 = (f32[9,136,128]{2,1,0:T(8,128)S(1)}, f32[9,136,128]{2,1,0:T(8,128)S(1)}, u32[]{:S(2)}, u32[]{:S(2)}) collective-permute-start(f32[9,136,128]{2,1,0:T(8,128)S(1)} %get-tuple-element.52), channel_id=1, source_target_pairs={{0,4},{4,0},{8,12},{12,8},{16,20},{20,16},{24,28},{28,24},{32,36},... | collective-permute-start | bytes 1880072 | tf_op jit(solution)/shard_map/ppermute | solution.py:521
  105.7 10.0 %collective-permute-start.15 = (f32[9,136,128]{2,1,0:T(8,128)S(1)}, f32[9,136,128]{2,1,0:T(8,128)S(1)}, u32[]{:S(2)}, u32[]{:S(2)}) collective-permute-start(f32[9,136,128]{2,1,0:T(8,128)S(1)} %get-tuple-element.53), channel_id=1, source_target_pairs={{0,124},{4,8},{8,4},{12,16},{16,12},{20,24},{24,20},{28,32},{32,28... | collective-permute-start | bytes 1880072 | tf_op jit(solution)/shard_map/ppermute | solution.py:517
  116.4 16.3 %collective-permute-start.16 = (f32[9,136,128]{2,1,0:T(8,128)S(1)}, f32[9,136,128]{2,1,0:T(8,128)S(1)}, u32[]{:S(2)}, u32[]{:S(2)}) collective-permute-start(f32[9,136,128]{2,1,0:T(8,128)S(1)} %get-tuple-element.54.own), channel_id=1, source_target_pairs={{0,4},{4,0},{8,12},{12,8},{16,20},{20,16},{24,28},{28,24},{32,36},... | collective-permute-start | bytes 1880072 | tf_op jit(solution)/shard_map/ppermute | solution.py:521
  119.6 13.1 %collective-permute-start.17 = (f32[9,136,128]{2,1,0:T(8,128)S(1)}, f32[9,136,128]{2,1,0:T(8,128)S(1)}, u32[]{:S(2)}, u32[]{:S(2)}) collective-permute-start(f32[9,136,128]{2,1,0:T(8,128)S(1)} %get-tuple-element.54.own), channel_id=1, source_target_pairs={{0,124},{4,8},{8,4},{12,16},{16,12},{20,24},{24,20},{28,32},{32,28... | collective-permute-start | bytes 1880072 | tf_op jit(solution)/shard_map/ppermute | solution.py:517
  119.6 4.7 %collective-permute-start.18 = (f32[9,16,128]{2,1,0:T(8,128)S(1)}, f32[9,16,128]{2,1,0:T(8,128)S(1)}, u32[]{:S(2)}, u32[]{:S(2)}) collective-permute-start(f32[9,16,128]{2,1,0:T(8,128)S(1)} %get-tuple-element.55.mine), channel_id=1, source_target_pairs={{0,1},{1,2},{2,3},{3,0},{4,5},{5,6},{6,7},{7,4},{8,9},{9,10},{10,1... | collective-permute-start | bytes 221192 | tf_op jit(solution)/shard_map/ppermute | solution.py:512
  119.6 4.7 %collective-permute-start.19 = (f32[9,16,128]{2,1,0:T(8,128)S(1)}, f32[9,16,128]{2,1,0:T(8,128)S(1)}, u32[]{:S(2)}, u32[]{:S(2)}) collective-permute-start(f32[9,16,128]{2,1,0:T(8,128)S(1)} %get-tuple-element.55.mine), channel_id=1, source_target_pairs={{0,3},{1,0},{2,1},{3,2},{4,7},{5,4},{6,5},{7,6},{8,11},{9,8},{10,9... | collective-permute-start | bytes 221192 | tf_op jit(solution)/shard_map/ppermute | solution.py:512
  124.9 5.0 %collective-permute-start.20 = (f32[9,16,128]{2,1,0:T(8,128)S(1)}, f32[9,16,128]{2,1,0:T(8,128)S(1)}, u32[]{:S(2)}, u32[]{:S(2)}) collective-permute-start(f32[9,16,128]{2,1,0:T(8,128)S(1)} %shard_map.86.e_own), channel_id=1, source_target_pairs={{0,4},{4,0},{8,12},{12,8},{16,20},{20,16},{24,28},{28,24},{32,36},... | collective-permute-start | bytes 221192 | tf_op jit(solution)/shard_map/ppermute | solution.py:521
  129.0 3.8 %collective-permute-start.21 = (f32[9,16,128]{2,1,0:T(8,128)S(1)}, f32[9,16,128]{2,1,0:T(8,128)S(1)}, u32[]{:S(2)}, u32[]{:S(2)}) collective-permute-start(f32[9,16,128]{2,1,0:T(8,128)S(1)} %shard_map.86.e_own), channel_id=1, source_target_pairs={{0,124},{4,8},{8,4},{12,16},{16,12},{20,24},{24,20},{28,32},{32,28... | collective-permute-start | bytes 221192 | tf_op jit(solution)/shard_map/ppermute | solution.py:517
  142.6 21.8 %collective-permute-start.22 = (f32[9,136,128]{2,1,0:T(8,128)S(1)}, f32[9,136,128]{2,1,0:T(8,128)S(1)}, u32[]{:S(2)}, u32[]{:S(2)}) collective-permute-start(f32[9,136,128]{2,1,0:T(8,128)S(1)} %get-tuple-element.59), channel_id=1, source_target_pairs={{0,4},{4,0},{8,12},{12,8},{16,20},{20,16},{24,28},{28,24},{32,36},... | collective-permute-start | bytes 1880072 | tf_op jit(solution)/shard_map/ppermute | solution.py:521
  146.3 18.1 %collective-permute-start.23 = (f32[9,136,128]{2,1,0:T(8,128)S(1)}, f32[9,136,128]{2,1,0:T(8,128)S(1)}, u32[]{:S(2)}, u32[]{:S(2)}) collective-permute-start(f32[9,136,128]{2,1,0:T(8,128)S(1)} %get-tuple-element.60), channel_id=1, source_target_pairs={{0,124},{4,8},{8,4},{12,16},{16,12},{20,24},{24,20},{28,32},{32,28... | collective-permute-start | bytes 1880072 | tf_op jit(solution)/shard_map/ppermute | solution.py:517
  165.2 4.5 %collective-permute-start.24 = (f32[9,16,128]{2,1,0:T(8,128)S(1)}, f32[9,16,128]{2,1,0:T(8,128)S(1)}, u32[]{:S(2)}, u32[]{:S(2)}) collective-permute-start(f32[9,16,128]{2,1,0:T(8,128)S(1)} %get-tuple-element.63.mine), channel_id=1, source_target_pairs={{0,1},{1,2},{2,3},{3,0},{4,5},{5,6},{6,7},{7,4},{8,9},{9,10},{10,1... | collective-permute-start | bytes 221192 | tf_op jit(solution)/shard_map/ppermute | solution.py:512
  165.6 4.1 %collective-permute-start.25 = (f32[9,16,128]{2,1,0:T(8,128)S(1)}, f32[9,16,128]{2,1,0:T(8,128)S(1)}, u32[]{:S(2)}, u32[]{:S(2)}) collective-permute-start(f32[9,16,128]{2,1,0:T(8,128)S(1)} %get-tuple-element.63.mine), channel_id=1, source_target_pairs={{0,3},{1,0},{2,1},{3,2},{4,7},{5,4},{6,5},{7,6},{8,11},{9,8},{10,9... | collective-permute-start | bytes 221192 | tf_op jit(solution)/shard_map/ppermute | solution.py:512

commit v4 on v3

--- a/solution.py
+++ b/solution.py
@@ -21,17 +21,15 @@
 BASE = (0, 10, 18, 24)
 PLANES = {(0, 1): 0, (0, 2): 1, (0, 3): 2, (1, 1): 3, (1, 2): 4, (2, 1): 5}
 VMEM = pl.BlockSpec(memory_space=pltpu.VMEM)
-HBM = pl.BlockSpec(memory_space=pltpu.HBM)
-SMEM = pl.BlockSpec(memory_space=pltpu.SMEM)
-
-
-def call(kernel, shapes, inputs, scratch=(), flops=0, hbm_in=(), hbm_out=()):
+
+
+def call(kernel, shapes, inputs, scratch=(), flops=0):
     nbytes = sum(x.size * x.dtype.itemsize for x in inputs)
     return pl.pallas_call(
         kernel,
         out_shape=[jax.ShapeDtypeStruct(s, F32) for s in shapes],
-        in_specs=[SMEM] + [HBM if i in hbm_in else VMEM for i in range(1, len(inputs))],
-        out_specs=[HBM if i in hbm_out else VMEM for i in range(len(shapes))],
+        in_specs=[VMEM] * len(inputs),
+        out_specs=[VMEM] * len(shapes),
         scratch_shapes=list(scratch),
         compiler_params=pltpu.CompilerParams(vmem_limit_bytes=32 << 20),
         cost_estimate=pl.CostEstimate(flops=flops, bytes_accessed=nbytes, transcendentals=0),
@@ -41,6 +39,15 @@
 def turn(x, shift):
     shift %= 128
     return pltpu.roll(x, shift, 1) if shift else x
+
+
+def is_odd():
+    return lax.rem(lax.axis_index("lon"), 2) == 1
+
+
+def has_bands():
+    band = lax.axis_index("lat")
+    return band > 0, band < lax.axis_size("lat") - 1
 
 
 def drop(x, by):
@@ -249,31 +256,11 @@
     return main + jnp.concatenate([rest[:, 128 * l : 128 * (l + 1)] for l in range(SLAB)], 0)
 
 
-def message_kernel(flags, given_weight, given, sent, error_weight, innovations, message, done):
-    copies = [
-        pltpu.make_async_copy(source, target, done.at[i])
-        for i, (source, target) in enumerate(((given_weight, error_weight), (given, innovations)))
-    ]
-    for copy in copies:
-        copy.start()
-    for copy in copies:
-        copy.wait()
-    owners = error_weight.shape[0] // (NT * SLOTS)
-    for t in range(NT):
-        for c in range(SLOTS):
-            here = pl.ds((t * owners) * SLOTS + c, owners, stride=SLOTS)
-            weight = error_weight[here]
-            message[pl.ds(t * SLOTS + c, owners, stride=2 * NT * SLOTS)] = weight * innovations[here]
-            message[pl.ds((NT + t) * SLOTS + c, owners, stride=2 * NT * SLOTS)] = weight
-    send = pltpu.make_async_copy(message, sent, done.at[2])
-    send.start()
-    send.wait()
-
-
-def prepare_kernel(flags, courant, weighting, own, own_left, to_near, to_far, edges, table, others, lay, mine, packed):
+def prepare_kernel(courant, weighting, own, own_left, out_packed, to_near, to_far, edges, table, others, *scratch):
+    lay, mine, packed = scratch
     depth = courant.shape[0] // (2 * NT * SLAB)
     main = depth - REST
-    odd = flags[0] == 1
+    odd = is_odd()
     lay[...] = jnp.zeros(lay.shape, F32)
     mine[...] = jnp.zeros(mine.shape, F32)
     packed[...] = jnp.zeros(packed.shape, F32)
@@ -301,8 +288,9 @@
                 west, east = own[8 * t + 4 * k + d - 1], own[8 * t + 4 * k + SLAB - d]
                 to_near[2 * PLANES[t, d] + k] = jnp.where(odd, west, east)
                 to_far[2 * PLANES[t, d] + k] = jnp.where(odd, east, west)
-        place(packed[...].T, to_near, 12 + k, 24 + k)
-        to_far[12 + k] = to_near[12 + k]
+        place(packed[...].T, out_packed, k, 24 + k)
+        to_near[12 + k] = out_packed[k]
+        to_far[12 + k] = out_packed[k]
     others[...] = jnp.zeros(others.shape, F32)
     for var in (0, 1):
         table[pl.ds(128 * var, main)] = weighting[pl.ds(depth * var, main)]
@@ -311,16 +299,17 @@
             others[pl.ds(128 * var + (SLAB + l) * REST, REST), pl.ds(128 * l, 128)] = rest
 
 
-def halo_kernel(flags, south, north, halo):
-    row = lax.broadcasted_iota(jnp.int32, south.shape[1:], 0)
+def halo_kernel(south, north, halo):
+    row = depths()
+    has_south, has_north = has_bands()
     for k in range(south.shape[0]):
-        below = jnp.where(flags[1] > 0, drop(south[k], 4), 0.0)
-        above = jnp.where(flags[1] < flags[2] - 1, drop(north[k], 4), 0.0)
+        below = jnp.where(has_south, drop(south[k], 4), 0.0)
+        above = jnp.where(has_north, drop(north[k], 4), 0.0)
         halo[k] = jnp.where(row < 4, below, above)
 
 
-def complete(flags, mine, south, north, k):
-    has_south, has_north = flags[1] > 0, flags[1] < flags[2] - 1
+def complete(mine, south, north, k):
+    has_south, has_north = has_bands()
     low = jnp.where(has_south, south[k, pl.ds(8, 8)], 0.0) + mine[k, pl.ds(0, 8)]
     high = jnp.where(has_north, north[k, pl.ds(0, 8)], 0.0) + mine[k, pl.ds(8, 8)]
     row = depths()
@@ -330,14 +319,14 @@
     )
 
 
-def edge_kernel(flags, mine, south, north, edge):
+def edge_kernel(mine, south, north, edge):
     for k in range(edge.shape[0]):
-        low, high = complete(flags, mine, south, north, k)
+        low, high = complete(mine, south, north, k)
         edge[k, pl.ds(0, 8)] = low
         edge[k, pl.ds(8, 8)] = high
 
 
-def slots_kernel(flags, sent, index, counts, table, others, weights, grads):
+def slots_kernel(sent, index, counts, table, others, weights, grads):
     table, others = halves(table[...]), halves(others[...])
     owners = counts.shape[1]
     shape = (SLAB, TILES, 8, owners)
@@ -359,9 +348,9 @@
         spread(total[:, :128], table, others, grads, t)
 
 
-def right_side_kernel(flags, grads, own, own_left, packed, near, far, halo, halo_near, halo_far, *rest):
+def right_side_kernel(grads, own, own_left, packed, near, far, halo, halo_near, halo_far, *rest):
     out_own, out_near, out_far, main_c, left_c, whole, *scratch = rest
-    odd = flags[0] == 1
+    odd = is_odd()
     lane, row = lanes(), depths()
 
     def tiles(target, plane, tile_of, halo_of):
@@ -415,10 +404,10 @@
     adjoint_outputs(odd, ys[0], lefts[0], out_own, out_near, out_far)
 
 
-def hessian_kernel(flags, own, near, far, e_own, e_near, e_far, weights, table, others, moments, main_c, left_c, *rest):
+def hessian_kernel(own, near, far, e_own, e_near, e_far, weights, table, others, moments, main_c, left_c, *rest):
     out_own, out_near, out_far, out_field, out_moments, grads, *scratch = rest
     xs, lefts = scratch[: NT + 1], scratch[NT + 1 :]
-    odd = flags[0] == 1
+    odd = is_odd()
     lane = lanes()
     square = jnp.zeros((8, 128), F32)
     for m in range(TILES):
@@ -456,7 +445,7 @@
     adjoint_outputs(odd, xs[0], lefts[0], out_own, out_near, out_far)
 
 
-def gather_kernel(flags, own, near, far, *rest):
+def gather_kernel(own, near, far, *rest):
     main, rim = rest[-2:]
     lane = lanes()
     for k in range(2 * SLAB + 1):
@@ -475,7 +464,7 @@
             rim[k, pl.ds(m + 8, 1)] = main[k, pl.ds(8 * (m + 9) + 7, 1)]
 
 
-def final_kernel(flags, v0, v1, main, mine, south, north, sums, solution, residual, edge, lay_s, lay_r):
+def final_kernel(v0, v1, main, mine, south, north, sums, solution, residual, edge, lay_s, lay_r):
     total = jnp.sum(sums[...], axis=0, keepdims=True)
     lane = lanes(total.shape)
     m = [jnp.sum(jnp.where(lane == k, total, 0.0), axis=1, keepdims=True) for k in range(4)]
@@ -489,7 +478,7 @@
     for_s = (step0 + step1 * p, step1 * s)
     for_r = (keep - step1 * p, s - step1 * (p + s), -(step1 * s))
     depth = solution.shape[0] // (2 * SLAB)
-    edge_kernel(flags, mine, south, north, edge)
+    edge_kernel(mine, south, north, edge)
     for k in range(2 * SLAB + 1):
         for m in range(TILES):
             x0, x1 = v0[k, tile(m)], v1[k, tile(m)]
@@ -525,34 +514,24 @@
     depth = courant.shape[2]
     owners = slot_column_cells.shape[2]
     channels = weighting.shape[1]
-    flags = jnp.stack([lax.axis_index("lon") % 2, lax.axis_index("lat"), jnp.int32(lax.axis_size("lat"))]).astype(jnp.int32)
     slots = owners * SLOTS
 
-    (message,) = call(
-        message_kernel,
-        [(2 * NT * slots, channels)],
-        [flags, error_weight.reshape(NT * slots, channels), innovations.reshape(NT * slots, channels)],
-        [
-            pltpu.VMEM((NT * slots, channels), F32), pltpu.VMEM((NT * slots, channels), F32),
-            pltpu.VMEM((2 * NT * slots, channels), F32), pltpu.SemaphoreType.DMA((3,)),
-        ],
-        hbm_in=(1, 2),
-        hbm_out=(0,),
-    )
+    weight = error_weight[:, 0]
+    message = jnp.swapaxes(jnp.concatenate([weight * innovations[:, 0], weight], 0), 0, 1)
     sent = lax.all_to_all(
         message.reshape(owners, 2 * NT * SLOTS, channels), ("lon", "lat"), split_axis=0, concat_axis=0, tiled=True
     ).reshape(2 * NT * slots, channels)
-    own, own_left, to_near, to_far, edges, table, others = call(
+    own, own_left, packed, to_near, to_far, edges, table, others = call(
         prepare_kernel,
         [
-            (2 * NT * SLAB, ROWS, 128), (2 * NT, ROWS, 128), (14, ROWS, 128), (14, ROWS, 128), (26, 8, 128),
+            (2 * NT * SLAB, ROWS, 128), (2 * NT, ROWS, 128), (2, ROWS, 128), (14, ROWS, 128), (14, ROWS, 128), (26, 8, 128),
             (256, channels), (256, SLAB * channels),
         ],
-        [flags, courant.reshape(2 * NT * depth * SLAB, BAND), weighting],
+        [courant.reshape(2 * NT * depth * SLAB, BAND), weighting],
         [pltpu.VMEM((ROWS, 128), F32), pltpu.VMEM((128, 128), F32), pltpu.VMEM((128, 128), F32)],
     )
     c_far, c_near = far_swap(to_far), near_swap(to_near)
-    (halo,) = call(halo_kernel, [(26, 8, 128)], [flags, shift(edges, "lat", 1), shift(edges, "lat", -1)])
+    (halo,) = call(halo_kernel, [(26, 8, 128)], [shift(edges, "lat", 1), shift(edges, "lat", -1)])
     index = jnp.swapaxes(slot_column_cells[:, 0], 1, 2)
 
     parcel = (2 * SLAB + 1, ROWS, 128)
@@ -562,16 +541,16 @@
 
     def gathered(parts, *more):
         mine, to_near, to_far = parts
-        return call(gather_kernel, [parcel, rim], [flags, mine, near_swap(to_near), far_swap(to_far), *more])
+        return call(gather_kernel, [parcel, rim], [mine, near_swap(to_near), far_swap(to_far), *more])
 
     def hessian(state, moments, rows):
         main, mine = state
-        (edge,) = call(edge_kernel, [rim], [flags, mine, shift(mine, "lat", 1), shift(mine, "lat", -1)])
+        (edge,) = call(edge_kernel, [rim], [mine, shift(mine, "lat", 1), shift(mine, "lat", -1)])
         return call(
             hessian_kernel,
             [*pieces, parcel, (rows, 128)],
             [
-                flags, main, near_swap(main), far_swap(main), edge, near_swap(edge), far_swap(edge),
+                main, near_swap(main), far_swap(main), edge, near_swap(edge), far_swap(edge),
                 weights, table, others, moments, main_c, left_c,
             ],
             [pltpu.VMEM((10 * NT, ROWS, 128), F32), *steps],
@@ -580,12 +559,12 @@
     weights, right = call(
         slots_kernel,
         [(NT, SLAB * ROWS, channels), (10 * NT, ROWS, 128)],
-        [flags, sent, index, column_counts[:, 0], table, others],
+        [sent, index, column_counts[:, 0], table, others],
     )
     *parts, main_c, left_c = call(
         right_side_kernel,
         [*pieces, (60, ROWS, 128), (2 * NT, ROWS, 128)],
-        [flags, right, own, own_left, to_near[12:], c_near, c_far, halo, near_swap(halo), far_swap(halo)],
+        [right, own, own_left, packed, c_near, c_far, halo, near_swap(halo), far_swap(halo)],
         [pltpu.VMEM((3, ROWS, 128), F32), *steps],
     )
     *parts, v0, moments = hessian(gathered(parts), jnp.zeros((8, 128), F32), 8)
@@ -595,7 +574,7 @@
     solution, residual = call(
         final_kernel,
         [(2 * depth * SLAB, BAND)] * 2,
-        [flags, v0, v1, main, mine, shift(mine, "lat", 1), shift(mine, "lat", -1), sums],
+        [v0, v1, main, mine, shift(mine, "lat", 1), shift(mine, "lat", -1), sums],
         [pltpu.VMEM(rim, F32), pltpu.VMEM((ROWS, 128), F32), pltpu.VMEM((ROWS, 128), F32)],
     )
     shape = (2, depth, SLAB, BAND)

time: 173 us -> 165 us (0.954)
  Pallas kernels: 41.5 us -> 33.1 us
  waiting for transfers between devices: 48.8 us -> 51.6 us
    pallas_call x13 -> x12, Pallas kernels: 41.5 us -> 33.1 us  [call(): pl.pallas_call(kernel, out_shape=[jax.ShapeDtypeStruct(s, F32) for s in s...]
    unnamed x26 -> x21, local copies, waits for them, and re-layouts: 9.68 us -> 6.39 us
    reshape x0 -> x1, local copies, waits for them, and re-layouts: none -> 2.58 us  [body(): message.reshape(owners, 2 * NT * SLOTS, channels)]
    all_to_all x1, waiting for transfers between devices: 0.01 us -> 2.1 us  [body(): lax.all_to_all(message.reshape(owners, 2 * NT * SLOTS, channels), ('lon',...]
  transfers between devices with their start and end apart: 27 -> 27, of which waited for: 11 -> 12; matrix products, arithmetic and copies ran while one was open for 1% -> 0% of each run, Pallas kernels for 5% -> 4%
where the time goes in v4:
time: 165 us; the launch traced here: 164 us
  waiting for transfers between devices  51.6 us (31%)
  starting transfers between devices  51 us (31%)
  Pallas kernels  33.1 us (20%)
  blocking collectives  18.1 us (11%)
  local copies, waits for them, and re-layouts  8.97 us (5%)
    pallas_call x12, Pallas kernels, call(): pl.pallas_call(kernel, out_shape=[jax.ShapeDtypeStruct(s, F32) for s in s...  33.1 us
    ppermute x9, starting transfers between devices, near_swap(): lax.ppermute(x, 'lon', [(i, i ^ 1) for i in range(lax.axis_size('lon'))])  25.5 us
    ppermute x9, waiting for transfers between devices, far_swap(): lax.ppermute(x, 'lon', [(i, (i + 1 if i % 2 else i - 1) % n) for i in ran...  22.9 us
    ppermute x8, waiting for transfers between devices, shift(): return lax.ppermute(x, axis, [(i, (i + by) % n) for i in range(n)])  22.3 us
    all_to_all x1, blocking collectives, body(): lax.all_to_all(moments, ('lon', 'lat'), split_axis=0, concat_axis=0, tile...  18.1 us
    all_to_all x1, starting transfers between devices, body(): lax.all_to_all(message.reshape(owners, 2 * NT * SLOTS, channels), ('lon',...  11.5 us
    ppermute x8, starting transfers between devices, shift(): return lax.ppermute(x, axis, [(i, (i + by) % n) for i in range(n)])  10.9 us
    unnamed x21, local copies, waits for them, and re-layouts  6.39 us
  transfers between devices with their start and end apart: 27, of which 12 were waited for; matrix products, arithmetic and copies ran while one was open for 0% of the time, Pallas kernels for 4%

profile of v4, /device:TPU:1, one launch (start us, length us, event | category | flops | bytes accessed | tf_op | source)
XLA Modules:
  0.0 164.0 jit_solution(11976805361319234826)
XLA Ops:
  0.6 1.5 copy.19
  2.2 0.3 copy-done.9
  2.6 0.2 pad_maximum_fusion
  2.9 2.6 %copy.13 = f32[128,32,128]{2,1,0:T(8,128)} copy(f32[128,32,128]{2,0,1:T(8,128)S(1)} %bitcast.29) | data formatting | bytes 4194304 | tf_op jit(solution)/shard_map/reshape | solution.py:522
  5.5 11.5 %all-to-all-start = ((f32[128,32,128]{2,1,0:T(8,128)}), f32[128,32,128]{2,1,0:T(8,128)S(1)}, u32[]{:S(2)}, u32[]{:S(2)}) async-start(f32[128,32,128]{2,1,0:T(8,128)} %copy.13), calls=%async_computation | async-start | bytes 4194304 | tf_op jit(solution)/shard_map/all_to_all | solution.py:521
  17.0 1.6 copy-done
  18.6 2.4 %shard_map.77 = (f32[32,136,128]{2,1,0:T(8,128)S(1)}, f32[8,136,128]{2,1,0:T(8,128)S(1)}, f32[2,136,128]{2,1,0:T(8,128)S(1)}, f32[14,136,128]{2,1,0:T(8,128)}, f...) custom-call(f32[4384,128]{1,0:T(8,128)S(1)} %bitcast.23, ...), custom_call_target="tpu_custom_call" | custom-call | bytes 2384896 | tf_op jit(solution)/shard_map/pallas_call | solution.py:28
  21.0 1.4 copy-done.1
  22.4 1.1 collective-permute-start
  23.5 0.7 collective-permute-start.1
  24.2 1.2 collective-permute-start.2
  25.4 1.5 collective-permute-start.3
  26.9 17.1 %collective-permute-done.2.south = f32[26,8,128]{2,1,0:T(8,128)S(1)} collective-permute-done((f32[26,8,128]{2,1,0:T(8,128)S(1)}, f32[26,8,128]{2,1,0:T(8,128)S(1)}, u32[]{:S(2)}, u32[]{:S(2)}) %collective-permute-start.2) | collective-permute-done | bytes 106528 | tf_op jit(solution)/shard_map/ppermute | solution.py:501
  44.0 1.3 collective-permute-start.4
  45.3 1.4 collective-permute-start.5
  46.6 2.1 %all-to-all-done = f32[128,32,128]{2,1,0:T(8,128)S(1)} async-done(((f32[128,32,128]{2,1,0:T(8,128)}), f32[128,32,128]{2,1,0:T(8,128)S(1)}, u32[]{:S(2)}, u32[]{:S(2)}) %all-to-all-start) | async-done | bytes 2097184 | tf_op jit(solution)/shard_map/all_to_all | solution.py:521
  48.7 0.8 copy-done.6
  49.6 0.7 copy-done.7
  50.3 4.2 %shard_map.78 = (f32[4,544,128]{2,1,0:T(8,128)S(1)}, f32[40,136,128]{2,1,0:T(8,128)S(1)}) custom-call(f32[4096,128]{1,0:T(8,128)S(1)} %bitcast.22, s32[4,4,128]{2,1,0:T(4,128)S(1)} %bitcast.27, s32[4,128]{1,0:T(4,128)S(1)} %bitcast.28, f32[256,128]{1,0:T(8,128)S(1)} %get-tuple-element.35.table, f32[256,512]{1,0:T(8,128)S(1)} %get-tuple-element.36.others), custom_call_target="tpu_custom_call" | custom-call | bytes 2762752 | tf_op jit(solution)/shard_map/pallas_call | solution.py:28
  54.5 5.3 %shard_map.80 = (f32[10,136,128]{2,1,0:T(8,128)S(1)}, f32[9,136,128]{2,1,0:T(8,128)S(1)}, f32[9,136,128]{2,1,0:T(8,128)S(1)}, f32[60,136,128]{2,1,0:T(8,128)S(1)}, f32[8,136,128]{2,1,0:T(8,128)S(1)}) custom-call(f32[40,136,128]{2,1,0:T(8,128)S(1)} %get-tuple-element.37.grads, f32[32,136,128]{2,1,0:T(8,128)S(1)} %copy-done.2, ...), custom_call_target="tpu_custom_call" | custom-call | bytes 7979008 | tf_op jit(solution)/shard_map/pallas_call | solution.py:28
  59.9 3.7 %collective-permute-start.6 = (f32[9,136,128]{2,1,0:T(8,128)S(1)}, f32[9,136,128]{2,1,0:T(8,128)S(1)}, u32[]{:S(2)}, u32[]{:S(2)}) collective-permute-start(f32[9,136,128]{2,1,0:T(8,128)S(1)} %get-tuple-element.45), channel_id=1, source_target_pairs={{0,4},{4,0},{8,12},{12,8},{16,20},{20,16},{24,28},{28,24},{32,36},... | collective-permute-start | bytes 1880072 | tf_op jit(solution)/shard_map/ppermute | solution.py:510
  63.6 1.7 %collective-permute-done.6.near = f32[9,136,128]{2,1,0:T(8,128)S(1)} collective-permute-done((f32[9,136,128]{2,1,0:T(8,128)S(1)}, f32[9,136,128]{2,1,0:T(8,128)S(1)}, u32[]{:S(2)}, u32[]{:S(2)}) %collective-permute-start.6) | collective-permute-done | bytes 626720 | tf_op jit(solution)/shard_map/ppermute | solution.py:510
  65.2 8.3 %collective-permute-done.7.far = f32[9,136,128]{2,1,0:T(8,128)S(1)} collective-permute-done((f32[9,136,128]{2,1,0:T(8,128)S(1)}, f32[9,136,128]{2,1,0:T(8,128)S(1)}, u32[]{:S(2)}, u32[]{:S(2)}) %collective-permute-start.7) | collective-permute-done | bytes 626720 | tf_op jit(solution)/shard_map/ppermute | solution.py:506
  73.7 3.2 %collective-permute-start.8 = (f32[9,136,128]{2,1,0:T(8,128)S(1)}, f32[9,136,128]{2,1,0:T(8,128)S(1)}, u32[]{:S(2)}, u32[]{:S(2)}) collective-permute-start(f32[9,136,128]{2,1,0:T(8,128)S(1)} %get-tuple-element.47.own), channel_id=1, source_target_pairs={{0,4},{4,0},{8,12},{12,8},{16,20},{20,16},{24,28},{28,24},{32,36},... | collective-permute-start | bytes 1880072 | tf_op jit(solution)/shard_map/ppermute | solution.py:510
  76.9 1.0 collective-permute-start.10
  78.0 1.7 %collective-permute-start.11 = (f32[9,16,128]{2,1,0:T(8,128)S(1)}, f32[9,16,128]{2,1,0:T(8,128)S(1)}, u32[]{:S(2)}, u32[]{:S(2)}) collective-permute-start(f32[9,16,128]{2,1,0:T(8,128)S(1)} %get-tuple-element.48.mine), channel_id=1, source_target_pairs={{0,3},{1,0},{2,1},{3,2},{4,7},{5,4},{6,5},{7,6},{8,11},{9,8},{10,9... | collective-permute-start | bytes 221192 | tf_op jit(solution)/shard_map/ppermute | solution.py:501
  79.6 1.7 %collective-permute-done.10.south = f32[9,16,128]{2,1,0:T(8,128)S(1)} collective-permute-done((f32[9,16,128]{2,1,0:T(8,128)S(1)}, f32[9,16,128]{2,1,0:T(8,128)S(1)}, u32[]{:S(2)}, u32[]{:S(2)}) %collective-permute-start.10) | collective-permute-done | bytes 73760 | tf_op jit(solution)/shard_map/ppermute | solution.py:501
  81.4 2.1 %collective-permute-start.12 = (f32[9,16,128]{2,1,0:T(8,128)S(1)}, f32[9,16,128]{2,1,0:T(8,128)S(1)}, u32[]{:S(2)}, u32[]{:S(2)}) collective-permute-start(f32[9,16,128]{2,1,0:T(8,128)S(1)} %shard_map.82.e_own), channel_id=1, source_target_pairs={{0,4},{4,0},{8,12},{12,8},{16,20},{20,16},{24,28},{28,24},{32,36},... | collective-permute-start | bytes 221192 | tf_op jit(solution)/shard_map/ppermute | solution.py:510
  83.5 1.0 collective-permute-start.13
  84.5 3.2 %collective-permute-done.13.e_far = f32[9,16,128]{2,1,0:T(8,128)S(1)} collective-permute-done((f32[9,16,128]{2,1,0:T(8,128)S(1)}, f32[9,16,128]{2,1,0:T(8,128)S(1)}, u32[]{:S(2)}, u32[]{:S(2)}) %collective-permute-start.13) | collective-permute-done | bytes 73760 | tf_op jit(solution)/shard_map/ppermute | solution.py:506
  87.7 9.3 %shard_map.83 = (f32[10,136,128]{2,1,0:T(8,128)S(1)}, f32[9,136,128]{2,1,0:T(8,128)S(1)}, f32[9,136,128]{2,1,0:T(8,128)S(1)}, f32[9,136,128]{2,1,0:T(8,128)S(1)}, f32[8,128]{1,0:T(8,128)S(1)}) custom-call(f32[9,136,128]{2,1,0:T(8,128)S(1)} %get-tuple-element.47.own, f32[9,136,128]{2,1,0:T(8,128)S(1)} %collective-permute-done.8.near, ...), custom_call_target="tpu_custom_call" | custom-call | bytes 8609792 | tf_op jit(solution)/shard_map/pallas_call | solution.py:28
  97.1 3.2 %collective-permute-start.14 = (f32[9,136,128]{2,1,0:T(8,128)S(1)}, f32[9,136,128]{2,1,0:T(8,128)S(1)}, u32[]{:S(2)}, u32[]{:S(2)}) collective-permute-start(f32[9,136,128]{2,1,0:T(8,128)S(1)} %get-tuple-element.54), channel_id=1, source_target_pairs={{0,4},{4,0},{8,12},{12,8},{16,20},{20,16},{24,28},{28,24},{32,36},... | collective-permute-start | bytes 1880072 | tf_op jit(solution)/shard_map/ppermute | solution.py:510
  100.3 1.7 %collective-permute-done.14.near = f32[9,136,128]{2,1,0:T(8,128)S(1)} collective-permute-done((f32[9,136,128]{2,1,0:T(8,128)S(1)}, f32[9,136,128]{2,1,0:T(8,128)S(1)}, u32[]{:S(2)}, u32[]{:S(2)}) %collective-permute-start.14) | collective-permute-done | bytes 626720 | tf_op jit(solution)/shard_map/ppermute | solution.py:510
  102.0 8.3 %collective-permute-done.15.far = f32[9,136,128]{2,1,0:T(8,128)S(1)} collective-permute-done((f32[9,136,128]{2,1,0:T(8,128)S(1)}, f32[9,136,128]{2,1,0:T(8,128)S(1)}, u32[]{:S(2)}, u32[]{:S(2)}) %collective-permute-start.15) | collective-permute-done | bytes 626720 | tf_op jit(solution)/shard_map/ppermute | solution.py:506
  110.5 3.2 %collective-permute-start.16 = (f32[9,136,128]{2,1,0:T(8,128)S(1)}, f32[9,136,128]{2,1,0:T(8,128)S(1)}, u32[]{:S(2)}, u32[]{:S(2)}) collective-permute-start(f32[9,136,128]{2,1,0:T(8,128)S(1)} %get-tuple-element.56.own), channel_id=1, source_target_pairs={{0,4},{4,0},{8,12},{12,8},{16,20},{20,16},{24,28},{28,24},{32,36},... | collective-permute-start | bytes 1880072 | tf_op jit(solution)/shard_map/ppermute | solution.py:510
  113.7 1.0 collective-permute-start.18
  114.7 1.8 %collective-permute-start.19 = (f32[9,16,128]{2,1,0:T(8,128)S(1)}, f32[9,16,128]{2,1,0:T(8,128)S(1)}, u32[]{:S(2)}, u32[]{:S(2)}) collective-permute-start(f32[9,16,128]{2,1,0:T(8,128)S(1)} %get-tuple-element.57.mine), channel_id=1, source_target_pairs={{0,3},{1,0},{2,1},{3,2},{4,7},{5,4},{6,5},{7,6},{8,11},{9,8},{10,9... | collective-permute-start | bytes 221192 | tf_op jit(solution)/shard_map/ppermute | solution.py:501
  116.5 1.7 %collective-permute-done.18.south = f32[9,16,128]{2,1,0:T(8,128)S(1)} collective-permute-done((f32[9,16,128]{2,1,0:T(8,128)S(1)}, f32[9,16,128]{2,1,0:T(8,128)S(1)}, u32[]{:S(2)}, u32[]{:S(2)}) %collective-permute-start.18) | collective-permute-done | bytes 73760 | tf_op jit(solution)/shard_map/ppermute | solution.py:501
  118.3 4.2 %collective-permute-start.20 = (f32[9,16,128]{2,1,0:T(8,128)S(1)}, f32[9,16,128]{2,1,0:T(8,128)S(1)}, u32[]{:S(2)}, u32[]{:S(2)}) collective-permute-start(f32[9,16,128]{2,1,0:T(8,128)S(1)} %shard_map.85.e_own), channel_id=1, source_target_pairs={{0,4},{4,0},{8,12},{12,8},{16,20},{20,16},{24,28},{28,24},{32,36},... | collective-permute-start | bytes 221192 | tf_op jit(solution)/shard_map/ppermute | solution.py:510
  122.5 0.9 collective-permute-done.20.e_near
  123.4 3.0 %collective-permute-done.21.e_far = f32[9,16,128]{2,1,0:T(8,128)S(1)} collective-permute-done((f32[9,16,128]{2,1,0:T(8,128)S(1)}, f32[9,16,128]{2,1,0:T(8,128)S(1)}, u32[]{:S(2)}, u32[]{:S(2)}) %collective-permute-start.21) | collective-permute-done | bytes 73760 | tf_op jit(solution)/shard_map/ppermute | solution.py:506
  126.4 9.3 %shard_map.86 = (f32[10,136,128]{2,1,0:T(8,128)S(1)}, f32[9,136,128]{2,1,0:T(8,128)S(1)}, f32[9,136,128]{2,1,0:T(8,128)S(1)}, f32[9,136,128]{2,1,0:T(8,128)S(1)}, f32[128,128]{1,0:T(8,128)S(1)}) custom-call(f32[9,136,128]{2,1,0:T(8,128)S(1)} %get-tuple-element.56.own, f32[9,136,128]{2,1,0:T(8,128)S(1)} %collective-permute-done.16.near, ...), custom_call_target="tpu_custom_call" | custom-call | bytes 8609792 | tf_op jit(solution)/shard_map/pallas_call | solution.py:28
  135.7 3.6 %collective-permute-start.22 = (f32[9,136,128]{2,1,0:T(8,128)S(1)}, f32[9,136,128]{2,1,0:T(8,128)S(1)}, u32[]{:S(2)}, u32[]{:S(2)}) collective-permute-start(f32[9,136,128]{2,1,0:T(8,128)S(1)} %get-tuple-element.61), channel_id=1, source_target_pairs={{0,4},{4,0},{8,12},{12,8},{16,20},{20,16},{24,28},{28,24},{32,36},... | collective-permute-start | bytes 1880072 | tf_op jit(solution)/shard_map/ppermute | solution.py:510
  139.3 18.1 %all_to_all.16 = f32[128,1,128]{2,1,0:T(1,128)S(1)} all-to-all(f32[128,1,128]{2,1,0:T(1,128)S(1)} %bitcast.26), channel_id=1, replica_groups=mesh['lon'=32,'lat'=4] {'lon','lat'}, dimensions={0} | all-to-all | bytes 131072 | tf_op jit(solution)/shard_map/all_to_all | solution.py:572
  157.6 0.4 collective-permute-start.24
  158.1 2.3 %collective-permute-start.25 = (f32[9,16,128]{2,1,0:T(8,128)S(1)}, f32[9,16,128]{2,1,0:T(8,128)S(1)}, u32[]{:S(2)}, u32[]{:S(2)}) collective-permute-start(f32[9,16,128]{2,1,0:T(8,128)S(1)} %get-tuple-element.65.mine), channel_id=1, source_target_pairs={{0,3},{1,0},{2,1},{3,2},{4,7},{5,4},{6,5},{7,6},{8,11},{9,8},{10,9... | collective-permute-start | bytes 221192 | tf_op jit(solution)/shard_map/ppermute | solution.py:501
  160.4 1.7 %collective-permute-done.24.south = f32[9,16,128]{2,1,0:T(8,128)S(1)} collective-permute-done((f32[9,16,128]{2,1,0:T(8,128)S(1)}, f32[9,16,128]{2,1,0:T(8,128)S(1)}, u32[]{:S(2)}, u32[]{:S(2)}) %collective-permute-start.24) | collective-permute-done | bytes 73760 | tf_op jit(solution)/shard_map/ppermute | solution.py:501
  162.1 1.9 %shard_map.88 = (f32[1096,128]{1,0:T(8,128)}, f32[1096,128]{1,0:T(8,128)}) custom-call(f32[9,136,128]{2,1,0:T(8,128)S(1)} %get-tuple-element.52.v0, f32[9,136,128]{2,1,0:T(8,128)S(1)} %get-tuple-element.59.v1, f32[9,136,128]{2,1,0:T(8,128)S(1)} %get-tuple-element.64.main, f32[9,16,128]{2,1,0:T(8,128)S(1)} %get-tuple-element.65.mine, ...), custom_call_target="tpu_custom_call" | custom-call | bytes 2166784 | tf_op jit(solution)/shard_map/pallas_call | solution.py:28
  (44 shorter events, 0.9 us)
Async XLA Ops:
  0.6 1.5 copy-start.8
  0.6 1.8 %copy-start.9 = (f32[4,1,128,4,128]{4,3,2,1,0:T(4,128)S(1)}, f32[4,1,128,4,128]{4,3,2,1,0:T(4,128)}, u32[]{:S(2)}) copy-start(f32[4,1,128,4,128]{4,3,2,1,0:T(4,128)} %param.9) | copy-start | bytes 3145732
  5.5 11.5 %copy-start.3 = (f32[274,128]{1,0:T(8,128)S(1)}, f32[274,128]{1,0:T(8,128)}, u32[]{:S(2)}) copy-start(f32[274,128]{1,0:T(8,128)} %weighting.1) | copy-start | bytes 420868
  5.5 43.3 %all-to-all-start = ((f32[128,32,128]{2,1,0:T(8,128)}), f32[128,32,128]{2,1,0:T(8,128)S(1)}, u32[]{:S(2)}, u32[]{:S(2)}) async-start(f32[128,32,128]{2,1,0:T(8,128)} %copy.13), calls=%async_computation | async-start | bytes 4194304 | tf_op jit(solution)/shard_map/all_to_all | solution.py:521
  17.0 1.6 copy-start
  21.0 1.4 copy-start.1
  22.4 22.9 %copy-start.4 = (f32[2,136,128]{2,1,0:T(8,128)}, f32[2,136,128]{2,1,0:T(8,128)S(1)}, u32[]{:S(2)}) copy-start(f32[2,136,128]{2,1,0:T(8,128)S(1)} %get-tuple-element.40.packed) | copy-start | bytes 417796
  22.4 32.1 %collective-permute-start = (f32[14,136,128]{2,1,0:T(8,128)}, f32[14,136,128]{2,1,0:T(8,128)}, u32[]{:S(2)}, u32[]{:S(2)}) collective-permute-start(f32[14,136,128]{2,1,0:T(8,128)} %get-tuple-element.41), channel_id=1, source_target_pairs={{0,4},{4,0},{8,12},{12,8},{16,20},{20,16},{24,28},{28,24},{32,36},... | collective-permute-start | bytes 2924552 | tf_op jit(solution)/shard_map/ppermute | solution.py:510
  23.5 31.1 %collective-permute-start.1 = (f32[14,136,128]{2,1,0:T(8,128)}, f32[14,136,128]{2,1,0:T(8,128)}, u32[]{:S(2)}, u32[]{:S(2)}) collective-permute-start(f32[14,136,128]{2,1,0:T(8,128)} %get-tuple-element.42), channel_id=1, source_target_pairs={{0,124},{4,8},{8,4},{12,16},{16,12},{20,24},{24,20},{28,32},{32,28... | collective-permute-start | bytes 2924552 | tf_op jit(solution)/shard_map/ppermute | solution.py:506
  24.2 19.8 %collective-permute-start.2 = (f32[26,8,128]{2,1,0:T(8,128)S(1)}, f32[26,8,128]{2,1,0:T(8,128)S(1)}, u32[]{:S(2)}, u32[]{:S(2)}) collective-permute-start(f32[26,8,128]{2,1,0:T(8,128)S(1)} %get-tuple-element.43), channel_id=1, source_target_pairs={{0,1},{1,2},{2,3},{3,0},{4,5},{5,6},{6,7},{7,4},{8,9},{9,10},{10,1... | collective-permute-start | bytes 319496 | tf_op jit(solution)/shard_map/ppermute | solution.py:501
  25.4 18.6 %collective-permute-start.3 = (f32[26,8,128]{2,1,0:T(8,128)S(1)}, f32[26,8,128]{2,1,0:T(8,128)S(1)}, u32[]{:S(2)}, u32[]{:S(2)}) collective-permute-start(f32[26,8,128]{2,1,0:T(8,128)S(1)} %get-tuple-element.43), channel_id=1, source_target_pairs={{0,3},{1,0},{2,1},{3,2},{4,7},{5,4},{6,5},{7,6},{8,11},{9,8},{10,9... | collective-permute-start | bytes 319496 | tf_op jit(solution)/shard_map/ppermute | solution.py:501
  44.0 10.5 %collective-permute-start.4 = (f32[26,8,128]{2,1,0:T(8,128)S(1)}, f32[26,8,128]{2,1,0:T(8,128)}, u32[]{:S(2)}, u32[]{:S(2)}) collective-permute-start(f32[26,8,128]{2,1,0:T(8,128)S(1)} %shard_map.79.halo), channel_id=1, source_target_pairs={{0,4},{4,0},{8,12},{12,8},{16,20},{20,16},{24,28},{28,24},{32,36},... | collective-permute-start | bytes 319496 | tf_op jit(solution)/shard_map/ppermute | solution.py:510
  45.3 9.2 %collective-permute-start.5 = (f32[26,8,128]{2,1,0:T(8,128)S(1)}, f32[26,8,128]{2,1,0:T(8,128)}, u32[]{:S(2)}, u32[]{:S(2)}) collective-permute-start(f32[26,8,128]{2,1,0:T(8,128)S(1)} %shard_map.79.halo), channel_id=1, source_target_pairs={{0,124},{4,8},{8,4},{12,16},{16,12},{20,24},{24,20},{28,32},{32,28... | collective-permute-start | bytes 319496 | tf_op jit(solution)/shard_map/ppermute | solution.py:506
  46.6 7.9 %copy-start.5 = (f32[2,136,128]{2,1,0:T(8,128)S(1)}, f32[2,136,128]{2,1,0:T(8,128)}, u32[]{:S(2)}) copy-start(f32[2,136,128]{2,1,0:T(8,128)} %copy-done.4) | copy-start | bytes 417796
  48.7 5.8 %copy-start.2 = (f32[32,136,128]{2,1,0:T(8,128)S(1)}, f32[32,136,128]{2,1,0:T(8,128)}, u32[]{:S(2)}) copy-start(f32[32,136,128]{2,1,0:T(8,128)} %copy-done.1) | copy-start | bytes 6684676
  48.7 0.8 copy-start.6
  49.6 0.7 copy-start.7
  59.9 5.4 %collective-permute-start.6 = (f32[9,136,128]{2,1,0:T(8,128)S(1)}, f32[9,136,128]{2,1,0:T(8,128)S(1)}, u32[]{:S(2)}, u32[]{:S(2)}) collective-permute-start(f32[9,136,128]{2,1,0:T(8,128)S(1)} %get-tuple-element.45), channel_id=1, source_target_pairs={{0,4},{4,0},{8,12},{12,8},{16,20},{20,16},{24,28},{28,24},{32,36},... | collective-permute-start | bytes 1880072 | tf_op jit(solution)/shard_map/ppermute | solution.py:510
  63.6 10.0 %collective-permute-start.7 = (f32[9,136,128]{2,1,0:T(8,128)S(1)}, f32[9,136,128]{2,1,0:T(8,128)S(1)}, u32[]{:S(2)}, u32[]{:S(2)}) collective-permute-start(f32[9,136,128]{2,1,0:T(8,128)S(1)} %get-tuple-element.46), channel_id=1, source_target_pairs={{0,124},{4,8},{8,4},{12,16},{16,12},{20,24},{24,20},{28,32},{32,28... | collective-permute-start | bytes 1880072 | tf_op jit(solution)/shard_map/ppermute | solution.py:506
  73.7 14.0 %collective-permute-start.8 = (f32[9,136,128]{2,1,0:T(8,128)S(1)}, f32[9,136,128]{2,1,0:T(8,128)S(1)}, u32[]{:S(2)}, u32[]{:S(2)}) collective-permute-start(f32[9,136,128]{2,1,0:T(8,128)S(1)} %get-tuple-element.47.own), channel_id=1, source_target_pairs={{0,4},{4,0},{8,12},{12,8},{16,20},{20,16},{24,28},{28,24},{32,36},... | collective-permute-start | bytes 1880072 | tf_op jit(solution)/shard_map/ppermute | solution.py:510
  76.9 10.8 %collective-permute-start.9 = (f32[9,136,128]{2,1,0:T(8,128)S(1)}, f32[9,136,128]{2,1,0:T(8,128)S(1)}, u32[]{:S(2)}, u32[]{:S(2)}) collective-permute-start(f32[9,136,128]{2,1,0:T(8,128)S(1)} %get-tuple-element.47.own), channel_id=1, source_target_pairs={{0,124},{4,8},{8,4},{12,16},{16,12},{20,24},{24,20},{28,32},{32,28... | collective-permute-start | bytes 1880072 | tf_op jit(solution)/shard_map/ppermute | solution.py:506
  76.9 4.4 %collective-permute-start.10 = (f32[9,16,128]{2,1,0:T(8,128)S(1)}, f32[9,16,128]{2,1,0:T(8,128)S(1)}, u32[]{:S(2)}, u32[]{:S(2)}) collective-permute-start(f32[9,16,128]{2,1,0:T(8,128)S(1)} %get-tuple-element.48.mine), channel_id=1, source_target_pairs={{0,1},{1,2},{2,3},{3,0},{4,5},{5,6},{6,7},{7,4},{8,9},{9,10},{10,1... | collective-permute-start | bytes 221192 | tf_op jit(solution)/shard_map/ppermute | solution.py:501
  78.0 3.4 %collective-permute-start.11 = (f32[9,16,128]{2,1,0:T(8,128)S(1)}, f32[9,16,128]{2,1,0:T(8,128)S(1)}, u32[]{:S(2)}, u32[]{:S(2)}) collective-permute-start(f32[9,16,128]{2,1,0:T(8,128)S(1)} %get-tuple-element.48.mine), channel_id=1, source_target_pairs={{0,3},{1,0},{2,1},{3,2},{4,7},{5,4},{6,5},{7,6},{8,11},{9,8},{10,9... | collective-permute-start | bytes 221192 | tf_op jit(solution)/shard_map/ppermute | solution.py:501
  81.4 3.1 %collective-permute-start.12 = (f32[9,16,128]{2,1,0:T(8,128)S(1)}, f32[9,16,128]{2,1,0:T(8,128)S(1)}, u32[]{:S(2)}, u32[]{:S(2)}) collective-permute-start(f32[9,16,128]{2,1,0:T(8,128)S(1)} %shard_map.82.e_own), channel_id=1, source_target_pairs={{0,4},{4,0},{8,12},{12,8},{16,20},{20,16},{24,28},{28,24},{32,36},... | collective-permute-start | bytes 221192 | tf_op jit(solution)/shard_map/ppermute | solution.py:510
  83.5 4.2 %collective-permute-start.13 = (f32[9,16,128]{2,1,0:T(8,128)S(1)}, f32[9,16,128]{2,1,0:T(8,128)S(1)}, u32[]{:S(2)}, u32[]{:S(2)}) collective-permute-start(f32[9,16,128]{2,1,0:T(8,128)S(1)} %shard_map.82.e_own), channel_id=1, source_target_pairs={{0,124},{4,8},{8,4},{12,16},{16,12},{20,24},{24,20},{28,32},{32,28... | collective-permute-start | bytes 221192 | tf_op jit(solution)/shard_map/ppermute | solution.py:506
  97.1 4.9 %collective-permute-start.14 = (f32[9,136,128]{2,1,0:T(8,128)S(1)}, f32[9,136,128]{2,1,0:T(8,128)S(1)}, u32[]{:S(2)}, u32[]{:S(2)}) collective-permute-start(f32[9,136,128]{2,1,0:T(8,128)S(1)} %get-tuple-element.54), channel_id=1, source_target_pairs={{0,4},{4,0},{8,12},{12,8},{16,20},{20,16},{24,28},{28,24},{32,36},... | collective-permute-start | bytes 1880072 | tf_op jit(solution)/shard_map/ppermute | solution.py:510
  100.3 10.0 %collective-permute-start.15 = (f32[9,136,128]{2,1,0:T(8,128)S(1)}, f32[9,136,128]{2,1,0:T(8,128)S(1)}, u32[]{:S(2)}, u32[]{:S(2)}) collective-permute-start(f32[9,136,128]{2,1,0:T(8,128)S(1)} %get-tuple-element.55), channel_id=1, source_target_pairs={{0,124},{4,8},{8,4},{12,16},{16,12},{20,24},{24,20},{28,32},{32,28... | collective-permute-start | bytes 1880072 | tf_op jit(solution)/shard_map/ppermute | solution.py:506
  110.5 15.9 %collective-permute-start.16 = (f32[9,136,128]{2,1,0:T(8,128)S(1)}, f32[9,136,128]{2,1,0:T(8,128)S(1)}, u32[]{:S(2)}, u32[]{:S(2)}) collective-permute-start(f32[9,136,128]{2,1,0:T(8,128)S(1)} %get-tuple-element.56.own), channel_id=1, source_target_pairs={{0,4},{4,0},{8,12},{12,8},{16,20},{20,16},{24,28},{28,24},{32,36},... | collective-permute-start | bytes 1880072 | tf_op jit(solution)/shard_map/ppermute | solution.py:510
  113.7 12.7 %collective-permute-start.17 = (f32[9,136,128]{2,1,0:T(8,128)S(1)}, f32[9,136,128]{2,1,0:T(8,128)S(1)}, u32[]{:S(2)}, u32[]{:S(2)}) collective-permute-start(f32[9,136,128]{2,1,0:T(8,128)S(1)} %get-tuple-element.56.own), channel_id=1, source_target_pairs={{0,124},{4,8},{8,4},{12,16},{16,12},{20,24},{24,20},{28,32},{32,28... | collective-permute-start | bytes 1880072 | tf_op jit(solution)/shard_map/ppermute | solution.py:506
  113.7 4.6 %collective-permute-start.18 = (f32[9,16,128]{2,1,0:T(8,128)S(1)}, f32[9,16,128]{2,1,0:T(8,128)S(1)}, u32[]{:S(2)}, u32[]{:S(2)}) collective-permute-start(f32[9,16,128]{2,1,0:T(8,128)S(1)} %get-tuple-element.57.mine), channel_id=1, source_target_pairs={{0,1},{1,2},{2,3},{3,0},{4,5},{5,6},{6,7},{7,4},{8,9},{9,10},{10,1... | collective-permute-start | bytes 221192 | tf_op jit(solution)/shard_map/ppermute | solution.py:501
  114.7 3.6 %collective-permute-start.19 = (f32[9,16,128]{2,1,0:T(8,128)S(1)}, f32[9,16,128]{2,1,0:T(8,128)S(1)}, u32[]{:S(2)}, u32[]{:S(2)}) collective-permute-start(f32[9,16,128]{2,1,0:T(8,128)S(1)} %get-tuple-element.57.mine), channel_id=1, source_target_pairs={{0,3},{1,0},{2,1},{3,2},{4,7},{5,4},{6,5},{7,6},{8,11},{9,8},{10,9... | collective-permute-start | bytes 221192 | tf_op jit(solution)/shard_map/ppermute | solution.py:501
  118.3 5.1 %collective-permute-start.20 = (f32[9,16,128]{2,1,0:T(8,128)S(1)}, f32[9,16,128]{2,1,0:T(8,128)S(1)}, u32[]{:S(2)}, u32[]{:S(2)}) collective-permute-start(f32[9,16,128]{2,1,0:T(8,128)S(1)} %shard_map.85.e_own), channel_id=1, source_target_pairs={{0,4},{4,0},{8,12},{12,8},{16,20},{20,16},{24,28},{28,24},{32,36},... | collective-permute-start | bytes 221192 | tf_op jit(solution)/shard_map/ppermute | solution.py:510
  122.5 3.9 %collective-permute-start.21 = (f32[9,16,128]{2,1,0:T(8,128)S(1)}, f32[9,16,128]{2,1,0:T(8,128)S(1)}, u32[]{:S(2)}, u32[]{:S(2)}) collective-permute-start(f32[9,16,128]{2,1,0:T(8,128)S(1)} %shard_map.85.e_own), channel_id=1, source_target_pairs={{0,124},{4,8},{8,4},{12,16},{16,12},{20,24},{24,20},{28,32},{32,28... | collective-permute-start | bytes 221192 | tf_op jit(solution)/shard_map/ppermute | solution.py:506
  135.7 21.7 %collective-permute-start.22 = (f32[9,136,128]{2,1,0:T(8,128)S(1)}, f32[9,136,128]{2,1,0:T(8,128)S(1)}, u32[]{:S(2)}, u32[]{:S(2)}) collective-permute-start(f32[9,136,128]{2,1,0:T(8,128)S(1)} %get-tuple-element.61), channel_id=1, source_target_pairs={{0,4},{4,0},{8,12},{12,8},{16,20},{20,16},{24,28},{28,24},{32,36},... | collective-permute-start | bytes 1880072 | tf_op jit(solution)/shard_map/ppermute | solution.py:510
  139.3 18.1 %collective-permute-start.23 = (f32[9,136,128]{2,1,0:T(8,128)S(1)}, f32[9,136,128]{2,1,0:T(8,128)S(1)}, u32[]{:S(2)}, u32[]{:S(2)}) collective-permute-start(f32[9,136,128]{2,1,0:T(8,128)S(1)} %get-tuple-element.62), channel_id=1, source_target_pairs={{0,124},{4,8},{8,4},{12,16},{16,12},{20,24},{24,20},{28,32},{32,28... | collective-permute-start | bytes 1880072 | tf_op jit(solution)/shard_map/ppermute | solution.py:506
  157.6 4.5 %collective-permute-start.24 = (f32[9,16,128]{2,1,0:T(8,128)S(1)}, f32[9,16,128]{2,1,0:T(8,128)S(1)}, u32[]{:S(2)}, u32[]{:S(2)}) collective-permute-start(f32[9,16,128]{2,1,0:T(8,128)S(1)} %get-tuple-element.65.mine), channel_id=1, source_target_pairs={{0,1},{1,2},{2,3},{3,0},{4,5},{5,6},{6,7},{7,4},{8,9},{9,10},{10,1... | collective-permute-start | bytes 221192 | tf_op jit(solution)/shard_map/ppermute | solution.py:501
  158.1 4.1 %collective-permute-start.25 = (f32[9,16,128]{2,1,0:T(8,128)S(1)}, f32[9,16,128]{2,1,0:T(8,128)S(1)}, u32[]{:S(2)}, u32[]{:S(2)}) collective-permute-start(f32[9,16,128]{2,1,0:T(8,128)S(1)} %get-tuple-element.65.mine), channel_id=1, source_target_pairs={{0,3},{1,0},{2,1},{3,2},{4,7},{5,4},{6,5},{7,6},{8,11},{9,8},{10,9... | collective-permute-start | bytes 221192 | tf_op jit(solution)/shard_map/ppermute | solution.py:501

commit v5 on v4

--- a/solution.py
+++ b/solution.py
@@ -464,8 +464,16 @@
             rim[k, pl.ds(m + 8, 1)] = main[k, pl.ds(8 * (m + 9) + 7, 1)]
 
 
-def final_kernel(v0, v1, main, mine, south, north, sums, solution, residual, edge, lay_s, lay_r):
-    total = jnp.sum(sums[...], axis=0, keepdims=True)
+def last_gather_kernel(own, near, far, sums, main, rim, part):
+    gather_kernel(own, near, far, main, rim)
+    total = jnp.broadcast_to(jnp.sum(sums[...], axis=0, keepdims=True), part.shape)
+    part[...] = total
+    rim[2 * SLAB + 1] = jnp.broadcast_to(total[:1], rim.shape[1:])
+
+
+def final_kernel(v0, v1, main, mine, south, north, across, solution, residual, edge, lay_s, lay_r):
+    k = 2 * SLAB + 1
+    total = (mine[k, pl.ds(0, 1)] + across[pl.ds(0, 1)]) + (south[k, pl.ds(0, 1)] + north[k, pl.ds(0, 1)])
     lane = lanes(total.shape)
     m = [jnp.sum(jnp.where(lane == k, total, 0.0), axis=1, keepdims=True) for k in range(4)]
     a, c, d = m[1] / m[0], m[2] / m[0], m[3] / m[0]
@@ -539,9 +547,9 @@
     pieces = [(2 * SLAB + 2, ROWS, 128), parcel, parcel]
     steps = [pltpu.VMEM((2 * EXT, ROWS, 128), F32)] * (NT + 1) + [pltpu.VMEM((2, ROWS, 128), F32)] * (NT + 1)
 
-    def gathered(parts, *more):
+    def gathered(parts):
         mine, to_near, to_far = parts
-        return call(gather_kernel, [parcel, rim], [mine, near_swap(to_near), far_swap(to_far), *more])
+        return call(gather_kernel, [parcel, rim], [mine, near_swap(to_near), far_swap(to_far)])
 
     def hessian(state, moments, rows):
         main, mine = state
@@ -568,13 +576,18 @@
         [pltpu.VMEM((3, ROWS, 128), F32), *steps],
     )
     *parts, v0, moments = hessian(gathered(parts), jnp.zeros((8, 128), F32), 8)
-    *parts, v1, moments = hessian(gathered(parts), moments, owners)
-    sums = lax.all_to_all(moments, ("lon", "lat"), split_axis=0, concat_axis=0, tiled=True)
-    main, mine = gathered(parts, sums)
+    *parts, v1, moments = hessian(gathered(parts), moments, lax.axis_size("lon"))
+    sums = lax.all_to_all(moments, "lon", split_axis=0, concat_axis=0, tiled=True)
+    mine, to_near, to_far = parts
+    main, mine, part = call(
+        last_gather_kernel,
+        [parcel, (2 * SLAB + 2, 16, 128), (8, 128)],
+        [mine, near_swap(to_near), far_swap(to_far), sums],
+    )
     solution, residual = call(
         final_kernel,
         [(2 * depth * SLAB, BAND)] * 2,
-        [v0, v1, main, mine, shift(mine, "lat", 1), shift(mine, "lat", -1), sums],
+        [v0, v1, main, mine, shift(mine, "lat", 1), shift(mine, "lat", -1), shift(part, "lat", 2)],
         [pltpu.VMEM(rim, F32), pltpu.VMEM((ROWS, 128), F32), pltpu.VMEM((ROWS, 128), F32)],
     )
     shape = (2, depth, SLAB, BAND)

time: 165 us -> 163 us (0.988)
  blocking collectives: 18.1 us -> 13.3 us
    all_to_all x1, blocking collectives: 18.1 us -> 13.3 us  [body(): lax.all_to_all(moments, 'lon', split_axis=0, concat_axis=0, tiled=True)]
    ppermute x8 -> x9, starting transfers between devices: 10.9 us -> 12.5 us  [shift(): return lax.ppermute(x, axis, [(i, (i + by) % n) for i in range(n)])]
    ppermute x8 -> x9, waiting for transfers between devices: 22.3 us -> 23.3 us  [shift(): return lax.ppermute(x, axis, [(i, (i + by) % n) for i in range(n)])]
  transfers between devices with their start and end apart: 27 -> 28, of which waited for: 12 -> 12; matrix products, arithmetic and copies ran while one was open for 0% -> 0% of each run, Pallas kernels for 4% -> 4%
where the time goes in v5:
time: 163 us; the launch traced here: 162 us
  starting transfers between devices  52.6 us (32%)
  waiting for transfers between devices  52.6 us (32%)
  Pallas kernels  33.1 us (20%)
  blocking collectives  13.3 us (8%)
  local copies, waits for them, and re-layouts  8.96 us (5%)
    pallas_call x12, Pallas kernels, call(): pl.pallas_call(kernel, out_shape=[jax.ShapeDtypeStruct(s, F32) for s in s...  33.1 us
    ppermute x9, starting transfers between devices, near_swap(): lax.ppermute(x, 'lon', [(i, i ^ 1) for i in range(lax.axis_size('lon'))])  25.5 us
    ppermute x9, waiting for transfers between devices, shift(): return lax.ppermute(x, axis, [(i, (i + by) % n) for i in range(n)])  23.3 us
    ppermute x9, waiting for transfers between devices, far_swap(): lax.ppermute(x, 'lon', [(i, (i + 1 if i % 2 else i - 1) % n) for i in ran...  22.9 us
    all_to_all x1, blocking collectives, body(): lax.all_to_all(moments, 'lon', split_axis=0, concat_axis=0, tiled=True)  13.3 us
    ppermute x9, starting transfers between devices, shift(): return lax.ppermute(x, axis, [(i, (i + by) % n) for i in range(n)])  12.5 us
    all_to_all x1, starting transfers between devices, body(): lax.all_to_all(message.reshape(owners, 2 * NT * SLOTS, channels), ('lon',...  11.5 us
    unnamed x21, local copies, waits for them, and re-layouts  6.38 us
  transfers between devices with their start and end apart: 28, of which 12 were waited for; matrix products, arithmetic and copies ran while one was open for 0% of the time, Pallas kernels for 4%

profile of v5, /device:TPU:1, one launch (start us, length us, event | category | flops | bytes accessed | tf_op | source)
XLA Modules:
  0.0 161.8 jit_solution(1501370941507435464)
XLA Ops:
  0.6 1.5 copy.19
  2.2 0.3 copy-done.9
  2.9 2.6 %copy.13 = f32[128,32,128]{2,1,0:T(8,128)} copy(f32[128,32,128]{2,0,1:T(8,128)S(1)} %bitcast.28) | data formatting | bytes 4194304 | tf_op jit(solution)/shard_map/reshape | solution.py:530
  5.5 11.5 %all-to-all-start = ((f32[128,32,128]{2,1,0:T(8,128)}), f32[128,32,128]{2,1,0:T(8,128)S(1)}, u32[]{:S(2)}, u32[]{:S(2)}) async-start(f32[128,32,128]{2,1,0:T(8,128)} %copy.13), calls=%async_computation | async-start | bytes 4194304 | tf_op jit(solution)/shard_map/all_to_all | solution.py:529
  17.0 1.6 %copy-done = f32[4,2,137,4,128]{4,3,2,1,0:T(4,128)S(1)} copy-done((f32[4,2,137,4,128]{4,3,2,1,0:T(4,128)S(1)}, f32[4,2,137,4,128]{4,3,2,1,0:T(4,128)}, u32[]{:S(2)}) %copy-start) | copy-done | bytes 2244632
  18.6 2.4 %shard_map.77 = (f32[32,136,128]{2,1,0:T(8,128)S(1)}, f32[8,136,128]{2,1,0:T(8,128)S(1)}, f32[2,136,128]{2,1,0:T(8,128)S(1)}, f32[14,136,128]{2,1,0:T(8,128)}, f...) custom-call(f32[4384,128]{1,0:T(8,128)S(1)} %bitcast.23, ...), custom_call_target="tpu_custom_call" | custom-call | bytes 2384896 | tf_op jit(solution)/shard_map/pallas_call | solution.py:28
  21.0 1.4 copy-done.1
  22.4 1.1 collective-permute-start
  23.4 0.7 collective-permute-start.1
  24.2 1.2 collective-permute-start.2
  25.4 1.5 collective-permute-start.3
  26.8 17.1 %collective-permute-done.2.south = f32[26,8,128]{2,1,0:T(8,128)S(1)} collective-permute-done((f32[26,8,128]{2,1,0:T(8,128)S(1)}, f32[26,8,128]{2,1,0:T(8,128)S(1)}, u32[]{:S(2)}, u32[]{:S(2)}) %collective-permute-start.2) | collective-permute-done | bytes 106528 | tf_op jit(solution)/shard_map/ppermute | solution.py:509
  44.0 1.3 collective-permute-start.4
  45.3 1.4 collective-permute-start.5
  46.6 2.1 %all-to-all-done = f32[128,32,128]{2,1,0:T(8,128)S(1)} async-done(((f32[128,32,128]{2,1,0:T(8,128)}), f32[128,32,128]{2,1,0:T(8,128)S(1)}, u32[]{:S(2)}, u32[]{:S(2)}) %all-to-all-start) | async-done | bytes 2097184 | tf_op jit(solution)/shard_map/all_to_all | solution.py:529
  48.7 0.8 copy-done.6
  49.6 0.7 copy-done.7
  50.3 4.2 %shard_map.78 = (f32[4,544,128]{2,1,0:T(8,128)S(1)}, f32[40,136,128]{2,1,0:T(8,128)S(1)}) custom-call(f32[4096,128]{1,0:T(8,128)S(1)} %bitcast.22, s32[4,4,128]{2,1,0:T(4,128)S(1)} %bitcast.26, s32[4,128]{1,0:T(4,128)S(1)} %bitcast.27, f32[256,128]{1,0:T(8,128)S(1)} %get-tuple-element.36.table, f32[256,512]{1,0:T(8,128)S(1)} %get-tuple-element.37.others), custom_call_target="tpu_custom_call" | custom-call | bytes 2762752 | tf_op jit(solution)/shard_map/pallas_call | solution.py:28
  54.5 5.3 %shard_map.80 = (f32[10,136,128]{2,1,0:T(8,128)S(1)}, f32[9,136,128]{2,1,0:T(8,128)S(1)}, f32[9,136,128]{2,1,0:T(8,128)S(1)}, f32[60,136,128]{2,1,0:T(8,128)S(1)}, f32[8,136,128]{2,1,0:T(8,128)S(1)}) custom-call(f32[40,136,128]{2,1,0:T(8,128)S(1)} %get-tuple-element.38.grads, f32[32,136,128]{2,1,0:T(8,128)S(1)} %copy-done.2, ...), custom_call_target="tpu_custom_call" | custom-call | bytes 7979008 | tf_op jit(solution)/shard_map/pallas_call | solution.py:28
  59.9 3.7 %collective-permute-start.6 = (f32[9,136,128]{2,1,0:T(8,128)S(1)}, f32[9,136,128]{2,1,0:T(8,128)S(1)}, u32[]{:S(2)}, u32[]{:S(2)}) collective-permute-start(f32[9,136,128]{2,1,0:T(8,128)S(1)} %get-tuple-element.46), channel_id=1, source_target_pairs={{0,4},{4,0},{8,12},{12,8},{16,20},{20,16},{24,28},{28,24},{32,36},... | collective-permute-start | bytes 1880072 | tf_op jit(solution)/shard_map/ppermute | solution.py:518
  63.6 1.7 %collective-permute-done.6.near = f32[9,136,128]{2,1,0:T(8,128)S(1)} collective-permute-done((f32[9,136,128]{2,1,0:T(8,128)S(1)}, f32[9,136,128]{2,1,0:T(8,128)S(1)}, u32[]{:S(2)}, u32[]{:S(2)}) %collective-permute-start.6) | collective-permute-done | bytes 626720 | tf_op jit(solution)/shard_map/ppermute | solution.py:518
  65.2 8.3 %collective-permute-done.7.far = f32[9,136,128]{2,1,0:T(8,128)S(1)} collective-permute-done((f32[9,136,128]{2,1,0:T(8,128)S(1)}, f32[9,136,128]{2,1,0:T(8,128)S(1)}, u32[]{:S(2)}, u32[]{:S(2)}) %collective-permute-start.7) | collective-permute-done | bytes 626720 | tf_op jit(solution)/shard_map/ppermute | solution.py:514
  73.7 3.2 %collective-permute-start.8 = (f32[9,136,128]{2,1,0:T(8,128)S(1)}, f32[9,136,128]{2,1,0:T(8,128)S(1)}, u32[]{:S(2)}, u32[]{:S(2)}) collective-permute-start(f32[9,136,128]{2,1,0:T(8,128)S(1)} %get-tuple-element.48.own), channel_id=1, source_target_pairs={{0,4},{4,0},{8,12},{12,8},{16,20},{20,16},{24,28},{28,24},{32,36},... | collective-permute-start | bytes 1880072 | tf_op jit(solution)/shard_map/ppermute | solution.py:518
  76.9 1.0 collective-permute-start.10
  77.9 1.7 %collective-permute-start.11 = (f32[9,16,128]{2,1,0:T(8,128)S(1)}, f32[9,16,128]{2,1,0:T(8,128)S(1)}, u32[]{:S(2)}, u32[]{:S(2)}) collective-permute-start(f32[9,16,128]{2,1,0:T(8,128)S(1)} %get-tuple-element.49.mine), channel_id=1, source_target_pairs={{0,3},{1,0},{2,1},{3,2},{4,7},{5,4},{6,5},{7,6},{8,11},{9,8},{10,9... | collective-permute-start | bytes 221192 | tf_op jit(solution)/shard_map/ppermute | solution.py:509
  79.6 1.7 %collective-permute-done.10.south = f32[9,16,128]{2,1,0:T(8,128)S(1)} collective-permute-done((f32[9,16,128]{2,1,0:T(8,128)S(1)}, f32[9,16,128]{2,1,0:T(8,128)S(1)}, u32[]{:S(2)}, u32[]{:S(2)}) %collective-permute-start.10) | collective-permute-done | bytes 73760 | tf_op jit(solution)/shard_map/ppermute | solution.py:509
  81.4 2.1 %collective-permute-start.12 = (f32[9,16,128]{2,1,0:T(8,128)S(1)}, f32[9,16,128]{2,1,0:T(8,128)S(1)}, u32[]{:S(2)}, u32[]{:S(2)}) collective-permute-start(f32[9,16,128]{2,1,0:T(8,128)S(1)} %shard_map.82.e_own), channel_id=1, source_target_pairs={{0,4},{4,0},{8,12},{12,8},{16,20},{20,16},{24,28},{28,24},{32,36},... | collective-permute-start | bytes 221192 | tf_op jit(solution)/shard_map/ppermute | solution.py:518
  83.5 1.0 collective-permute-start.13
  84.5 3.2 %collective-permute-done.13.e_far = f32[9,16,128]{2,1,0:T(8,128)S(1)} collective-permute-done((f32[9,16,128]{2,1,0:T(8,128)S(1)}, f32[9,16,128]{2,1,0:T(8,128)S(1)}, u32[]{:S(2)}, u32[]{:S(2)}) %collective-permute-start.13) | collective-permute-done | bytes 73760 | tf_op jit(solution)/shard_map/ppermute | solution.py:514
  87.7 9.3 %shard_map.83 = (f32[10,136,128]{2,1,0:T(8,128)S(1)}, f32[9,136,128]{2,1,0:T(8,128)S(1)}, f32[9,136,128]{2,1,0:T(8,128)S(1)}, f32[9,136,128]{2,1,0:T(8,128)S(1)}, f32[8,128]{1,0:T(8,128)S(1)}) custom-call(f32[9,136,128]{2,1,0:T(8,128)S(1)} %get-tuple-element.48.own, f32[9,136,128]{2,1,0:T(8,128)S(1)} %collective-permute-done.8.near, ...), custom_call_target="tpu_custom_call" | custom-call | bytes 8609792 | tf_op jit(solution)/shard_map/pallas_call | solution.py:28
  97.1 3.2 %collective-permute-start.14 = (f32[9,136,128]{2,1,0:T(8,128)S(1)}, f32[9,136,128]{2,1,0:T(8,128)S(1)}, u32[]{:S(2)}, u32[]{:S(2)}) collective-permute-start(f32[9,136,128]{2,1,0:T(8,128)S(1)} %get-tuple-element.55), channel_id=1, source_target_pairs={{0,4},{4,0},{8,12},{12,8},{16,20},{20,16},{24,28},{28,24},{32,36},... | collective-permute-start | bytes 1880072 | tf_op jit(solution)/shard_map/ppermute | solution.py:518
  100.3 1.7 %collective-permute-done.14.near = f32[9,136,128]{2,1,0:T(8,128)S(1)} collective-permute-done((f32[9,136,128]{2,1,0:T(8,128)S(1)}, f32[9,136,128]{2,1,0:T(8,128)S(1)}, u32[]{:S(2)}, u32[]{:S(2)}) %collective-permute-start.14) | collective-permute-done | bytes 626720 | tf_op jit(solution)/shard_map/ppermute | solution.py:518
  102.0 8.3 %collective-permute-done.15.far = f32[9,136,128]{2,1,0:T(8,128)S(1)} collective-permute-done((f32[9,136,128]{2,1,0:T(8,128)S(1)}, f32[9,136,128]{2,1,0:T(8,128)S(1)}, u32[]{:S(2)}, u32[]{:S(2)}) %collective-permute-start.15) | collective-permute-done | bytes 626720 | tf_op jit(solution)/shard_map/ppermute | solution.py:514
  110.5 3.2 %collective-permute-start.16 = (f32[9,136,128]{2,1,0:T(8,128)S(1)}, f32[9,136,128]{2,1,0:T(8,128)S(1)}, u32[]{:S(2)}, u32[]{:S(2)}) collective-permute-start(f32[9,136,128]{2,1,0:T(8,128)S(1)} %get-tuple-element.57.own), channel_id=1, source_target_pairs={{0,4},{4,0},{8,12},{12,8},{16,20},{20,16},{24,28},{28,24},{32,36},... | collective-permute-start | bytes 1880072 | tf_op jit(solution)/shard_map/ppermute | solution.py:518
  113.7 1.0 collective-permute-start.18
  114.7 1.8 %collective-permute-start.19 = (f32[9,16,128]{2,1,0:T(8,128)S(1)}, f32[9,16,128]{2,1,0:T(8,128)S(1)}, u32[]{:S(2)}, u32[]{:S(2)}) collective-permute-start(f32[9,16,128]{2,1,0:T(8,128)S(1)} %get-tuple-element.58.mine), channel_id=1, source_target_pairs={{0,3},{1,0},{2,1},{3,2},{4,7},{5,4},{6,5},{7,6},{8,11},{9,8},{10,9... | collective-permute-start | bytes 221192 | tf_op jit(solution)/shard_map/ppermute | solution.py:509
  116.5 1.7 %collective-permute-done.18.south = f32[9,16,128]{2,1,0:T(8,128)S(1)} collective-permute-done((f32[9,16,128]{2,1,0:T(8,128)S(1)}, f32[9,16,128]{2,1,0:T(8,128)S(1)}, u32[]{:S(2)}, u32[]{:S(2)}) %collective-permute-start.18) | collective-permute-done | bytes 73760 | tf_op jit(solution)/shard_map/ppermute | solution.py:509
  118.3 4.2 %collective-permute-start.20 = (f32[9,16,128]{2,1,0:T(8,128)S(1)}, f32[9,16,128]{2,1,0:T(8,128)S(1)}, u32[]{:S(2)}, u32[]{:S(2)}) collective-permute-start(f32[9,16,128]{2,1,0:T(8,128)S(1)} %shard_map.85.e_own), channel_id=1, source_target_pairs={{0,4},{4,0},{8,12},{12,8},{16,20},{20,16},{24,28},{28,24},{32,36},... | collective-permute-start | bytes 221192 | tf_op jit(solution)/shard_map/ppermute | solution.py:518
  122.5 0.9 collective-permute-done.20.e_near
  123.4 3.0 %collective-permute-done.21.e_far = f32[9,16,128]{2,1,0:T(8,128)S(1)} collective-permute-done((f32[9,16,128]{2,1,0:T(8,128)S(1)}, f32[9,16,128]{2,1,0:T(8,128)S(1)}, u32[]{:S(2)}, u32[]{:S(2)}) %collective-permute-start.21) | collective-permute-done | bytes 73760 | tf_op jit(solution)/shard_map/ppermute | solution.py:514
  126.4 9.3 %shard_map.86 = (f32[10,136,128]{2,1,0:T(8,128)S(1)}, f32[9,136,128]{2,1,0:T(8,128)S(1)}, f32[9,136,128]{2,1,0:T(8,128)S(1)}, f32[9,136,128]{2,1,0:T(8,128)S(1)}, f32[32,128]{1,0:T(8,128)S(1)}) custom-call(f32[9,136,128]{2,1,0:T(8,128)S(1)} %get-tuple-element.57.own, f32[9,136,128]{2,1,0:T(8,128)S(1)} %collective-permute-done.16.near, ...), custom_call_target="tpu_custom_call" | custom-call | bytes 8609792 | tf_op jit(solution)/shard_map/pallas_call | solution.py:28
  135.7 3.6 %collective-permute-start.22 = (f32[9,136,128]{2,1,0:T(8,128)S(1)}, f32[9,136,128]{2,1,0:T(8,128)S(1)}, u32[]{:S(2)}, u32[]{:S(2)}) collective-permute-start(f32[9,136,128]{2,1,0:T(8,128)S(1)} %get-tuple-element.62), channel_id=1, source_target_pairs={{0,4},{4,0},{8,12},{12,8},{16,20},{20,16},{24,28},{28,24},{32,36},... | collective-permute-start | bytes 1880072 | tf_op jit(solution)/shard_map/ppermute | solution.py:518
  139.3 13.3 %all_to_all.16 = f32[32,1,128]{2,1,0:T(1,128)S(1)} all-to-all(f32[32,1,128]{2,1,0:T(1,128)S(1)} %bitcast.25), channel_id=1, replica_groups=mesh['lon'=32,'lat'=4] {'lon'}, dimensions={0} | all-to-all | bytes 32768 | tf_op jit(solution)/shard_map/all_to_all | solution.py:580
  152.8 1.2 collective-permute-start.24
  154.0 1.9 %collective-permute-start.25 = (f32[10,16,128]{2,1,0:T(8,128)S(1)}, f32[10,16,128]{2,1,0:T(8,128)S(1)}, u32[]{:S(2)}, u32[]{:S(2)}) collective-permute-start(f32[10,16,128]{2,1,0:T(8,128)S(1)} %get-tuple-element.66.mine), channel_id=1, source_target_pairs={{0,3},{1,0},{2,1},{3,2},{4,7},{5,4},{6,5},{7,6},{8,11},{9,8},{10,9... | collective-permute-start | bytes 245768 | tf_op jit(solution)/shard_map/ppermute | solution.py:509
  155.9 1.3 collective-permute-start.26
  157.2 2.7 %collective-permute-done.26.across = f32[8,128]{1,0:T(8,128)S(1)} collective-permute-done((f32[8,128]{1,0:T(8,128)S(1)}, f32[8,128]{1,0:T(8,128)S(1)}, u32[]{:S(2)}, u32[]{:S(2)}) %collective-permute-start.26) | collective-permute-done | bytes 4128 | tf_op jit(solution)/shard_map/ppermute | solution.py:509
  159.9 1.9 %shard_map.88 = (f32[1096,128]{1,0:T(8,128)}, f32[1096,128]{1,0:T(8,128)}) custom-call(f32[9,136,128]{2,1,0:T(8,128)S(1)} %get-tuple-element.53.v0, f32[9,136,128]{2,1,0:T(8,128)S(1)} %get-tuple-element.60.v1, f32[9,136,128]{2,1,0:T(8,128)S(1)} %get-tuple-element.65.main, f32[10,16,128]{2,1,0:T(8,128)S(1)} %get-tuple-element.66.mine, ...), custom_call_target="tpu_custom_call" | custom-call | bytes 2129920 | tf_op jit(solution)/shard_map/pallas_call | solution.py:28
  (46 shorter events, 1.1 us)
Async XLA Ops:
  0.6 1.5 copy-start.8
  0.6 1.8 %copy-start.9 = (f32[4,1,128,4,128]{4,3,2,1,0:T(4,128)S(1)}, f32[4,1,128,4,128]{4,3,2,1,0:T(4,128)}, u32[]{:S(2)}) copy-start(f32[4,1,128,4,128]{4,3,2,1,0:T(4,128)} %param.9) | copy-start | bytes 3145732
  5.4 11.5 %copy-start.3 = (f32[274,128]{1,0:T(8,128)S(1)}, f32[274,128]{1,0:T(8,128)}, u32[]{:S(2)}) copy-start(f32[274,128]{1,0:T(8,128)} %weighting.1) | copy-start | bytes 420868
  5.5 43.3 %all-to-all-start = ((f32[128,32,128]{2,1,0:T(8,128)}), f32[128,32,128]{2,1,0:T(8,128)S(1)}, u32[]{:S(2)}, u32[]{:S(2)}) async-start(f32[128,32,128]{2,1,0:T(8,128)} %copy.13), calls=%async_computation | async-start | bytes 4194304 | tf_op jit(solution)/shard_map/all_to_all | solution.py:529
  17.0 1.6 %copy-start = (f32[4,2,137,4,128]{4,3,2,1,0:T(4,128)S(1)}, f32[4,2,137,4,128]{4,3,2,1,0:T(4,128)}, u32[]{:S(2)}) copy-start(f32[4,2,137,4,128]{4,3,2,1,0:T(4,128)} %param.6) | copy-start | bytes 6733828
  21.0 1.4 copy-start.1
  22.4 22.9 %copy-start.4 = (f32[2,136,128]{2,1,0:T(8,128)}, f32[2,136,128]{2,1,0:T(8,128)S(1)}, u32[]{:S(2)}) copy-start(f32[2,136,128]{2,1,0:T(8,128)S(1)} %get-tuple-element.41.packed) | copy-start | bytes 417796
  22.4 32.1 %collective-permute-start = (f32[14,136,128]{2,1,0:T(8,128)}, f32[14,136,128]{2,1,0:T(8,128)}, u32[]{:S(2)}, u32[]{:S(2)}) collective-permute-start(f32[14,136,128]{2,1,0:T(8,128)} %get-tuple-element.42), channel_id=1, source_target_pairs={{0,4},{4,0},{8,12},{12,8},{16,20},{20,16},{24,28},{28,24},{32,36},... | collective-permute-start | bytes 2924552 | tf_op jit(solution)/shard_map/ppermute | solution.py:518
  23.4 31.1 %collective-permute-start.1 = (f32[14,136,128]{2,1,0:T(8,128)}, f32[14,136,128]{2,1,0:T(8,128)}, u32[]{:S(2)}, u32[]{:S(2)}) collective-permute-start(f32[14,136,128]{2,1,0:T(8,128)} %get-tuple-element.43), channel_id=1, source_target_pairs={{0,124},{4,8},{8,4},{12,16},{16,12},{20,24},{24,20},{28,32},{32,28... | collective-permute-start | bytes 2924552 | tf_op jit(solution)/shard_map/ppermute | solution.py:514
  24.2 19.8 %collective-permute-start.2 = (f32[26,8,128]{2,1,0:T(8,128)S(1)}, f32[26,8,128]{2,1,0:T(8,128)S(1)}, u32[]{:S(2)}, u32[]{:S(2)}) collective-permute-start(f32[26,8,128]{2,1,0:T(8,128)S(1)} %get-tuple-element.44), channel_id=1, source_target_pairs={{0,1},{1,2},{2,3},{3,0},{4,5},{5,6},{6,7},{7,4},{8,9},{9,10},{10,1... | collective-permute-start | bytes 319496 | tf_op jit(solution)/shard_map/ppermute | solution.py:509
  25.4 18.6 %collective-permute-start.3 = (f32[26,8,128]{2,1,0:T(8,128)S(1)}, f32[26,8,128]{2,1,0:T(8,128)S(1)}, u32[]{:S(2)}, u32[]{:S(2)}) collective-permute-start(f32[26,8,128]{2,1,0:T(8,128)S(1)} %get-tuple-element.44), channel_id=1, source_target_pairs={{0,3},{1,0},{2,1},{3,2},{4,7},{5,4},{6,5},{7,6},{8,11},{9,8},{10,9... | collective-permute-start | bytes 319496 | tf_op jit(solution)/shard_map/ppermute | solution.py:509
  44.0 10.5 %collective-permute-start.4 = (f32[26,8,128]{2,1,0:T(8,128)S(1)}, f32[26,8,128]{2,1,0:T(8,128)}, u32[]{:S(2)}, u32[]{:S(2)}) collective-permute-start(f32[26,8,128]{2,1,0:T(8,128)S(1)} %shard_map.79.halo), channel_id=1, source_target_pairs={{0,4},{4,0},{8,12},{12,8},{16,20},{20,16},{24,28},{28,24},{32,36},... | collective-permute-start | bytes 319496 | tf_op jit(solution)/shard_map/ppermute | solution.py:518
  45.3 9.2 %collective-permute-start.5 = (f32[26,8,128]{2,1,0:T(8,128)S(1)}, f32[26,8,128]{2,1,0:T(8,128)}, u32[]{:S(2)}, u32[]{:S(2)}) collective-permute-start(f32[26,8,128]{2,1,0:T(8,128)S(1)} %shard_map.79.halo), channel_id=1, source_target_pairs={{0,124},{4,8},{8,4},{12,16},{16,12},{20,24},{24,20},{28,32},{32,28... | collective-permute-start | bytes 319496 | tf_op jit(solution)/shard_map/ppermute | solution.py:514
  46.6 7.9 %copy-start.5 = (f32[2,136,128]{2,1,0:T(8,128)S(1)}, f32[2,136,128]{2,1,0:T(8,128)}, u32[]{:S(2)}) copy-start(f32[2,136,128]{2,1,0:T(8,128)} %copy-done.4) | copy-start | bytes 417796
  48.7 5.8 %copy-start.2 = (f32[32,136,128]{2,1,0:T(8,128)S(1)}, f32[32,136,128]{2,1,0:T(8,128)}, u32[]{:S(2)}) copy-start(f32[32,136,128]{2,1,0:T(8,128)} %copy-done.1) | copy-start | bytes 6684676
  48.7 0.8 copy-start.6
  49.6 0.7 copy-start.7
  59.9 5.3 %collective-permute-start.6 = (f32[9,136,128]{2,1,0:T(8,128)S(1)}, f32[9,136,128]{2,1,0:T(8,128)S(1)}, u32[]{:S(2)}, u32[]{:S(2)}) collective-permute-start(f32[9,136,128]{2,1,0:T(8,128)S(1)} %get-tuple-element.46), channel_id=1, source_target_pairs={{0,4},{4,0},{8,12},{12,8},{16,20},{20,16},{24,28},{28,24},{32,36},... | collective-permute-start | bytes 1880072 | tf_op jit(solution)/shard_map/ppermute | solution.py:518
  63.5 10.0 %collective-permute-start.7 = (f32[9,136,128]{2,1,0:T(8,128)S(1)}, f32[9,136,128]{2,1,0:T(8,128)S(1)}, u32[]{:S(2)}, u32[]{:S(2)}) collective-permute-start(f32[9,136,128]{2,1,0:T(8,128)S(1)} %get-tuple-element.47), channel_id=1, source_target_pairs={{0,124},{4,8},{8,4},{12,16},{16,12},{20,24},{24,20},{28,32},{32,28... | collective-permute-start | bytes 1880072 | tf_op jit(solution)/shard_map/ppermute | solution.py:514
  73.7 14.0 %collective-permute-start.8 = (f32[9,136,128]{2,1,0:T(8,128)S(1)}, f32[9,136,128]{2,1,0:T(8,128)S(1)}, u32[]{:S(2)}, u32[]{:S(2)}) collective-permute-start(f32[9,136,128]{2,1,0:T(8,128)S(1)} %get-tuple-element.48.own), channel_id=1, source_target_pairs={{0,4},{4,0},{8,12},{12,8},{16,20},{20,16},{24,28},{28,24},{32,36},... | collective-permute-start | bytes 1880072 | tf_op jit(solution)/shard_map/ppermute | solution.py:518
  76.9 10.8 %collective-permute-start.9 = (f32[9,136,128]{2,1,0:T(8,128)S(1)}, f32[9,136,128]{2,1,0:T(8,128)S(1)}, u32[]{:S(2)}, u32[]{:S(2)}) collective-permute-start(f32[9,136,128]{2,1,0:T(8,128)S(1)} %get-tuple-element.48.own), channel_id=1, source_target_pairs={{0,124},{4,8},{8,4},{12,16},{16,12},{20,24},{24,20},{28,32},{32,28... | collective-permute-start | bytes 1880072 | tf_op jit(solution)/shard_map/ppermute | solution.py:514
  76.9 4.4 %collective-permute-start.10 = (f32[9,16,128]{2,1,0:T(8,128)S(1)}, f32[9,16,128]{2,1,0:T(8,128)S(1)}, u32[]{:S(2)}, u32[]{:S(2)}) collective-permute-start(f32[9,16,128]{2,1,0:T(8,128)S(1)} %get-tuple-element.49.mine), channel_id=1, source_target_pairs={{0,1},{1,2},{2,3},{3,0},{4,5},{5,6},{6,7},{7,4},{8,9},{9,10},{10,1... | collective-permute-start | bytes 221192 | tf_op jit(solution)/shard_map/ppermute | solution.py:509
  77.9 3.4 %collective-permute-start.11 = (f32[9,16,128]{2,1,0:T(8,128)S(1)}, f32[9,16,128]{2,1,0:T(8,128)S(1)}, u32[]{:S(2)}, u32[]{:S(2)}) collective-permute-start(f32[9,16,128]{2,1,0:T(8,128)S(1)} %get-tuple-element.49.mine), channel_id=1, source_target_pairs={{0,3},{1,0},{2,1},{3,2},{4,7},{5,4},{6,5},{7,6},{8,11},{9,8},{10,9... | collective-permute-start | bytes 221192 | tf_op jit(solution)/shard_map/ppermute | solution.py:509
  81.4 3.1 %collective-permute-start.12 = (f32[9,16,128]{2,1,0:T(8,128)S(1)}, f32[9,16,128]{2,1,0:T(8,128)S(1)}, u32[]{:S(2)}, u32[]{:S(2)}) collective-permute-start(f32[9,16,128]{2,1,0:T(8,128)S(1)} %shard_map.82.e_own), channel_id=1, source_target_pairs={{0,4},{4,0},{8,12},{12,8},{16,20},{20,16},{24,28},{28,24},{32,36},... | collective-permute-start | bytes 221192 | tf_op jit(solution)/shard_map/ppermute | solution.py:518
  83.5 4.2 %collective-permute-start.13 = (f32[9,16,128]{2,1,0:T(8,128)S(1)}, f32[9,16,128]{2,1,0:T(8,128)S(1)}, u32[]{:S(2)}, u32[]{:S(2)}) collective-permute-start(f32[9,16,128]{2,1,0:T(8,128)S(1)} %shard_map.82.e_own), channel_id=1, source_target_pairs={{0,124},{4,8},{8,4},{12,16},{16,12},{20,24},{24,20},{28,32},{32,28... | collective-permute-start | bytes 221192 | tf_op jit(solution)/shard_map/ppermute | solution.py:514
  97.1 4.9 %collective-permute-start.14 = (f32[9,136,128]{2,1,0:T(8,128)S(1)}, f32[9,136,128]{2,1,0:T(8,128)S(1)}, u32[]{:S(2)}, u32[]{:S(2)}) collective-permute-start(f32[9,136,128]{2,1,0:T(8,128)S(1)} %get-tuple-element.55), channel_id=1, source_target_pairs={{0,4},{4,0},{8,12},{12,8},{16,20},{20,16},{24,28},{28,24},{32,36},... | collective-permute-start | bytes 1880072 | tf_op jit(solution)/shard_map/ppermute | solution.py:518
  100.3 10.0 %collective-permute-start.15 = (f32[9,136,128]{2,1,0:T(8,128)S(1)}, f32[9,136,128]{2,1,0:T(8,128)S(1)}, u32[]{:S(2)}, u32[]{:S(2)}) collective-permute-start(f32[9,136,128]{2,1,0:T(8,128)S(1)} %get-tuple-element.56), channel_id=1, source_target_pairs={{0,124},{4,8},{8,4},{12,16},{16,12},{20,24},{24,20},{28,32},{32,28... | collective-permute-start | bytes 1880072 | tf_op jit(solution)/shard_map/ppermute | solution.py:514
  110.5 15.9 %collective-permute-start.16 = (f32[9,136,128]{2,1,0:T(8,128)S(1)}, f32[9,136,128]{2,1,0:T(8,128)S(1)}, u32[]{:S(2)}, u32[]{:S(2)}) collective-permute-start(f32[9,136,128]{2,1,0:T(8,128)S(1)} %get-tuple-element.57.own), channel_id=1, source_target_pairs={{0,4},{4,0},{8,12},{12,8},{16,20},{20,16},{24,28},{28,24},{32,36},... | collective-permute-start | bytes 1880072 | tf_op jit(solution)/shard_map/ppermute | solution.py:518
  113.7 12.7 %collective-permute-start.17 = (f32[9,136,128]{2,1,0:T(8,128)S(1)}, f32[9,136,128]{2,1,0:T(8,128)S(1)}, u32[]{:S(2)}, u32[]{:S(2)}) collective-permute-start(f32[9,136,128]{2,1,0:T(8,128)S(1)} %get-tuple-element.57.own), channel_id=1, source_target_pairs={{0,124},{4,8},{8,4},{12,16},{16,12},{20,24},{24,20},{28,32},{32,28... | collective-permute-start | bytes 1880072 | tf_op jit(solution)/shard_map/ppermute | solution.py:514
  113.7 4.6 %collective-permute-start.18 = (f32[9,16,128]{2,1,0:T(8,128)S(1)}, f32[9,16,128]{2,1,0:T(8,128)S(1)}, u32[]{:S(2)}, u32[]{:S(2)}) collective-permute-start(f32[9,16,128]{2,1,0:T(8,128)S(1)} %get-tuple-element.58.mine), channel_id=1, source_target_pairs={{0,1},{1,2},{2,3},{3,0},{4,5},{5,6},{6,7},{7,4},{8,9},{9,10},{10,1... | collective-permute-start | bytes 221192 | tf_op jit(solution)/shard_map/ppermute | solution.py:509
  114.7 3.6 %collective-permute-start.19 = (f32[9,16,128]{2,1,0:T(8,128)S(1)}, f32[9,16,128]{2,1,0:T(8,128)S(1)}, u32[]{:S(2)}, u32[]{:S(2)}) collective-permute-start(f32[9,16,128]{2,1,0:T(8,128)S(1)} %get-tuple-element.58.mine), channel_id=1, source_target_pairs={{0,3},{1,0},{2,1},{3,2},{4,7},{5,4},{6,5},{7,6},{8,11},{9,8},{10,9... | collective-permute-start | bytes 221192 | tf_op jit(solution)/shard_map/ppermute | solution.py:509
  118.3 5.1 %collective-permute-start.20 = (f32[9,16,128]{2,1,0:T(8,128)S(1)}, f32[9,16,128]{2,1,0:T(8,128)S(1)}, u32[]{:S(2)}, u32[]{:S(2)}) collective-permute-start(f32[9,16,128]{2,1,0:T(8,128)S(1)} %shard_map.85.e_own), channel_id=1, source_target_pairs={{0,4},{4,0},{8,12},{12,8},{16,20},{20,16},{24,28},{28,24},{32,36},... | collective-permute-start | bytes 221192 | tf_op jit(solution)/shard_map/ppermute | solution.py:518
  122.5 3.9 %collective-permute-start.21 = (f32[9,16,128]{2,1,0:T(8,128)S(1)}, f32[9,16,128]{2,1,0:T(8,128)S(1)}, u32[]{:S(2)}, u32[]{:S(2)}) collective-permute-start(f32[9,16,128]{2,1,0:T(8,128)S(1)} %shard_map.85.e_own), channel_id=1, source_target_pairs={{0,124},{4,8},{8,4},{12,16},{16,12},{20,24},{24,20},{28,32},{32,28... | collective-permute-start | bytes 221192 | tf_op jit(solution)/shard_map/ppermute | solution.py:514
  135.7 16.9 %collective-permute-start.22 = (f32[9,136,128]{2,1,0:T(8,128)S(1)}, f32[9,136,128]{2,1,0:T(8,128)S(1)}, u32[]{:S(2)}, u32[]{:S(2)}) collective-permute-start(f32[9,136,128]{2,1,0:T(8,128)S(1)} %get-tuple-element.62), channel_id=1, source_target_pairs={{0,4},{4,0},{8,12},{12,8},{16,20},{20,16},{24,28},{28,24},{32,36},... | collective-permute-start | bytes 1880072 | tf_op jit(solution)/shard_map/ppermute | solution.py:518
  139.3 13.3 %collective-permute-start.23 = (f32[9,136,128]{2,1,0:T(8,128)S(1)}, f32[9,136,128]{2,1,0:T(8,128)S(1)}, u32[]{:S(2)}, u32[]{:S(2)}) collective-permute-start(f32[9,136,128]{2,1,0:T(8,128)S(1)} %get-tuple-element.63), channel_id=1, source_target_pairs={{0,124},{4,8},{8,4},{12,16},{16,12},{20,24},{24,20},{28,32},{32,28... | collective-permute-start | bytes 1880072 | tf_op jit(solution)/shard_map/ppermute | solution.py:514
  152.8 7.1 %collective-permute-start.24 = (f32[10,16,128]{2,1,0:T(8,128)S(1)}, f32[10,16,128]{2,1,0:T(8,128)S(1)}, u32[]{:S(2)}, u32[]{:S(2)}) collective-permute-start(f32[10,16,128]{2,1,0:T(8,128)S(1)} %get-tuple-element.66.mine), channel_id=1, source_target_pairs={{0,1},{1,2},{2,3},{3,0},{4,5},{5,6},{6,7},{7,4},{8,9},{9,10},{10,1... | collective-permute-start | bytes 245768 | tf_op jit(solution)/shard_map/ppermute | solution.py:509
  154.0 5.9 %collective-permute-start.25 = (f32[10,16,128]{2,1,0:T(8,128)S(1)}, f32[10,16,128]{2,1,0:T(8,128)S(1)}, u32[]{:S(2)}, u32[]{:S(2)}) collective-permute-start(f32[10,16,128]{2,1,0:T(8,128)S(1)} %get-tuple-element.66.mine), channel_id=1, source_target_pairs={{0,3},{1,0},{2,1},{3,2},{4,7},{5,4},{6,5},{7,6},{8,11},{9,8},{10,9... | collective-permute-start | bytes 245768 | tf_op jit(solution)/shard_map/ppermute | solution.py:509
  155.9 4.0 %collective-permute-start.26 = (f32[8,128]{1,0:T(8,128)S(1)}, f32[8,128]{1,0:T(8,128)S(1)}, u32[]{:S(2)}, u32[]{:S(2)}) collective-permute-start(f32[8,128]{1,0:T(8,128)S(1)} %get-tuple-element.67), channel_id=1, source_target_pairs={{0,2},{1,3},{2,0},{3,1},{4,6},{5,7},{6,4},{7,5},{8,10},{9,11},{10,... | collective-permute-start | bytes 12296 | tf_op jit(solution)/shard_map/ppermute | solution.py:509
